TPU v7x, 256 devices: a whole 4x4x8 slice. The times are simulated.
256 devices in a mesh: ctx: 8 (over y, z_hi), dec: 8 (over z_lo, core), grp: 4 (over x).
Axes of the slice: x: 4, y: 4, z: 8 (z_hi: 2, z_lo: 4; z = z_hi * 4 + z_lo), core: 2. Of those that a mesh axis runs over, the one named last changes fastest.
Arguments:
- queries: bfloat16 [4, 128, 8192], P('grp', 'dec', 'ctx'), may hold values from -16 to 16
- prompt_kv: bfloat16 [4, 2, 32768, 2, 1024], P('grp', None, ('ctx', 'dec')), may hold values from -12 to 12
- suffix_kv: bfloat16 [4, 128, 256, 2, 1024], P('grp', 'dec', None, None, 'ctx'), may hold values from -18 to 18
- suffix_len: int32 [4, 128], P('grp', 'dec'), may hold values from 1 to 256, as said below
- group_of: int32 [4, 128], P('grp'), may hold values from 0 to 1, as said below
Outputs:
- attended: bfloat16 [4, 128, 8192], P('grp', 'dec', 'ctx')
Inputs may be any that keep to these rules, and one draw needn't show every extreme that they name: `group_of`: in every block of 128 rows each value names exactly 64 rows. `suffix_len`: every block has a row of length 256.
All inputs are finite; a program needn't handle non-finite values.
Results may differ from a plain program's by a relative error of at most 0.012.
Values may be sent and summed in bfloat16 or wider, within the bound.
No kernel may reach another device: no remote copies, remote signals or barrier semaphores. Data moves between devices by JAX's collectives and lax.ppermute only.
A program may use at most 192 MiB of HBM per device.

v0:
```python
import jax
import jax.numpy as jnp
from jax import lax
from jax.sharding import PartitionSpec as P

H = 64
KVH = 8
HD = 128


def shards(queries, prompt_kv, suffix_kv, suffix_len, group_of):
    n_ctx = lax.axis_size("ctx")
    n_dec = lax.axis_size("dec")
    row_dev = queries.shape[1]
    rows = row_dev * n_dec
    heads_loc = H // n_ctx
    kv_loc = KVH // n_ctx
    repeat = H // KVH
    scale = HD ** (-0.5)
    local_q = queries[0]
    partial_q = lax.all_gather(local_q, "dec", axis=0, tiled=True)
    whole = lax.all_gather(partial_q, "ctx", axis=1, tiled=True)
    groups = prompt_kv.shape[1]
    span = prompt_kv.shape[2]
    prompt = prompt_kv[0].reshape(groups, span, 2, KVH, HD)
    member_ids = group_of[0]
    heads_q = whole.reshape(rows, KVH, repeat, HD)
    member = member_ids[None, :] == jnp.arange(groups, dtype=jnp.int32)[:, None]
    member = jnp.repeat(member, repeat, axis=1)

    def head_scores(index):
        query_block = heads_q[:, index].reshape(rows * repeat, HD)
        return (
            jnp.einsum(
                "qd,gpd->gqp",
                query_block,
                prompt[:, :, 0, index],
                preferred_element_type=jnp.float32,
            )
            * scale
        )

    def row_peak(scores):
        return jnp.max(jnp.where(member[:, :, None], scores, -jnp.inf), axis=(0, 2)).reshape(
            rows, repeat
        )

    suffix = suffix_kv[0].reshape(row_dev, suffix_kv.shape[2], 2, kv_loc, HD)
    own_q = local_q.reshape(row_dev, kv_loc, repeat, HD)
    suffix_scores = (
        jnp.einsum("rjhd,rsjd->rjhs", own_q, suffix[:, :, 0], preferred_element_type=jnp.float32)
        * scale
    )
    valid = jnp.arange(suffix_kv.shape[2], dtype=jnp.int32)[None, :] < suffix_len[0][:, None]
    valid = valid[:, None, None, :]
    suffix_peak = jnp.max(jnp.where(valid, suffix_scores, -jnp.inf), axis=3).reshape(
        row_dev, heads_loc
    )
    row_start = lax.axis_index("dec") * row_dev
    head_start = lax.axis_index("ctx") * heads_loc

    def to_blocks(array, width):
        return (
            array.reshape(n_dec, row_dev, n_ctx, heads_loc * width)
            .transpose(2, 0, 1, 3)
            .reshape(n_ctx * n_dec * row_dev, heads_loc * width)
        )

    prefix_peak = jnp.stack([row_peak(head_scores(index)) for index in range(KVH)], axis=1).reshape(
        rows, H
    )
    placed = lax.dynamic_update_slice(
        jnp.full((rows, H), -jnp.inf, jnp.float32), suffix_peak, (row_start, head_start)
    )
    peak = lax.pmax(jnp.maximum(prefix_peak, placed).astype(jnp.bfloat16), ("ctx", "dec")).astype(
        jnp.float32
    )
    peak_heads = peak.reshape(rows, KVH, repeat)
    numer_list = []
    total_list = []
    for index in range(KVH):
        row_scores = head_scores(index)
        peak_head = peak_heads[:, index]
        shifted = row_scores - peak_head.reshape(1, rows * repeat, 1)
        probs = jnp.where(member[:, :, None], jnp.exp(shifted), 0.0)
        row_totals = jnp.sum(probs, axis=(0, 2)).reshape(rows, repeat)
        weights = probs.astype(jnp.bfloat16)
        row_numer = jnp.einsum(
            "gqp,gpd->qd", weights, prompt[:, :, 1, index], preferred_element_type=jnp.float32
        )
        numer_head = row_numer.reshape(rows, repeat, HD)
        numer_list.append(numer_head)
        total_list.append(row_totals)
    numer = jnp.stack(numer_list, axis=1).reshape(rows, H * HD)
    totals = jnp.stack(total_list, axis=1).reshape(rows, H)
    numer_mine, totals_mine = (
        lax.psum_scatter(to_blocks(numer, HD), ("ctx", "dec"), scatter_dimension=0, tiled=True),
        lax.psum_scatter(to_blocks(totals, 1), ("ctx", "dec"), scatter_dimension=0, tiled=True),
    )
    numer_mine = numer_mine.reshape(row_dev, heads_loc, HD)
    own_peak = lax.dynamic_slice(peak, (row_start, head_start), (row_dev, heads_loc)).reshape(
        row_dev, kv_loc, repeat
    )
    suffix_probs = jnp.where(valid, jnp.exp(suffix_scores - own_peak[:, :, :, None]), 0.0)
    suffix_totals = jnp.sum(suffix_probs, axis=3).reshape(row_dev, heads_loc)
    suffix_weights = suffix_probs.astype(jnp.bfloat16)
    suffix_numer = jnp.einsum(
        "rjhs,rsjd->rjhd", suffix_weights, suffix[:, :, 1], preferred_element_type=jnp.float32
    )
    suffix_numer = suffix_numer.reshape(row_dev, heads_loc, HD)
    all_totals = totals_mine + suffix_totals
    result = (numer_mine + suffix_numer) / all_totals[:, :, None]
    return result.reshape(1, row_dev, heads_loc * HD).astype(jnp.bfloat16)


def solution(mesh):
    placed = (
        P("grp", "dec", "ctx"),
        P("grp", None, ("ctx", "dec"), None, None),
        P("grp", "dec", None, None, "ctx"),
        P("grp", "dec"),
        P("grp", None),
    )
    return jax.shard_map(
        shards, mesh=mesh, in_specs=placed, out_specs=P("grp", "dec", "ctx"), check_vma=False
    )
```

profile of v0, /device:TPU:2, one launch (start us, length us, event | category | flops | bytes accessed | tf_op | source)
XLA Modules:
  0.0 705.2 jit_solution(18176793363939766013)
XLA Ops:
  6.5 16.6 %all-gather = bf16[1,128,1024]{2,1,0:T(8,128)(2,1)} all-gather(bf16[1,16,1024]{2,1,0:T(8,128)(2,1)} %param.5), channel_id=2, replica_groups=mesh['ctx'=8,'dec'=8,'grp'=4] {'dec'}, dimensions={1}, use_global_device_ids=true | all-gather | bytes 294912 | tf_op jit(solution)/shard_map/all_gather | solution.py:21
  24.9 2.1 copy.178
  27.0 1.2 copy-done.6
  28.8 11.1 %copy.83 = bf16[1,2,512,2,1024]{2,4,3,1,0:T(8,128)(2,1)} copy(bf16[1,2,512,2,1024]{4,3,2,1,0:T(2,128)(2,1)} %param.6) | data formatting | bytes 8388608 | tf_op args[1]
  40.2 61.3 %all-gather.4.cloned.1.call-done = bf16[1,128,8192]{2,1,0:T(8,128)(2,1)} async-done(((bf16[1,128,1024]{2,1,0:T(8,128)(2,1)}), bf16[1,128,8192]{2,1,0:T(8,128)(2,1)}) %all-gather.4.cloned.1.call-update) | async-done | bytes 2097168 | tf_op jit(solution)/shard_map/all_gather | solution.py:22
  101.5 2.2 copy.167
  103.7 1.9 fusion.50
  105.5 1.9 fusion.51
  107.4 1.9 fusion.52
  109.3 1.9 fusion.53
  111.2 1.9 fusion.54
  113.1 3.8 fusion.55
  116.9 3.7 fusion.56
  120.6 8.3 %select_reduce_fusion.8 = (bf16[1024]{0:T(1024)(128)(2,1)S(1)}, bf16[1024]{0:T(1024)(128)(2,1)S(1)}, bf16[1024]{0:T(1024)(128)(2,1)S(1)}, bf16[1024]{0:T(1024)(1...) fusion(pred[2,1024]{1,0:T(4,128)(4,1)S(1)} %broadcast_in_dim.11, ...), kind=kOutput, calls=%fused_computation.32 | convolution fusion | flops 293593088 | bytes 34097152 | tf_op jit(solution)/shard_map/qd,gpd->gqp/dot_general | solution.py:34
  130.4 246.5 %pmax.7 = bf16[128,64]{0,1:T(8,128)(2,1)S(1)} all-reduce(bf16[128,64]{0,1:T(8,128)(2,1)S(1)} %fusion.64), channel_id=1, replica_groups=mesh['ctx'=8,'dec'=8,'grp'=4] {'ctx','dec'}, use_global_device_ids=true, to_apply=%region_9.10 | all-reduce | flops 8192 | bytes 32768 | tf_op jit(solution)/shard_map/pmax | solution.py:75
  378.5 14.0 %select_reduce_fusion = (f32[1024]{0:T(1024)S(1)}, f32[1024]{0:T(1024)S(1)}, f32[1024]{0:T(1024)S(1)}, f32[1024]{0:T(1024)S(1)}, f32[1024]{0:T(1024)S(1)}, /*ind...) fusion(f32[2,512,1024]{2,1,0:T(8,128)} %get-tuple-element.39, f32[1024]{0:T(1024)S(1)} %sub.134, ...), kind=kLoop, calls=%fused_computation.16 | loop fusion | flops 33546240 | bytes 33622016 | tf_op jit(solution)/shard_map/reduce_sum | solution.py:86
  392.4 18.7 %fusion = (bf16[1024,2,512]{0,2,1:T(8,128)(2,1)S(1)}, bf16[1024,2,512]{0,2,1:T(8,128)(2,1)}, bf16[1024,2,512]{0,2,1:T(8,128)(2,1)}, bf16[1024,2,512]{0,2,1:T(8,1...) fusion(f32[2,512,1024]{2,1,0:T(8,128)} %get-tuple-element.39, ...), kind=kLoop, calls=%fused_computation.1 | loop fusion | flops 33554432 | bytes 50366464 | tf_op jit(solution)/shard_map/convert_element_type | solution.py:87
  411.1 2.6 copy.132
  413.7 2.3 fusion.45
  418.0 2.9 copy.114
  420.9 2.5 fusion.27
  423.4 1.1 stack.43
  424.5 2.9 copy.117
  427.4 2.5 fusion.30
  429.9 1.9 stack.44
  431.8 2.9 copy.120
  434.7 2.5 fusion.33
  437.2 1.9 stack.45
  439.1 2.9 copy.123
  442.0 2.5 fusion.36
  444.4 1.9 stack.46
  446.4 2.9 copy.126
  449.3 2.5 fusion.39
  451.7 1.9 stack.47
  453.7 2.9 copy.129
  456.6 2.5 fusion.42
  459.0 1.9 stack.48
  461.0 2.9 copy.111
  463.8 2.5 fusion.24
  466.3 1.2 stack.42
  468.3 0.8 constant_dynamic-update-slice_fusion.14
  469.2 1.9 constant_dynamic-update-slice_fusion.13
  471.1 0.8 constant_dynamic-update-slice_fusion.12
  472.8 0.8 constant_dynamic-update-slice_fusion.10
  474.5 0.8 constant_dynamic-update-slice_fusion.8
  476.0 74.7 %reduce-scatter.5.cloned.1.call-done = f32[16,8]{1,0:T(8,128)} async-done(((f32[1024,8]{1,0:T(8,128)}), f32[16,8]{1,0:T(8,128)}) %reduce-scatter.5.cloned.1.call-update) | async-done | bytes 528 | tf_op jit(solution)/shard_map/reduce_scatter | solution.py:98
  551.4 145.8 %reduce-scatter.3.cloned.1.call-done = f32[16,1024]{1,0:T(8,128)} async-done(((f32[1024,1024]{1,0:T(8,128)}), f32[16,1024]{1,0:T(8,128)}) %reduce-scatter.3.cloned.1.call-update) | async-done | bytes 65552 | tf_op jit(solution)/shard_map/reduce_scatter | solution.py:97
  697.2 1.5 fusion.65
  (111 shorter events, 11.4 us)
Async XLA Ops:
  6.5 20.4 %copy-start.13 = (s32[1,16]{1,0:T(1,128)S(1)}, s32[1,16]{1,0:T(1,128)}, u32[]{:S(2)}) copy-start(s32[1,16]{1,0:T(1,128)} %param.8) | copy-start | bytes 196
  6.5 94.9 %all-gather.4.cloned.1.call-start = ((), (), s32[]{:S(2)}) async-start(), calls=%async_computation.4 | async-start | bytes 2359296 | tf_op jit(solution)/shard_map/all_gather | solution.py:22
  23.1 527.5 %reduce-scatter.5.cloned.1.call-start = ((), (), s32[]{:S(2)}) async-start(), calls=%async_computation.3 | async-start | bytes 532480 | tf_op jit(solution)/shard_map/reduce_scatter | solution.py:98
  26.9 1.3 copy-start.6
  103.6 13.3 %copy-start.5 = (bf16[16,8,64,128]{3,2,1,0:T(8,128)(2,1)}, bf16[16,8,64,128]{3,2,1,0:T(8,128)(2,1)S(1)}, u32[]{:S(2)}) copy-start(bf16[16,8,64,128]{3,2,1,0:T(8,128)(2,1)S(1)} %copy.167) | copy-start | bytes 6291460
  105.5 15.1 %copy-start = (f32[2,512,1024]{2,1,0:T(8,128)}, f32[2,512,1024]{2,1,0:T(8,128)S(1)}, u32[]{:S(2)}) copy-start(f32[2,512,1024]{2,1,0:T(8,128)S(1)} %fusion.50) | copy-start | bytes 12582916
  107.4 13.2 %copy-start.1 = (f32[2,512,1024]{2,1,0:T(8,128)}, f32[2,512,1024]{2,1,0:T(8,128)S(1)}, u32[]{:S(2)}) copy-start(f32[2,512,1024]{2,1,0:T(8,128)S(1)} %fusion.51) | copy-start | bytes 12582916
  109.3 11.3 %copy-start.2 = (f32[2,512,1024]{2,1,0:T(8,128)}, f32[2,512,1024]{2,1,0:T(8,128)S(1)}, u32[]{:S(2)}) copy-start(f32[2,512,1024]{2,1,0:T(8,128)S(1)} %fusion.52) | copy-start | bytes 12582916
  111.2 9.4 %copy-start.3 = (f32[2,512,1024]{2,1,0:T(8,128)}, f32[2,512,1024]{2,1,0:T(8,128)S(1)}, u32[]{:S(2)}) copy-start(f32[2,512,1024]{2,1,0:T(8,128)S(1)} %fusion.53) | copy-start | bytes 12582916
  113.1 7.5 %copy-start.4 = (f32[2,512,1024]{2,1,0:T(8,128)}, f32[2,512,1024]{2,1,0:T(8,128)S(1)}, u32[]{:S(2)}) copy-start(f32[2,512,1024]{2,1,0:T(8,128)S(1)} %fusion.54) | copy-start | bytes 12582916
  416.9 0.8 copy-start.12
  417.7 279.4 %reduce-scatter.3.cloned.1.call-start = ((), (), s32[]{:S(2)}) async-start(), calls=%async_computation.2 | async-start | bytes 4259840 | tf_op jit(solution)/shard_map/reduce_scatter | solution.py:97
  466.3 4.8 copy-start.8
  467.5 4.5 copy-start.9
  467.5 5.3 copy-start.10
  467.5 6.1 copy-start.11
  471.9 3.7 copy-start.7
Sparse Core Ops, SparseCore 0:
  23.3 78.1 all-gather.3
  417.9 132.7 reduce-scatter.4
  554.8 142.2 reduce-scatter.2
where the time goes:
time: 707 us; the launch traced here: 705 us
  waiting for transfers between devices  282 us (40%)
  blocking collectives  263 us (37%)
  local copies, waits for them, and re-layouts  65.2 us (9%)
  matrix products  45.5 us (6%)
  other arithmetic  35.8 us (5%)
  between operations  13.6 us (2%)
    pmax x1, blocking collectives, shards(): lax.pmax(jnp.maximum(prefix_peak, placed).astype(jnp.bfloat16), ('ctx', '...  246 us
    reduce_scatter x1, waiting for transfers between devices, shards(): lax.psum_scatter(to_blocks(numer, HD), ('ctx', 'dec'), scatter_dimension=...  146 us
    reduce_scatter x1, waiting for transfers between devices, shards(): lax.psum_scatter(to_blocks(totals, 1), ('ctx', 'dec'), scatter_dimension=...  74.7 us
    all_gather x1, waiting for transfers between devices, shards(): whole = lax.all_gather(partial_q, 'ctx', axis=1, tiled=True)  61.3 us
    unnamed x53, local copies, waits for them, and re-layouts  25.2 us
    dot_general x8, matrix products, head_scores(): jnp.einsum('qd,gpd->gqp', query_block, prompt[:, :, 0, index], preferred_...  25.1 us
    convert_element_type x8, local copies, waits for them, and re-layouts, shards(): weights = probs.astype(jnp.bfloat16)  22.6 us
    dot_general x8, matrix products, shards(): jnp.einsum('gqp,gpd->qd', weights, prompt[:, :, 1, index], preferred_elem...  19.6 us
  transfers between devices with their start and end apart: 3, of which 3 were waited for; matrix products, arithmetic and copies ran while one was open for 11% of the time, Pallas kernels for 0%

commit v1 on v0

v1 whole, which is shorter than its diff:
```python
import functools
import math

import jax
import jax.numpy as jnp
import numpy as np
from jax import lax
from jax.experimental import pallas as pl
from jax.experimental.pallas import tpu as pltpu
from jax.sharding import Mesh
from jax.sharding import PartitionSpec as P

HD = 128
REP = 8
C2 = HD ** (-0.5) * math.log2(math.e)
BIG = 1e30
F32 = jnp.float32
BF16 = jnp.bfloat16


def _dot_t(a, b):
    return lax.dot_general(a, b, (((1,), (1,)), ((), ())), preferred_element_type=F32)


def _pack(l2):
    hi = l2.astype(BF16).astype(F32)
    rest = l2 - hi
    mid = rest.astype(BF16).astype(F32)
    return hi, mid, rest - mid


def _stats(l2):
    lane = lax.broadcasted_iota(jnp.int32, l2.shape, 1)
    hi, mid, lo = _pack(jnp.where(lane < REP, l2, 0.0))
    return (hi + pltpu.roll(mid, REP, 1) + pltpu.roll(lo, 2 * REP, 1)).astype(BF16)


def _prompt_kernel(distance, ids_ref, q_ref, own_hbm, par_hbm, o_ref, kv_ref, s_ref, sem):
    zs, row_dev = q_ref.shape[:2]
    per = zs // 2
    rows = per * row_dev
    span = own_hbm.shape[2]
    width = 2 * HD
    n_y = own_hbm.shape[3] // width
    at = pl.multiple_of(lax.rem(lax.axis_index("y") + distance, n_y) * width, width)
    copies = []
    for which in range(2):
        for k, ref in enumerate((own_hbm, par_hbm)):
            copy = pltpu.make_async_copy(
                ref.at[:, which, :, pl.ds(at, width)],
                kv_ref.at[which, :, pl.ds(k * span, span), :],
                sem.at[2 * which + k],
            )
            copy.start()
            copies.append(copy)

    total = ids_ref.shape[1]
    shape = (per, row_dev, total)
    source = lax.broadcasted_iota(jnp.int32, shape, 0) * (2 * row_dev)
    source += lax.axis_index("core") * row_dev + lax.broadcasted_iota(jnp.int32, shape, 1)
    source = source.reshape(rows, total)
    lane = lax.broadcasted_iota(jnp.int32, (rows, total), 1)
    ids = jnp.broadcast_to(ids_ref[...].astype(F32), (rows, total))
    member = jnp.sum(jnp.where(lane == source, ids, 0.0), axis=1, keepdims=True)
    member = jnp.broadcast_to(member, (rows, HD))
    lane = lax.broadcasted_iota(jnp.int32, (rows, HD), 1)

    def scores(h):
        q = q_ref[h * per : (h + 1) * per].reshape(rows, REP * HD)
        q = jnp.concatenate([q[:, r * HD : (r + 1) * HD] for r in range(REP)], axis=0)
        one = jnp.concatenate([member] * REP, axis=0)
        q = jnp.concatenate([q * (1.0 - one).astype(BF16), q * one.astype(BF16)], axis=1)
        lanes = slice(h * HD, (h + 1) * HD)
        k = jnp.concatenate([kv_ref[0, 0, :, lanes], kv_ref[0, 1, :, lanes]], axis=1)
        s = _dot_t(q, k)
        s_ref[h] = s
        return jnp.max(s, axis=1, keepdims=True) * C2

    def attend(h, peak):
        w = jnp.exp2(s_ref[h] * C2 - peak)
        totals = jnp.sum(w, axis=1, keepdims=True)
        lanes = slice(h * HD, (h + 1) * HD)
        v = jnp.concatenate([kv_ref[1, 0, :, lanes], kv_ref[1, 1, :, lanes]], axis=1)
        acc = jnp.dot(w.astype(BF16), v, preferred_element_type=F32)
        inverse = 1.0 / totals
        weight = jnp.ones((rows, HD), F32)
        top = jnp.zeros((rows, HD), F32)
        zone = slice(h * per, (h + 1) * per)
        for r in range(REP):
            sl = slice(r * rows, (r + 1) * rows)
            o = jnp.where(member > 0.5, acc[sl, HD:], acc[sl, :HD]) * inverse[sl]
            o_ref[zone, :, r * HD : (r + 1) * HD] = o.astype(BF16).reshape(per, row_dev, HD)
            weight = jnp.where(lane == r, totals[sl], weight)
            top = jnp.where(lane == r, peak[sl], top)
        stats = _stats(top + jnp.log2(weight))
        o_ref[zone, :, REP * HD :] = stats.reshape(per, row_dev, HD)

    copies[0].wait()
    copies[1].wait()
    peak0 = scores(0)
    peak1 = scores(1)
    copies[2].wait()
    copies[3].wait()
    attend(0, peak0)
    attend(1, peak1)


def _prompt(distance, ids, q, own, par):
    zs, row_dev, width = q.shape
    span = own.shape[2]
    rows = zs // 2 * row_dev
    vmem = pl.BlockSpec(memory_space=pltpu.VMEM)
    hbm = pl.BlockSpec(memory_space=pl.ANY)
    return pl.pallas_call(
        functools.partial(_prompt_kernel, distance),
        out_shape=jax.ShapeDtypeStruct((zs, row_dev, width + HD), BF16),
        in_specs=[vmem, vmem, hbm, hbm],
        out_specs=vmem,
        scratch_shapes=[
            pltpu.VMEM((2, 2, 2 * span, 2 * HD), BF16),
            pltpu.VMEM((2, rows * REP, 2 * span), F32),
            pltpu.SemaphoreType.DMA((4,)),
        ],
        compiler_params=pltpu.CompilerParams(vmem_limit_bytes=58 * 2**20),
        cost_estimate=pl.CostEstimate(
            flops=2 * 2 * 2 * rows * REP * 2 * span * 2 * HD,
            bytes_accessed=2 * 2 * 4 * span * HD * 2,
            transcendentals=2 * rows * REP * 2 * span,
        ),
    )(ids, q, own, par)


def _lse(x):
    s = x.astype(F32)
    return s + pltpu.roll(s, HD - REP, 1) + pltpu.roll(s, HD - 2 * REP, 1)


def _weights(l2s):
    top = functools.reduce(jnp.maximum, l2s)
    es = [jnp.exp2(l2 - top) for l2 in l2s]
    total = functools.reduce(jnp.add, es)
    return [e / total for e in es], top + jnp.log2(total)


def _merge_kernel(a_ref, b_ref, c_ref, d_ref, o_ref):
    lead = a_ref.shape[:2]
    rows = lead[0] * lead[1]
    refs = (a_ref, b_ref, c_ref, d_ref)
    lane = lax.broadcasted_iota(jnp.int32, (rows, HD), 1)
    l2s = [_lse(ref[:, :, REP * HD :].reshape(rows, HD)) for ref in refs]
    l2s = [jnp.where(lane < REP, x, 0.0) for x in l2s]
    ws, l2 = _weights(l2s)
    for r in range(REP):
        acc = None
        for w, ref in zip(ws, refs):
            x = ref[:, :, r * HD : (r + 1) * HD].reshape(rows, HD).astype(F32)
            x = x * w[:, r : r + 1]
            acc = x if acc is None else acc + x
        o_ref[:, :, r * HD : (r + 1) * HD] = acc.astype(BF16).reshape(*lead, HD)
    o_ref[:, :, REP * HD :] = _stats(l2).reshape(*lead, HD)


def _merge(parts):
    return pl.pallas_call(
        _merge_kernel,
        out_shape=jax.ShapeDtypeStruct(parts[0].shape, BF16),
        compiler_params=pltpu.CompilerParams(vmem_limit_bytes=58 * 2**20),
    )(*parts)


def _final_kernel(p_ref, so_ref, sl_ref, o_ref):
    n = p_ref.shape[0]
    rows = p_ref.shape[1]
    lane = lax.broadcasted_iota(jnp.int32, (rows, HD), 1)
    l2s = [_lse(p_ref[i, :, REP * HD :]) for i in range(n)] + [sl_ref[...]]
    ws, _ = _weights([jnp.where(lane < REP, x, 0.0) for x in l2s])
    for r in range(REP):
        sl = slice(r * HD, (r + 1) * HD)
        acc = so_ref[:, sl] * ws[n][:, r : r + 1]
        for i in range(n):
            acc += p_ref[i, :, sl].astype(F32) * ws[i][:, r : r + 1]
        o_ref[:, sl] = acc.astype(BF16)


def _final(parts, suffix_o, suffix_l2):
    return pl.pallas_call(
        _final_kernel,
        out_shape=jax.ShapeDtypeStruct(suffix_o.shape, BF16),
        compiler_params=pltpu.CompilerParams(vmem_limit_bytes=58 * 2**20),
    )(parts, suffix_o, suffix_l2)


def _suffix(q, kv, lengths):
    rows, suf = kv.shape[0], kv.shape[1]
    own_q = q.reshape(rows, REP, HD)
    scores = jnp.einsum("rhd,rsd->rhs", own_q, kv[:, :, 0], preferred_element_type=F32) * C2
    valid = jnp.arange(suf, dtype=jnp.int32)[None, None, :] < lengths[:, None, None]
    scores = jnp.where(valid, scores, -BIG)
    peak = jnp.max(scores, axis=2, keepdims=True)
    probs = jnp.exp2(scores - peak)
    total = jnp.sum(probs, axis=2)
    numer = jnp.einsum("rhs,rsd->rhd", probs.astype(BF16), kv[:, :, 1], preferred_element_type=F32)
    o = (numer / total[:, :, None]).reshape(rows, REP * HD)
    l2 = jnp.pad(peak[:, :, 0] + jnp.log2(total), ((0, 0), (0, HD - REP)))
    return o, l2


def _shards(queries, prompt_kv, suffix_kv, suffix_len, group_of):
    n_y = lax.axis_size("y")
    q = queries[0]
    own = jnp.transpose(prompt_kv[0], (0, 2, 1, 3))
    par = lax.ppermute(own, "core", [(0, 1), (1, 0)])

    n_z = lax.axis_size("zh") * lax.axis_size("zl")
    spread = jnp.broadcast_to(q[None], (n_z, *q.shape))
    q0 = lax.all_to_all(spread, ("zh", "zl"), 0, 0, tiled=True)
    qs = [q0] + [
        lax.ppermute(q0, "y", [((i + d) % n_y, i) for i in range(n_y)]) for d in range(1, n_y)
    ]

    suffix_o, suffix_l2 = _suffix(q, suffix_kv[0], suffix_len[0])

    parts = []
    for d in range(n_y):
        part = _prompt(d, group_of, qs[d], own, par)
        if d:
            part = lax.ppermute(part, "y", [(i, (i + d) % n_y) for i in range(n_y)])
        parts.append(part)
    merged = _merge(parts)
    got = lax.all_to_all(merged, ("zh", "zl"), 0, 0, tiled=True)
    return _final(got, suffix_o, suffix_l2)[None]


def solution(mesh):
    fine = Mesh(
        np.asarray(mesh.devices).reshape(4, 2, 4, 2, 4), ("y", "zh", "zl", "core", "grp")
    )
    ctx, dec = ("y", "zh"), ("zl", "core")
    placed = (
        P("grp", dec, ctx),
        P("grp", None, ctx + dec, None, None),
        P("grp", dec, None, None, ctx),
        P("grp", dec),
        P("grp", None),
    )
    return jax.shard_map(
        _shards, mesh=fine, in_specs=placed, out_specs=P("grp", dec, ctx), check_vma=False
    )
```

time: 707 us -> 88.1 us (0.12)
  waiting for transfers between devices: 282 us -> 12 us
  blocking collectives: 263 us -> 20.8 us
  local copies, waits for them, and re-layouts: 65.2 us -> 10.3 us
  matrix products: 45.5 us -> 0.75 us
  other arithmetic: 35.8 us -> 0.25 us
  Pallas kernels: 0 us -> 24.6 us
  starting transfers between devices: 0.31 us -> 18.7 us
  between operations: 13.6 us -> 0.16 us
    pmax x1 -> x0, blocking collectives: 246 us -> none  [shards(): lax.pmax(jnp.maximum(prefix_peak, placed).astype(jnp.bfloat16), ('ctx', '...]
    reduce_scatter x2 -> x0, waiting for transfers between devices: 220 us -> none  [the longest x1 146 us: shards(): lax.psum_scatter(to_blocks(numer, HD), ('ctx', 'dec'), scatter_dimension=...]
    all_gather x1 -> x0, waiting for transfers between devices: 61.3 us -> none  [shards(): whole = lax.all_gather(partial_q, 'ctx', axis=1, tiled=True)]
    dot_general x18 -> x2, matrix products: 45.5 us -> 0.75 us  [the longest x1 0.45 us: _suffix(): jnp.einsum('rhd,rsd->rhs', own_q, kv[:, :, 0], preferred_element_type=F32)]
    pallas_call x0 -> x6, Pallas kernels: none -> 24.6 us  [the longest x4 19.9 us: _prompt(): pl.pallas_call(functools.partial(_prompt_kernel, distance), out_shape=jax...]
    convert_element_type x8 -> x0, local copies, waits for them, and re-layouts: 22.6 us -> none  [shards(): weights = probs.astype(jnp.bfloat16)]
    all_to_all x0 -> x1, blocking collectives: none -> 20.8 us  [_shards(): q0 = lax.all_to_all(spread, ('zh', 'zl'), 0, 0, tiled=True)]
    convert_element_type x3 -> x0, other arithmetic: 20.2 us -> none  [the longest x1 18.7 us: shards(): weights = probs.astype(jnp.bfloat16)]
  transfers between devices with their start and end apart: 3 -> 8, of which waited for: 3 -> 3; matrix products, arithmetic and copies ran while one was open for 11% -> 5% of each run, Pallas kernels for 0% -> 23%
where the time goes in v1:
time: 88.1 us; the launch traced here: 87.6 us
  Pallas kernels  24.6 us (28%)
  blocking collectives  20.8 us (24%)
  starting transfers between devices  18.7 us (21%)
  waiting for transfers between devices  12 us (14%)
  local copies, waits for them, and re-layouts  10.3 us (12%)
    all_to_all x1, blocking collectives, _shards(): q0 = lax.all_to_all(spread, ('zh', 'zl'), 0, 0, tiled=True)  20.8 us
    pallas_call x4, Pallas kernels, _prompt(): pl.pallas_call(functools.partial(_prompt_kernel, distance), out_shape=jax...  19.9 us
    unnamed x30, local copies, waits for them, and re-layouts  9.71 us
    ppermute x3, starting transfers between devices, _shards(): part = lax.ppermute(part, 'y', [(i, (i + d) % n_y) for i in range(n_y)])  9.38 us
    all_to_all x1, waiting for transfers between devices, _shards(): got = lax.all_to_all(merged, ('zh', 'zl'), 0, 0, tiled=True)  9.02 us
    ppermute x3, starting transfers between devices, _shards(): lax.ppermute(q0, 'y', [((i + d) % n_y, i) for i in range(n_y)])  5.83 us
    all_to_all x1, starting transfers between devices, _shards(): got = lax.all_to_all(merged, ('zh', 'zl'), 0, 0, tiled=True)  3.42 us
    pallas_call x1, Pallas kernels, _merge(): pl.pallas_call(_merge_kernel, out_shape=jax.ShapeDtypeStruct(parts[0].sha...  2.77 us
  transfers between devices with their start and end apart: 8, of which 3 were waited for; matrix products, arithmetic and copies ran while one was open for 5% of the time, Pallas kernels for 23%

profile of v1, /device:TPU:2, one launch (start us, length us, event | category | flops | bytes accessed | tf_op | source)
XLA Modules:
  0.0 87.6 jit_solution(13081440588395996788)
XLA Ops:
  0.0 3.6 %copy.13 = bf16[1,2,512,2,1024]{4,2,3,1,0:T(8,128)(2,1)S(1)} copy(bf16[1,2,512,2,1024]{4,3,2,1,0:T(2,128)(2,1)} %param.6) | data formatting | bytes 8388608 | tf_op args[1]
  3.7 0.0 copy-start
  3.7 0.1 collective-permute-start
  3.8 0.0 copy-done.11
  3.8 20.8 %all_to_all.10.q_ref = bf16[8,16,1024]{2,1,0:T(8,128)(2,1)S(1)} all-to-all(bf16[8,16,1024]{2,1,0:T(8,128)(2,1)S(1)} %broadcast_in_dim.26), channel_id=1, replica_groups=mesh['y'=4,'zh'=2,'zl'=4,'core'=2,'grp'=4] {'zh','zl'}, dimensions={0} | all-to-all | bytes 524288 | tf_op jit(solution)/shard_map/all_to_all | solution.py:216
  24.6 1.6 %collective-permute-start.5 = (bf16[8,16,1024]{2,1,0:T(8,128)(2,1)S(1)}, bf16[8,16,1024]{2,1,0:T(8,128)(2,1)S(1)}, u32[]{:S(2)}, u32[]{:S(2)}) collective-permute-start(bf16[8,16,1024]{2,1,0:T(8,128)(2,1)S(1)} %all_to_all.10.q_ref), channel_id=1, source_target_pairs={{192,0},{0,64},{64,128},{128,192},{193,1},{1,65},{65,129},{129,193... | collective-permute-start | bytes 786440 | tf_op jit(solution)/shard_map/ppermute | solution.py:218
  26.2 2.9 %collective-permute-start.3 = (bf16[8,16,1024]{2,1,0:T(8,128)(2,1)S(1)}, bf16[8,16,1024]{2,1,0:T(8,128)(2,1)S(1)}, u32[]{:S(2)}, u32[]{:S(2)}) collective-permute-start(bf16[8,16,1024]{2,1,0:T(8,128)(2,1)S(1)} %all_to_all.10.q_ref), channel_id=1, source_target_pairs={{128,0},{192,64},{0,128},{64,192},{129,1},{193,65},{1,129},{65,193... | collective-permute-start | bytes 786440 | tf_op jit(solution)/shard_map/ppermute | solution.py:218
  29.1 1.3 %collective-permute-start.1 = (bf16[8,16,1024]{2,1,0:T(8,128)(2,1)S(1)}, bf16[8,16,1024]{2,1,0:T(8,128)(2,1)S(1)}, u32[]{:S(2)}, u32[]{:S(2)}) collective-permute-start(bf16[8,16,1024]{2,1,0:T(8,128)(2,1)S(1)} %all_to_all.10.q_ref), channel_id=1, source_target_pairs={{64,0},{128,64},{192,128},{0,192},{65,1},{129,65},{193,129},{1,193... | collective-permute-start | bytes 786440 | tf_op jit(solution)/shard_map/ppermute | solution.py:218
  30.4 0.0 copy-done.12
  30.4 0.1 iota_compare_fusion
  30.5 0.0 copy-done.2
  30.5 1.9 %copy.14 = bf16[1,16,256,2,128]{4,2,1,3,0:T(8,128)(2,1)} copy(bf16[1,16,256,2,128]{4,3,2,1,0:T(2,128)(2,1)S(1)} %copy-done.2) | data formatting | bytes 4194304 | tf_op args[2]
  32.4 0.0 copy-done
  32.4 0.0 copy-done.4
  32.4 1.7 %collective-permute-done.5.q_ref = bf16[8,16,1024]{2,1,0:T(8,128)(2,1)S(1)} collective-permute-done((bf16[8,16,1024]{2,1,0:T(8,128)(2,1)S(1)}, bf16[8,16,1024]{2,1,0:T(8,128)(2,1)S(1)}, u32[]{:S(2)}, u32[]{:S(2)}) %collective-permute-start.5) | collective-permute-done | bytes 262176 | tf_op jit(solution)/shard_map/ppermute | solution.py:218
  34.1 0.0 collective-permute-done.par_hbm
  34.1 0.7 copy-done.10
  34.8 5.0 %shard_map.58 = bf16[8,16,1152]{2,1,0:T(8,128)(2,1)} custom-call(s32[1,128]{1,0:T(1,128)} %ids_ref.7, bf16[8,16,1024]{2,1,0:T(8,128)(2,1)} %copy-done.10, bf16[2,2,512,1024]{3,2,1,0:T(8,128)(2,1)} %bitcast.28, bf16[2,2,512,1024]{3,2,1,0:T(8,128)(2,1)} %collective-permute-done.par_hbm), custom_call_target="tpu_custom_call" | custom-call | flops 1073741824 | bytes 2097152 | tf_op jit(solution)/shard_map/pallas_call | solution.py:114
  39.8 2.7 %collective-permute-start.6 = (bf16[8,16,1152]{2,1,0:T(8,128)(2,1)}, bf16[8,16,1152]{2,1,0:T(8,128)(2,1)S(1)}, u32[]{:S(2)}, u32[]{:S(2)}) collective-permute-start(bf16[8,16,1152]{2,1,0:T(8,128)(2,1)} %shard_map.58), channel_id=1, source_target_pairs={{0,192},{64,0},{128,64},{192,128},{1,193},{65,1},{129,65},{193,129... | collective-permute-start | bytes 884744 | tf_op jit(solution)/shard_map/ppermute | solution.py:227
  42.5 0.0 collective-permute-done.3.q_ref
  42.5 0.7 copy-done.9
  43.2 5.0 %shard_map.57 = bf16[8,16,1152]{2,1,0:T(8,128)(2,1)} custom-call(s32[1,128]{1,0:T(1,128)} %ids_ref.7, bf16[8,16,1024]{2,1,0:T(8,128)(2,1)} %copy-done.9, bf16[2,2,512,1024]{3,2,1,0:T(8,128)(2,1)} %bitcast.29, bf16[2,2,512,1024]{3,2,1,0:T(8,128)(2,1)} %collective-permute-done.par_hbm), custom_call_target="tpu_custom_call" | custom-call | flops 1073741824 | bytes 2097152 | tf_op jit(solution)/shard_map/pallas_call | solution.py:114
  48.2 0.0 copy-start.1
  48.2 5.0 %collective-permute-start.4 = (bf16[8,16,1152]{2,1,0:T(8,128)(2,1)}, bf16[8,16,1152]{2,1,0:T(8,128)(2,1)S(1)}, u32[]{:S(2)}, u32[]{:S(2)}) collective-permute-start(bf16[8,16,1152]{2,1,0:T(8,128)(2,1)} %shard_map.57), channel_id=1, source_target_pairs={{0,128},{64,192},{128,0},{192,64},{1,129},{65,193},{129,1},{193,65... | collective-permute-start | bytes 884744 | tf_op jit(solution)/shard_map/ppermute | solution.py:227
  53.2 0.0 collective-permute-done.1.q_ref
  53.2 0.7 copy-done.8
  53.9 5.0 %shard_map.56 = bf16[8,16,1152]{2,1,0:T(8,128)(2,1)} custom-call(s32[1,128]{1,0:T(1,128)} %ids_ref.7, bf16[8,16,1024]{2,1,0:T(8,128)(2,1)} %copy-done.8, bf16[2,2,512,1024]{3,2,1,0:T(8,128)(2,1)} %bitcast.30, bf16[2,2,512,1024]{3,2,1,0:T(8,128)(2,1)} %collective-permute-done.par_hbm), custom_call_target="tpu_custom_call" | custom-call | flops 1073741824 | bytes 2097152 | tf_op jit(solution)/shard_map/pallas_call | solution.py:114
  58.9 1.7 %collective-permute-start.2 = (bf16[8,16,1152]{2,1,0:T(8,128)(2,1)}, bf16[8,16,1152]{2,1,0:T(8,128)(2,1)S(1)}, u32[]{:S(2)}, u32[]{:S(2)}) collective-permute-start(bf16[8,16,1152]{2,1,0:T(8,128)(2,1)} %shard_map.56), channel_id=1, source_target_pairs={{0,64},{64,128},{128,192},{192,0},{1,65},{65,129},{129,193},{193,1... | collective-permute-start | bytes 884744 | tf_op jit(solution)/shard_map/ppermute | solution.py:227
  60.5 0.0 copy-done.1
  60.5 0.5 fusion.7
  61.0 5.0 %shard_map.55.a_ref = bf16[8,16,1152]{2,1,0:T(8,128)(2,1)} custom-call(s32[1,128]{1,0:T(1,128)} %ids_ref.7, bf16[8,16,1024]{2,1,0:T(8,128)(2,1)} %copy-done.4, bf16[2,2,512,1024]{3,2,1,0:T(8,128)(2,1)} %bitcast.31, bf16[2,2,512,1024]{3,2,1,0:T(8,128)(2,1)} %collective-permute-done.par_hbm), custom_call_target="tpu_custom_call" | custom-call | flops 1073741824 | bytes 2097152 | tf_op jit(solution)/shard_map/pallas_call | solution.py:114
  66.0 0.0 collective-permute-done.6.d_ref
  66.0 0.0 copy-start.5
  66.0 0.0 collective-permute-done.4.c_ref
  66.0 0.0 copy-start.6
  66.0 1.3 %collective-permute-done.2.b_ref = bf16[8,16,1152]{2,1,0:T(8,128)(2,1)S(1)} collective-permute-done((bf16[8,16,1152]{2,1,0:T(8,128)(2,1)}, bf16[8,16,1152]{2,1,0:T(8,128)(2,1)S(1)}, u32[]{:S(2)}, u32[]{:S(2)}) %collective-permute-start.2) | collective-permute-done | bytes 294944 | tf_op jit(solution)/shard_map/ppermute | solution.py:227
  67.3 0.0 copy-done.5
  67.3 0.0 copy-done.6
  67.3 0.7 copy-done.7
  68.0 2.8 %shard_map.59 = bf16[8,16,1152]{2,1,0:T(8,128)(2,1)} custom-call(bf16[8,16,1152]{2,1,0:T(8,128)(2,1)} %shard_map.55.a_ref, bf16[8,16,1152]{2,1,0:T(8,128)(2,1)} %copy-done.7, bf16[8,16,1152]{2,1,0:T(8,128)(2,1)} %copy-done.6, bf16[8,16,1152]{2,1,0:T(8,128)(2,1)} %copy-done.5), custom_call_target="tpu_custom_call" | custom-call | tf_op jit(solution)/shard_map/pallas_call | solution.py:164
  70.8 3.4 %all-to-all-start.1 = ((bf16[8,16,1152]{2,1,0:T(8,128)(2,1)}), bf16[8,16,1152]{2,1,0:T(8,128)(2,1)S(1)}, u32[]{:S(2)}, u32[]{:S(2)}) async-start(bf16[8,16,1152]{2,1,0:T(8,128)(2,1)} %shard_map.59), calls=%async_computation.1 | async-start | bytes 589824 | tf_op jit(solution)/shard_map/all_to_all | solution.py:230
  74.2 0.2 fusion.1
  74.4 0.3 convolution_divide_fusion
  74.7 0.7 copy.15
  75.3 0.6 pad.4.sl_ref
  75.9 9.0 %all-to-all-done.1.p_ref = bf16[8,16,1152]{2,1,0:T(8,128)(2,1)S(1)} async-done(((bf16[8,16,1152]{2,1,0:T(8,128)(2,1)}), bf16[8,16,1152]{2,1,0:T(8,128)(2,1)S(1)}, u32[]{:S(2)}, u32[]{:S(2)}) %all-to-all-start.1) | async-done | bytes 294944 | tf_op jit(solution)/shard_map/all_to_all | solution.py:230
  84.9 0.7 copy-done.3
  85.7 2.0 %shard_map.60 = bf16[16,1024]{1,0:T(8,128)(2,1)} custom-call(bf16[8,16,1152]{2,1,0:T(8,128)(2,1)} %copy-done.3, f32[16,1024]{1,0:T(8,128)} %bitcast.34, f32[16,128]{1,0:T(8,128)} %pad.4.sl_ref), custom_call_target="tpu_custom_call" | custom-call | tf_op jit(solution)/shard_map/pallas_call | solution.py:186
  (12 shorter events, 0.0 us)
Async XLA Ops:
  0.0 3.8 %copy-start.11 = (bf16[1,16,1024]{2,1,0:T(8,128)(2,1)S(1)}, bf16[1,16,1024]{2,1,0:T(8,128)(2,1)}, u32[]{:S(2)}) copy-start(bf16[1,16,1024]{2,1,0:T(8,128)(2,1)} %param.5) | copy-start | bytes 98308
  0.0 30.4 %copy-start.12 = (s32[1,16]{1,0:T(1,128)S(1)}, s32[1,16]{1,0:T(1,128)}, u32[]{:S(2)}) copy-start(s32[1,16]{1,0:T(1,128)} %param.8) | copy-start | bytes 196
  0.0 30.5 %copy-start.2 = (bf16[1,16,256,2,128]{4,3,2,1,0:T(2,128)(2,1)S(1)}, bf16[1,16,256,2,128]{4,3,2,1,0:T(2,128)(2,1)}, u32[]{:S(2)}) copy-start(bf16[1,16,256,2,128]{4,3,2,1,0:T(2,128)(2,1)} %param.7) | copy-start | bytes 6291460
  3.7 28.7 %copy-start = (bf16[1,2,512,2,1024]{4,2,3,1,0:T(8,128)(2,1)}, bf16[1,2,512,2,1024]{4,2,3,1,0:T(8,128)(2,1)S(1)}, u32[]{:S(2)}) copy-start(bf16[1,2,512,2,1024]{4,2,3,1,0:T(8,128)(2,1)S(1)} %copy.13) | copy-start | bytes 12582916
  3.7 30.5 %collective-permute-start = (bf16[2,2,512,1024]{3,2,1,0:T(8,128)(2,1)S(1)}, bf16[2,2,512,1024]{3,2,1,0:T(8,128)(2,1)}, u32[]{:S(2)}, u32[]{:S(2)}) collective-permute-start(bf16[2,2,512,1024]{3,2,1,0:T(8,128)(2,1)S(1)} %bitcast.27), channel_id=1, source_target_pairs={{0,4},{4,0},{1,5},{5,1},{2,6},{6,2},{3,7},{7,3},{8,12},{12,8},{9,1... | collective-permute-start | bytes 12582920 | tf_op jit(solution)/shard_map/ppermute | solution.py:212
  24.6 7.8 %copy-start.4 = (bf16[8,16,1024]{2,1,0:T(8,128)(2,1)}, bf16[8,16,1024]{2,1,0:T(8,128)(2,1)S(1)}, u32[]{:S(2)}) copy-start(bf16[8,16,1024]{2,1,0:T(8,128)(2,1)S(1)} %all_to_all.10.q_ref) | copy-start | bytes 786436
  24.6 9.5 %collective-permute-start.5 = (bf16[8,16,1024]{2,1,0:T(8,128)(2,1)S(1)}, bf16[8,16,1024]{2,1,0:T(8,128)(2,1)S(1)}, u32[]{:S(2)}, u32[]{:S(2)}) collective-permute-start(bf16[8,16,1024]{2,1,0:T(8,128)(2,1)S(1)} %all_to_all.10.q_ref), channel_id=1, source_target_pairs={{192,0},{0,64},{64,128},{128,192},{193,1},{1,65},{65,129},{129,193... | collective-permute-start | bytes 786440 | tf_op jit(solution)/shard_map/ppermute | solution.py:218
  26.2 16.4 %collective-permute-start.3 = (bf16[8,16,1024]{2,1,0:T(8,128)(2,1)S(1)}, bf16[8,16,1024]{2,1,0:T(8,128)(2,1)S(1)}, u32[]{:S(2)}, u32[]{:S(2)}) collective-permute-start(bf16[8,16,1024]{2,1,0:T(8,128)(2,1)S(1)} %all_to_all.10.q_ref), channel_id=1, source_target_pairs={{128,0},{192,64},{0,128},{64,192},{129,1},{193,65},{1,129},{65,193... | collective-permute-start | bytes 786440 | tf_op jit(solution)/shard_map/ppermute | solution.py:218
  29.1 24.1 %collective-permute-start.1 = (bf16[8,16,1024]{2,1,0:T(8,128)(2,1)S(1)}, bf16[8,16,1024]{2,1,0:T(8,128)(2,1)S(1)}, u32[]{:S(2)}, u32[]{:S(2)}) collective-permute-start(bf16[8,16,1024]{2,1,0:T(8,128)(2,1)S(1)} %all_to_all.10.q_ref), channel_id=1, source_target_pairs={{64,0},{128,64},{192,128},{0,192},{65,1},{129,65},{193,129},{1,193... | collective-permute-start | bytes 786440 | tf_op jit(solution)/shard_map/ppermute | solution.py:218
  34.1 0.7 copy-start.10
  39.8 26.2 %collective-permute-start.6 = (bf16[8,16,1152]{2,1,0:T(8,128)(2,1)}, bf16[8,16,1152]{2,1,0:T(8,128)(2,1)S(1)}, u32[]{:S(2)}, u32[]{:S(2)}) collective-permute-start(bf16[8,16,1152]{2,1,0:T(8,128)(2,1)} %shard_map.58), channel_id=1, source_target_pairs={{0,192},{64,0},{128,64},{192,128},{1,193},{65,1},{129,65},{193,129... | collective-permute-start | bytes 884744 | tf_op jit(solution)/shard_map/ppermute | solution.py:227
  42.5 0.7 copy-start.9
  48.2 12.3 %copy-start.1 = (bf16[1,16,256,2,128]{4,2,1,3,0:T(8,128)(2,1)S(1)}, bf16[1,16,256,2,128]{4,2,1,3,0:T(8,128)(2,1)}, u32[]{:S(2)}) copy-start(bf16[1,16,256,2,128]{4,2,1,3,0:T(8,128)(2,1)} %copy.14) | copy-start | bytes 6291460
  48.2 17.8 %collective-permute-start.4 = (bf16[8,16,1152]{2,1,0:T(8,128)(2,1)}, bf16[8,16,1152]{2,1,0:T(8,128)(2,1)S(1)}, u32[]{:S(2)}, u32[]{:S(2)}) collective-permute-start(bf16[8,16,1152]{2,1,0:T(8,128)(2,1)} %shard_map.57), channel_id=1, source_target_pairs={{0,128},{64,192},{128,0},{192,64},{1,129},{65,193},{129,1},{193,65... | collective-permute-start | bytes 884744 | tf_op jit(solution)/shard_map/ppermute | solution.py:227
  53.2 0.7 copy-start.8
  58.9 8.4 %collective-permute-start.2 = (bf16[8,16,1152]{2,1,0:T(8,128)(2,1)}, bf16[8,16,1152]{2,1,0:T(8,128)(2,1)S(1)}, u32[]{:S(2)}, u32[]{:S(2)}) collective-permute-start(bf16[8,16,1152]{2,1,0:T(8,128)(2,1)} %shard_map.56), channel_id=1, source_target_pairs={{0,64},{64,128},{128,192},{192,0},{1,65},{65,129},{129,193},{193,1... | collective-permute-start | bytes 884744 | tf_op jit(solution)/shard_map/ppermute | solution.py:227
  66.0 1.3 %copy-start.5 = (bf16[8,16,1152]{2,1,0:T(8,128)(2,1)}, bf16[8,16,1152]{2,1,0:T(8,128)(2,1)S(1)}, u32[]{:S(2)}) copy-start(bf16[8,16,1152]{2,1,0:T(8,128)(2,1)S(1)} %collective-permute-done.6.d_ref) | copy-start | bytes 884740
  66.0 1.3 %copy-start.6 = (bf16[8,16,1152]{2,1,0:T(8,128)(2,1)}, bf16[8,16,1152]{2,1,0:T(8,128)(2,1)S(1)}, u32[]{:S(2)}) copy-start(bf16[8,16,1152]{2,1,0:T(8,128)(2,1)S(1)} %collective-permute-done.4.c_ref) | copy-start | bytes 884740
  67.3 0.7 copy-start.7
  70.8 14.2 %all-to-all-start.1 = ((bf16[8,16,1152]{2,1,0:T(8,128)(2,1)}), bf16[8,16,1152]{2,1,0:T(8,128)(2,1)S(1)}, u32[]{:S(2)}, u32[]{:S(2)}) async-start(bf16[8,16,1152]{2,1,0:T(8,128)(2,1)} %shard_map.59), calls=%async_computation.1 | async-start | bytes 589824 | tf_op jit(solution)/shard_map/all_to_all | solution.py:230
  84.9 0.7 copy-start.3

commit v2 on v1

--- a/solution.py
+++ b/solution.py
@@ -14,6 +14,7 @@
 REP = 8
 C2 = HD ** (-0.5) * math.log2(math.e)
 BIG = 1e30
+VMEM_LIMIT = 28 * 2**20
 F32 = jnp.float32
 BF16 = jnp.bfloat16
 
@@ -35,24 +36,29 @@
     return (hi + pltpu.roll(mid, REP, 1) + pltpu.roll(lo, 2 * REP, 1)).astype(BF16)
 
 
-def _prompt_kernel(distance, ids_ref, q_ref, own_hbm, par_hbm, o_ref, kv_ref, s_ref, sem):
-    zs, row_dev = q_ref.shape[:2]
+def _prompt_kernel(distances, ids_ref, *refs):
+    n = len(distances)
+    q_refs, (own_hbm, par_hbm), o_refs = refs[:n], refs[n : n + 2], refs[n + 2 : 2 * n + 2]
+    kv_ref, s_ref, sem = refs[2 * n + 2 :]
+    zs, row_dev = q_refs[0].shape[:2]
     per = zs // 2
     rows = per * row_dev
     span = own_hbm.shape[2]
     width = 2 * HD
     n_y = own_hbm.shape[3] // width
-    at = pl.multiple_of(lax.rem(lax.axis_index("y") + distance, n_y) * width, width)
+    y = lax.axis_index("y")
     copies = []
-    for which in range(2):
-        for k, ref in enumerate((own_hbm, par_hbm)):
-            copy = pltpu.make_async_copy(
-                ref.at[:, which, :, pl.ds(at, width)],
-                kv_ref.at[which, :, pl.ds(k * span, span), :],
-                sem.at[2 * which + k],
-            )
-            copy.start()
-            copies.append(copy)
+    for i, distance in enumerate(distances):
+        at = pl.multiple_of(lax.rem(y + distance, n_y) * width, width)
+        for which in range(2):
+            for k, ref in enumerate((own_hbm, par_hbm)):
+                copy = pltpu.make_async_copy(
+                    ref.at[:, which, :, pl.ds(at, width)],
+                    kv_ref.at[i, which, :, pl.ds(k * span, span), :],
+                    sem.at[len(copies)],
+                )
+                copy.start()
+                copies.append(copy)
 
     total = ids_ref.shape[1]
     shape = (per, row_dev, total)
@@ -64,23 +70,27 @@
     member = jnp.sum(jnp.where(lane == source, ids, 0.0), axis=1, keepdims=True)
     member = jnp.broadcast_to(member, (rows, HD))
     lane = lax.broadcasted_iota(jnp.int32, (rows, HD), 1)
-
-    def scores(h):
-        q = q_ref[h * per : (h + 1) * per].reshape(rows, REP * HD)
-        q = jnp.concatenate([q[:, r * HD : (r + 1) * HD] for r in range(REP)], axis=0)
-        one = jnp.concatenate([member] * REP, axis=0)
-        q = jnp.concatenate([q * (1.0 - one).astype(BF16), q * one.astype(BF16)], axis=1)
+    keep = ((1.0 - member).astype(BF16), member.astype(BF16))
+
+    def scores(i, h):
+        q = q_refs[i][h * per : (h + 1) * per].reshape(rows, REP * HD)
         lanes = slice(h * HD, (h + 1) * HD)
-        k = jnp.concatenate([kv_ref[0, 0, :, lanes], kv_ref[0, 1, :, lanes]], axis=1)
-        s = _dot_t(q, k)
-        s_ref[h] = s
-        return jnp.max(s, axis=1, keepdims=True) * C2
-
-    def attend(h, peak):
+        k = jnp.concatenate([kv_ref[i, 0, 0, :, lanes], kv_ref[i, 0, 1, :, lanes]], axis=1)
+        tops = []
+        half = REP // 2
+        for part in range(2):
+            block = [q[:, r * HD : (r + 1) * HD] for r in range(part * half, (part + 1) * half)]
+            block = [jnp.concatenate([x * keep[0], x * keep[1]], axis=1) for x in block]
+            s = _dot_t(jnp.concatenate(block, axis=0), k)
+            s_ref[h, part * half * rows : (part + 1) * half * rows] = s
+            tops.append(jnp.max(s, axis=1, keepdims=True) * C2)
+        return jnp.concatenate(tops, axis=0)
+
+    def attend(i, h, peak):
         w = jnp.exp2(s_ref[h] * C2 - peak)
         totals = jnp.sum(w, axis=1, keepdims=True)
         lanes = slice(h * HD, (h + 1) * HD)
-        v = jnp.concatenate([kv_ref[1, 0, :, lanes], kv_ref[1, 1, :, lanes]], axis=1)
+        v = jnp.concatenate([kv_ref[i, 1, 0, :, lanes], kv_ref[i, 1, 1, :, lanes]], axis=1)
         acc = jnp.dot(w.astype(BF16), v, preferred_element_type=F32)
         inverse = 1.0 / totals
         weight = jnp.ones((rows, HD), F32)
@@ -89,45 +99,45 @@
         for r in range(REP):
             sl = slice(r * rows, (r + 1) * rows)
             o = jnp.where(member > 0.5, acc[sl, HD:], acc[sl, :HD]) * inverse[sl]
-            o_ref[zone, :, r * HD : (r + 1) * HD] = o.astype(BF16).reshape(per, row_dev, HD)
+            o = o.astype(BF16).reshape(per, row_dev, HD)
+            o_refs[i][zone, :, r * HD : (r + 1) * HD] = o
             weight = jnp.where(lane == r, totals[sl], weight)
             top = jnp.where(lane == r, peak[sl], top)
         stats = _stats(top + jnp.log2(weight))
-        o_ref[zone, :, REP * HD :] = stats.reshape(per, row_dev, HD)
-
-    copies[0].wait()
-    copies[1].wait()
-    peak0 = scores(0)
-    peak1 = scores(1)
-    copies[2].wait()
-    copies[3].wait()
-    attend(0, peak0)
-    attend(1, peak1)
-
-
-def _prompt(distance, ids, q, own, par):
-    zs, row_dev, width = q.shape
+        o_refs[i][zone, :, REP * HD :] = stats.reshape(per, row_dev, HD)
+
+    for i in range(n):
+        for copy in copies[4 * i : 4 * i + 4]:
+            copy.wait()
+        peaks = [scores(i, h) for h in range(2)]
+        for h in range(2):
+            attend(i, h, peaks[h])
+
+
+def _prompt(distances, ids, qs, own, par):
+    n = len(distances)
+    zs, row_dev, width = qs[0].shape
     span = own.shape[2]
     rows = zs // 2 * row_dev
     vmem = pl.BlockSpec(memory_space=pltpu.VMEM)
     hbm = pl.BlockSpec(memory_space=pl.ANY)
     return pl.pallas_call(
-        functools.partial(_prompt_kernel, distance),
-        out_shape=jax.ShapeDtypeStruct((zs, row_dev, width + HD), BF16),
-        in_specs=[vmem, vmem, hbm, hbm],
-        out_specs=vmem,
+        functools.partial(_prompt_kernel, distances),
+        out_shape=[jax.ShapeDtypeStruct((zs, row_dev, width + HD), BF16)] * n,
+        in_specs=[vmem] * (n + 1) + [hbm, hbm],
+        out_specs=[vmem] * n,
         scratch_shapes=[
-            pltpu.VMEM((2, 2, 2 * span, 2 * HD), BF16),
+            pltpu.VMEM((n, 2, 2, 2 * span, 2 * HD), BF16),
             pltpu.VMEM((2, rows * REP, 2 * span), F32),
-            pltpu.SemaphoreType.DMA((4,)),
+            pltpu.SemaphoreType.DMA((4 * n,)),
         ],
-        compiler_params=pltpu.CompilerParams(vmem_limit_bytes=58 * 2**20),
+        compiler_params=pltpu.CompilerParams(vmem_limit_bytes=VMEM_LIMIT),
         cost_estimate=pl.CostEstimate(
-            flops=2 * 2 * 2 * rows * REP * 2 * span * 2 * HD,
-            bytes_accessed=2 * 2 * 4 * span * HD * 2,
-            transcendentals=2 * rows * REP * 2 * span,
+            flops=n * 2 * 2 * 2 * rows * REP * 2 * span * 2 * HD,
+            bytes_accessed=n * 2 * 2 * 4 * span * HD * 2,
+            transcendentals=n * 2 * rows * REP * 2 * span,
         ),
-    )(ids, q, own, par)
+    )(ids, *qs, own, par)
 
 
 def _lse(x):
@@ -164,7 +174,7 @@
     return pl.pallas_call(
         _merge_kernel,
         out_shape=jax.ShapeDtypeStruct(parts[0].shape, BF16),
-        compiler_params=pltpu.CompilerParams(vmem_limit_bytes=58 * 2**20),
+        compiler_params=pltpu.CompilerParams(vmem_limit_bytes=VMEM_LIMIT),
     )(*parts)
 
 
@@ -186,7 +196,7 @@
     return pl.pallas_call(
         _final_kernel,
         out_shape=jax.ShapeDtypeStruct(suffix_o.shape, BF16),
-        compiler_params=pltpu.CompilerParams(vmem_limit_bytes=58 * 2**20),
+        compiler_params=pltpu.CompilerParams(vmem_limit_bytes=VMEM_LIMIT),
     )(parts, suffix_o, suffix_l2)
 
 
@@ -220,12 +230,10 @@
 
     suffix_o, suffix_l2 = _suffix(q, suffix_kv[0], suffix_len[0])
 
-    parts = []
-    for d in range(n_y):
-        part = _prompt(d, group_of, qs[d], own, par)
-        if d:
-            part = lax.ppermute(part, "y", [(i, (i + d) % n_y) for i in range(n_y)])
-        parts.append(part)
+    away = tuple(range(1, n_y))
+    parts = list(_prompt((0,), group_of, qs[:1], own, par))
+    for d, part in zip(away, _prompt(away, group_of, qs[1:], own, par)):
+        parts.append(lax.ppermute(part, "y", [(i, (i + d) % n_y) for i in range(n_y)]))
     merged = _merge(parts)
     got = lax.all_to_all(merged, ("zh", "zl"), 0, 0, tiled=True)
     return _final(got, suffix_o, suffix_l2)[None]

time: 88.1 us -> 84.4 us (0.958)
  waiting for transfers between devices: 12 us -> 35.3 us
  Pallas kernels: 24.6 us -> 11.2 us
  starting transfers between devices: 18.7 us -> 11.5 us
  local copies, waits for them, and re-layouts: 10.3 us -> 4.21 us
    pallas_call x4 -> x2, Pallas kernels: 19.9 us -> 8.68 us  [_prompt(): pl.pallas_call(functools.partial(_prompt_kernel, distances), out_shape=[j...]
    ppermute x3, waiting for transfers between devices: 1.74 us -> 12.9 us  [_shards(): lax.ppermute(q0, 'y', [((i + d) % n_y, i) for i in range(n_y)])]
    ppermute x3, waiting for transfers between devices: 1.27 us -> 11.1 us  [_shards(): lax.ppermute(part, 'y', [(i, (i + d) % n_y) for i in range(n_y)])]
    ppermute x3, starting transfers between devices: 9.38 us -> 3.33 us  [_shards(): lax.ppermute(part, 'y', [(i, (i + d) % n_y) for i in range(n_y)])]
    unnamed x30 -> x12, local copies, waits for them, and re-layouts: 9.71 us -> 4.18 us
    all_to_all x1, waiting for transfers between devices: 9.02 us -> 11.3 us  [_shards(): got = lax.all_to_all(merged, ('zh', 'zl'), 0, 0, tiled=True)]
    ppermute x3, starting transfers between devices: 5.83 us -> 4.61 us  [_shards(): lax.ppermute(q0, 'y', [((i + d) % n_y, i) for i in range(n_y)])]
    pallas_call x1, Pallas kernels: 2.77 us -> 1.56 us  [_merge(): pl.pallas_call(_merge_kernel, out_shape=jax.ShapeDtypeStruct(parts[0].sha...]
  transfers between devices with their start and end apart: 8 -> 8, of which waited for: 3 -> 5; matrix products, arithmetic and copies ran while one was open for 5% -> 2% of each run, Pallas kernels for 23% -> 3%
where the time goes in v2:
time: 84.4 us; the launch traced here: 84.1 us
  waiting for transfers between devices  35.3 us (42%)
  blocking collectives  20.8 us (25%)
  starting transfers between devices  11.5 us (14%)
  Pallas kernels  11.2 us (13%)
  local copies, waits for them, and re-layouts  4.21 us (5%)
    all_to_all x1, blocking collectives, _shards(): q0 = lax.all_to_all(spread, ('zh', 'zl'), 0, 0, tiled=True)  20.8 us
    ppermute x3, waiting for transfers between devices, _shards(): lax.ppermute(q0, 'y', [((i + d) % n_y, i) for i in range(n_y)])  12.9 us
    all_to_all x1, waiting for transfers between devices, _shards(): got = lax.all_to_all(merged, ('zh', 'zl'), 0, 0, tiled=True)  11.3 us
    ppermute x3, waiting for transfers between devices, _shards(): lax.ppermute(part, 'y', [(i, (i + d) % n_y) for i in range(n_y)])  11.1 us
    pallas_call x2, Pallas kernels, _prompt(): pl.pallas_call(functools.partial(_prompt_kernel, distances), out_shape=[j...  8.68 us
    ppermute x3, starting transfers between devices, _shards(): lax.ppermute(q0, 'y', [((i + d) % n_y, i) for i in range(n_y)])  4.61 us
    unnamed x12, local copies, waits for them, and re-layouts  4.18 us
    all_to_all x1, starting transfers between devices, _shards(): got = lax.all_to_all(merged, ('zh', 'zl'), 0, 0, tiled=True)  3.42 us
  transfers between devices with their start and end apart: 8, of which 5 were waited for; matrix products, arithmetic and copies ran while one was open for 2% of the time, Pallas kernels for 3%

profile of v2, /device:TPU:2, one launch (start us, length us, event | category | flops | bytes accessed | tf_op | source)
XLA Modules:
  0.0 84.1 jit_solution(4007460590889521037)
XLA Ops:
  0.0 0.0 copy-start.2
  0.0 0.0 copy-start.1
  0.0 3.6 %copy.13 = bf16[1,2,512,2,1024]{4,2,3,1,0:T(8,128)(2,1)S(1)} copy(bf16[1,2,512,2,1024]{4,3,2,1,0:T(2,128)(2,1)} %param.6) | data formatting | bytes 8388608 | tf_op args[1]
  3.7 0.1 collective-permute-start
  3.8 0.0 copy-done.2
  3.8 20.8 %all_to_all.10.refs_0_ = bf16[8,16,1024]{2,1,0:T(8,128)(2,1)S(1)} all-to-all(bf16[8,16,1024]{2,1,0:T(8,128)(2,1)S(1)} %broadcast_in_dim.26), channel_id=1, replica_groups=mesh['y'=4,'zh'=2,'zl'=4,'core'=2,'grp'=4] {'zh','zl'}, dimensions={0} | all-to-all | bytes 524288 | tf_op jit(solution)/shard_map/all_to_all | solution.py:226
  24.6 0.0 copy-start.3
  24.6 0.0 copy-start
  24.6 3.0 %collective-permute-start.1 = (bf16[8,16,1024]{2,1,0:T(8,128)(2,1)S(1)}, bf16[8,16,1024]{2,1,0:T(8,128)(2,1)S(1)}, u32[]{:S(2)}, u32[]{:S(2)}) collective-permute-start(bf16[8,16,1024]{2,1,0:T(8,128)(2,1)S(1)} %all_to_all.10.refs_0_), channel_id=1, source_target_pairs={{64,0},{128,64},{192,128},{0,192},{65,1},{129,65},{193,129},{1,193... | collective-permute-start | bytes 786440 | tf_op jit(solution)/shard_map/ppermute | solution.py:228
  27.6 0.6 collective-permute-start.2
  28.2 1.0 %collective-permute-start.3 = (bf16[8,16,1024]{2,1,0:T(8,128)(2,1)S(1)}, bf16[8,16,1024]{2,1,0:T(8,128)(2,1)S(1)}, u32[]{:S(2)}, u32[]{:S(2)}) collective-permute-start(bf16[8,16,1024]{2,1,0:T(8,128)(2,1)S(1)} %all_to_all.10.refs_0_), channel_id=1, source_target_pairs={{192,0},{0,64},{64,128},{128,192},{193,1},{1,65},{65,129},{129,193... | collective-permute-start | bytes 786440 | tf_op jit(solution)/shard_map/ppermute | solution.py:228
  29.2 0.0 copy-done.1
  29.2 0.5 copy.14
  29.7 0.0 copy-done.3
  29.7 0.1 iota_compare_fusion
  29.8 9.2 %collective-permute-done.1.refs_0_ = bf16[8,16,1024]{2,1,0:T(8,128)(2,1)S(1)} collective-permute-done((bf16[8,16,1024]{2,1,0:T(8,128)(2,1)S(1)}, bf16[8,16,1024]{2,1,0:T(8,128)(2,1)S(1)}, u32[]{:S(2)}, u32[]{:S(2)}) %collective-permute-start.1) | collective-permute-done | bytes 262176 | tf_op jit(solution)/shard_map/ppermute | solution.py:228
  39.0 0.0 collective-permute-done.2.refs_1_
  39.0 3.7 %collective-permute-done.3.refs_2_ = bf16[8,16,1024]{2,1,0:T(8,128)(2,1)S(1)} collective-permute-done((bf16[8,16,1024]{2,1,0:T(8,128)(2,1)S(1)}, bf16[8,16,1024]{2,1,0:T(8,128)(2,1)S(1)}, u32[]{:S(2)}, u32[]{:S(2)}) %collective-permute-start.3) | collective-permute-done | bytes 262176 | tf_op jit(solution)/shard_map/ppermute | solution.py:228
  42.7 0.0 collective-permute-done.refs_2_.refs_4_
  42.7 0.0 copy-done
  42.7 6.4 %shard_map.56 = (bf16[8,16,1152]{2,1,0:T(8,128)(2,1)S(1)}, bf16[8,16,1152]{2,1,0:T(8,128)(2,1)S(1)}, bf16[8,16,1152]{2,1,0:T(8,128)(2,1)S(1)}) custom-call(s32[1,128]{1,0:T(1,128)S(1)} %copy-done, bf16[8,16,1024]{2,1,0:T(8,128)(2,1)S(1)} %collective-permute-done.1.refs_0_, bf16[8,16,1024]{2,1,0:T(8,128)(2,1)S(1)} %collective-permute-done.2.refs_1_, ...), custom_call_target="tpu_custom_call" | custom-call | flops 3221225472 | bytes 6291456 | tf_op jit(solution)/shard_map/pallas_call | solution.py:124
  49.1 0.1 collective-permute-start.4
  49.2 2.1 %collective-permute-start.5 = (bf16[8,16,1152]{2,1,0:T(8,128)(2,1)S(1)}, bf16[8,16,1152]{2,1,0:T(8,128)(2,1)S(1)}, u32[]{:S(2)}, u32[]{:S(2)}) collective-permute-start(bf16[8,16,1152]{2,1,0:T(8,128)(2,1)S(1)} %get-tuple-element.9), channel_id=1, source_target_pairs={{0,128},{64,192},{128,0},{192,64},{1,129},{65,193},{129,1},{193,65... | collective-permute-start | bytes 884744 | tf_op jit(solution)/shard_map/ppermute | solution.py:236
  51.3 1.2 %collective-permute-start.6 = (bf16[8,16,1152]{2,1,0:T(8,128)(2,1)S(1)}, bf16[8,16,1152]{2,1,0:T(8,128)(2,1)S(1)}, u32[]{:S(2)}, u32[]{:S(2)}) collective-permute-start(bf16[8,16,1152]{2,1,0:T(8,128)(2,1)S(1)} %get-tuple-element.10), channel_id=1, source_target_pairs={{0,192},{64,0},{128,64},{192,128},{1,193},{65,1},{129,65},{193,129... | collective-permute-start | bytes 884744 | tf_op jit(solution)/shard_map/ppermute | solution.py:236
  52.5 0.5 fusion.7
  52.9 2.3 %shard_map.55.a_ref = bf16[8,16,1152]{2,1,0:T(8,128)(2,1)S(1)} custom-call(s32[1,128]{1,0:T(1,128)S(1)} %copy-done, bf16[8,16,1024]{2,1,0:T(8,128)(2,1)S(1)} %all_to_all.10.refs_0_, bf16[2,2,512,1024]{3,2,1,0:T(8,128)(2,1)S(1)} %bitcast.29, bf16[2,2,512,1024]{3,2,1,0:T(8,128)(2,1)S(1)} %collective-permute-done.refs_2_.refs_4_), custom_call_target="tpu_custom_call" | custom-call | flops 1073741824 | bytes 2097152 | tf_op jit(solution)/shard_map/pallas_call | solution.py:124
  55.2 10.5 %collective-permute-done.4.b_ref = bf16[8,16,1152]{2,1,0:T(8,128)(2,1)S(1)} collective-permute-done((bf16[8,16,1152]{2,1,0:T(8,128)(2,1)S(1)}, bf16[8,16,1152]{2,1,0:T(8,128)(2,1)S(1)}, u32[]{:S(2)}, u32[]{:S(2)}) %collective-permute-start.4) | collective-permute-done | bytes 294944 | tf_op jit(solution)/shard_map/ppermute | solution.py:236
  65.7 0.0 collective-permute-done.5.c_ref
  65.7 0.6 collective-permute-done.6.d_ref
  66.3 1.6 %shard_map.57 = bf16[8,16,1152]{2,1,0:T(8,128)(2,1)} custom-call(bf16[8,16,1152]{2,1,0:T(8,128)(2,1)S(1)} %shard_map.55.a_ref, bf16[8,16,1152]{2,1,0:T(8,128)(2,1)S(1)} %collective-permute-done.4.b_ref, bf16[8,16,1152]{2,1,0:T(8,128)(2,1)S(1)} %collective-permute-done.5.c_ref, bf16[8,16,1152]{2,1,0:T(8,128)(2,1)S(1)} %collective-permute-done.6.d_ref), custom_call_target="tpu_custom_call" | custom-call | tf_op jit(solution)/shard_map/pallas_call | solution.py:174
  67.9 3.4 %all-to-all-start.1 = ((bf16[8,16,1152]{2,1,0:T(8,128)(2,1)}), bf16[8,16,1152]{2,1,0:T(8,128)(2,1)S(1)}, u32[]{:S(2)}, u32[]{:S(2)}) async-start(bf16[8,16,1152]{2,1,0:T(8,128)(2,1)} %shard_map.57), calls=%async_computation.1 | async-start | bytes 589824 | tf_op jit(solution)/shard_map/all_to_all | solution.py:238
  71.3 0.2 fusion.1
  71.5 0.3 convolution_divide_fusion
  71.8 11.3 %all-to-all-done.1.p_ref = bf16[8,16,1152]{2,1,0:T(8,128)(2,1)S(1)} async-done(((bf16[8,16,1152]{2,1,0:T(8,128)(2,1)}), bf16[8,16,1152]{2,1,0:T(8,128)(2,1)S(1)}, u32[]{:S(2)}, u32[]{:S(2)}) %all-to-all-start.1) | async-done | bytes 294944 | tf_op jit(solution)/shard_map/all_to_all | solution.py:238
  83.1 1.0 %shard_map.58 = bf16[16,1024]{1,0:T(8,128)(2,1)} custom-call(bf16[8,16,1152]{2,1,0:T(8,128)(2,1)S(1)} %all-to-all-done.1.p_ref, f32[16,1024]{1,0:T(8,128)S(1)} %bitcast.30, f32[16,128]{1,0:T(8,128)S(1)} %pad.4.sl_ref), custom_call_target="tpu_custom_call" | custom-call | tf_op jit(solution)/shard_map/pallas_call | solution.py:196
  (5 shorter events, 0.1 us)
Async XLA Ops:
  0.0 3.8 %copy-start.2 = (bf16[1,16,1024]{2,1,0:T(8,128)(2,1)S(1)}, bf16[1,16,1024]{2,1,0:T(8,128)(2,1)}, u32[]{:S(2)}) copy-start(bf16[1,16,1024]{2,1,0:T(8,128)(2,1)} %param.5) | copy-start | bytes 98308
  0.0 29.2 %copy-start.1 = (bf16[1,16,256,2,128]{4,3,2,1,0:T(2,128)(2,1)S(1)}, bf16[1,16,256,2,128]{4,3,2,1,0:T(2,128)(2,1)}, u32[]{:S(2)}) copy-start(bf16[1,16,256,2,128]{4,3,2,1,0:T(2,128)(2,1)} %param.7) | copy-start | bytes 6291460
  3.7 39.1 %collective-permute-start = (bf16[2,2,512,1024]{3,2,1,0:T(8,128)(2,1)S(1)}, bf16[2,2,512,1024]{3,2,1,0:T(8,128)(2,1)S(1)}, u32[]{:S(2)}, u32[]{:S(2)}) collective-permute-start(bf16[2,2,512,1024]{3,2,1,0:T(8,128)(2,1)S(1)} %bitcast.27), channel_id=1, source_target_pairs={{0,4},{4,0},{1,5},{5,1},{2,6},{6,2},{3,7},{7,3},{8,12},{12,8},{9,1... | collective-permute-start | bytes 12582920 | tf_op jit(solution)/shard_map/ppermute | solution.py:222
  24.6 5.1 %copy-start.3 = (s32[1,16]{1,0:T(1,128)S(1)}, s32[1,16]{1,0:T(1,128)}, u32[]{:S(2)}) copy-start(s32[1,16]{1,0:T(1,128)} %param.8) | copy-start | bytes 196
  24.6 18.1 %copy-start = (s32[1,128]{1,0:T(1,128)S(1)}, s32[1,128]{1,0:T(1,128)}, u32[]{:S(2)}) copy-start(s32[1,128]{1,0:T(1,128)} %ids_ref.3) | copy-start | bytes 1540
  24.6 14.4 %collective-permute-start.1 = (bf16[8,16,1024]{2,1,0:T(8,128)(2,1)S(1)}, bf16[8,16,1024]{2,1,0:T(8,128)(2,1)S(1)}, u32[]{:S(2)}, u32[]{:S(2)}) collective-permute-start(bf16[8,16,1024]{2,1,0:T(8,128)(2,1)S(1)} %all_to_all.10.refs_0_), channel_id=1, source_target_pairs={{64,0},{128,64},{192,128},{0,192},{65,1},{129,65},{193,129},{1,193... | collective-permute-start | bytes 786440 | tf_op jit(solution)/shard_map/ppermute | solution.py:228
  27.6 11.4 %collective-permute-start.2 = (bf16[8,16,1024]{2,1,0:T(8,128)(2,1)S(1)}, bf16[8,16,1024]{2,1,0:T(8,128)(2,1)S(1)}, u32[]{:S(2)}, u32[]{:S(2)}) collective-permute-start(bf16[8,16,1024]{2,1,0:T(8,128)(2,1)S(1)} %all_to_all.10.refs_0_), channel_id=1, source_target_pairs={{128,0},{192,64},{0,128},{64,192},{129,1},{193,65},{1,129},{65,193... | collective-permute-start | bytes 786440 | tf_op jit(solution)/shard_map/ppermute | solution.py:228
  28.2 14.5 %collective-permute-start.3 = (bf16[8,16,1024]{2,1,0:T(8,128)(2,1)S(1)}, bf16[8,16,1024]{2,1,0:T(8,128)(2,1)S(1)}, u32[]{:S(2)}, u32[]{:S(2)}) collective-permute-start(bf16[8,16,1024]{2,1,0:T(8,128)(2,1)S(1)} %all_to_all.10.refs_0_), channel_id=1, source_target_pairs={{192,0},{0,64},{64,128},{128,192},{193,1},{1,65},{65,129},{129,193... | collective-permute-start | bytes 786440 | tf_op jit(solution)/shard_map/ppermute | solution.py:228
  49.1 16.5 %collective-permute-start.4 = (bf16[8,16,1152]{2,1,0:T(8,128)(2,1)S(1)}, bf16[8,16,1152]{2,1,0:T(8,128)(2,1)S(1)}, u32[]{:S(2)}, u32[]{:S(2)}) collective-permute-start(bf16[8,16,1152]{2,1,0:T(8,128)(2,1)S(1)} %get-tuple-element.8), channel_id=1, source_target_pairs={{0,64},{64,128},{128,192},{192,0},{1,65},{65,129},{129,193},{193,1... | collective-permute-start | bytes 884744 | tf_op jit(solution)/shard_map/ppermute | solution.py:236
  49.2 16.5 %collective-permute-start.5 = (bf16[8,16,1152]{2,1,0:T(8,128)(2,1)S(1)}, bf16[8,16,1152]{2,1,0:T(8,128)(2,1)S(1)}, u32[]{:S(2)}, u32[]{:S(2)}) collective-permute-start(bf16[8,16,1152]{2,1,0:T(8,128)(2,1)S(1)} %get-tuple-element.9), channel_id=1, source_target_pairs={{0,128},{64,192},{128,0},{192,64},{1,129},{65,193},{129,1},{193,65... | collective-permute-start | bytes 884744 | tf_op jit(solution)/shard_map/ppermute | solution.py:236
  51.3 15.0 %collective-permute-start.6 = (bf16[8,16,1152]{2,1,0:T(8,128)(2,1)S(1)}, bf16[8,16,1152]{2,1,0:T(8,128)(2,1)S(1)}, u32[]{:S(2)}, u32[]{:S(2)}) collective-permute-start(bf16[8,16,1152]{2,1,0:T(8,128)(2,1)S(1)} %get-tuple-element.10), channel_id=1, source_target_pairs={{0,192},{64,0},{128,64},{192,128},{1,193},{65,1},{129,65},{193,129... | collective-permute-start | bytes 884744 | tf_op jit(solution)/shard_map/ppermute | solution.py:236
  67.9 15.3 %all-to-all-start.1 = ((bf16[8,16,1152]{2,1,0:T(8,128)(2,1)}), bf16[8,16,1152]{2,1,0:T(8,128)(2,1)S(1)}, u32[]{:S(2)}, u32[]{:S(2)}) async-start(bf16[8,16,1152]{2,1,0:T(8,128)(2,1)} %shard_map.57), calls=%async_computation.1 | async-start | bytes 589824 | tf_op jit(solution)/shard_map/all_to_all | solution.py:238

commit v3 on v2

--- a/solution.py
+++ b/solution.py
@@ -36,8 +36,13 @@
     return (hi + pltpu.roll(mid, REP, 1) + pltpu.roll(lo, 2 * REP, 1)).astype(BF16)
 
 
-def _prompt_kernel(distances, ids_ref, *refs):
-    n = len(distances)
+def _partners(y, core):
+    a, b = y + 1 - 2 * lax.rem(y, 2), 3 - y
+    return y, jnp.where(core == 0, a, b), jnp.where(core == 0, b, a), lax.rem(y + 2, 4)
+
+
+def _prompt_kernel(wanted, ids_ref, *refs):
+    n = len(wanted)
     q_refs, (own_hbm, par_hbm), o_refs = refs[:n], refs[n : n + 2], refs[n + 2 : 2 * n + 2]
     kv_ref, s_ref, sem = refs[2 * n + 2 :]
     zs, row_dev = q_refs[0].shape[:2]
@@ -45,11 +50,11 @@
     rows = per * row_dev
     span = own_hbm.shape[2]
     width = 2 * HD
-    n_y = own_hbm.shape[3] // width
-    y = lax.axis_index("y")
+    core = lax.axis_index("core")
+    partners = _partners(lax.axis_index("y"), core)
     copies = []
-    for i, distance in enumerate(distances):
-        at = pl.multiple_of(lax.rem(y + distance, n_y) * width, width)
+    for i, partner in enumerate(wanted):
+        at = pl.multiple_of(partners[partner] * width, width)
         for which in range(2):
             for k, ref in enumerate((own_hbm, par_hbm)):
                 copy = pltpu.make_async_copy(
@@ -63,7 +68,7 @@
     total = ids_ref.shape[1]
     shape = (per, row_dev, total)
     source = lax.broadcasted_iota(jnp.int32, shape, 0) * (2 * row_dev)
-    source += lax.axis_index("core") * row_dev + lax.broadcasted_iota(jnp.int32, shape, 1)
+    source += core * row_dev + lax.broadcasted_iota(jnp.int32, shape, 1)
     source = source.reshape(rows, total)
     lane = lax.broadcasted_iota(jnp.int32, (rows, total), 1)
     ids = jnp.broadcast_to(ids_ref[...].astype(F32), (rows, total))
@@ -114,15 +119,15 @@
             attend(i, h, peaks[h])
 
 
-def _prompt(distances, ids, qs, own, par):
-    n = len(distances)
+def _prompt(wanted, ids, qs, own, par):
+    n = len(wanted)
     zs, row_dev, width = qs[0].shape
     span = own.shape[2]
     rows = zs // 2 * row_dev
     vmem = pl.BlockSpec(memory_space=pltpu.VMEM)
     hbm = pl.BlockSpec(memory_space=pl.ANY)
     return pl.pallas_call(
-        functools.partial(_prompt_kernel, distances),
+        functools.partial(_prompt_kernel, wanted),
         out_shape=[jax.ShapeDtypeStruct((zs, row_dev, width + HD), BF16)] * n,
         in_specs=[vmem] * (n + 1) + [hbm, hbm],
         out_specs=[vmem] * n,
@@ -152,10 +157,10 @@
     return [e / total for e in es], top + jnp.log2(total)
 
 
-def _merge_kernel(a_ref, b_ref, c_ref, d_ref, o_ref):
-    lead = a_ref.shape[:2]
+def _merge_kernel(*all_refs):
+    *refs, o_ref = all_refs
+    lead = o_ref.shape[:2]
     rows = lead[0] * lead[1]
-    refs = (a_ref, b_ref, c_ref, d_ref)
     lane = lax.broadcasted_iota(jnp.int32, (rows, HD), 1)
     l2s = [_lse(ref[:, :, REP * HD :].reshape(rows, HD)) for ref in refs]
     l2s = [jnp.where(lane < REP, x, 0.0) for x in l2s]
@@ -215,26 +220,39 @@
     return o, l2
 
 
+def _pairs(which):
+    out = []
+    for y in range(4):
+        for core in range(2):
+            to = 3 - y if (which == 1) == (core == 1) else y ^ 1
+            out.append((2 * y + core, 2 * to + core))
+    return out
+
+
 def _shards(queries, prompt_kv, suffix_kv, suffix_len, group_of):
-    n_y = lax.axis_size("y")
     q = queries[0]
     own = jnp.transpose(prompt_kv[0], (0, 2, 1, 3))
-    par = lax.ppermute(own, "core", [(0, 1), (1, 0)])
 
     n_z = lax.axis_size("zh") * lax.axis_size("zl")
     spread = jnp.broadcast_to(q[None], (n_z, *q.shape))
     q0 = lax.all_to_all(spread, ("zh", "zl"), 0, 0, tiled=True)
-    qs = [q0] + [
-        lax.ppermute(q0, "y", [((i + d) % n_y, i) for i in range(n_y)]) for d in range(1, n_y)
-    ]
+    q0, own = lax.optimization_barrier((q0, own))
+    par = lax.ppermute(own, "core", [(0, 1), (1, 0)])
+    first = lax.ppermute(q0, ("y", "core"), _pairs(1))
+    second = lax.ppermute(q0, ("y", "core"), _pairs(2))
+    third = lax.ppermute(first, ("y", "core"), _pairs(2))
 
     suffix_o, suffix_l2 = _suffix(q, suffix_kv[0], suffix_len[0])
 
-    away = tuple(range(1, n_y))
-    parts = list(_prompt((0,), group_of, qs[:1], own, par))
-    for d, part in zip(away, _prompt(away, group_of, qs[1:], own, par)):
-        parts.append(lax.ppermute(part, "y", [(i, (i + d) % n_y) for i in range(n_y)]))
-    merged = _merge(parts)
+    def part(which, block):
+        return _prompt((which,), group_of, [block], own, par)[0]
+
+    part_second, third = lax.optimization_barrier((part(2, second), third))
+    back_second = lax.ppermute(part_second, ("y", "core"), _pairs(2))
+    back_third = lax.ppermute(part(3, third), ("y", "core"), _pairs(2))
+    merged = _merge([part(1, first), back_third])
+    back_first = lax.ppermute(merged, ("y", "core"), _pairs(1))
+    merged = _merge([part(0, q0), back_second, back_first])
     got = lax.all_to_all(merged, ("zh", "zl"), 0, 0, tiled=True)
     return _final(got, suffix_o, suffix_l2)[None]
 

time: 84.4 us -> 73.8 us (0.87)
  blocking collectives: 20.8 us -> 0 us
  starting transfers between devices: 11.5 us -> 23.6 us
  waiting for transfers between devices: 35.3 us -> 27.6 us
  local copies, waits for them, and re-layouts: 4.21 us -> 9.06 us
    all_to_all x1 -> x0, blocking collectives: 20.8 us -> none  [_shards(): q0 = lax.all_to_all(spread, ('zh', 'zl'), 0, 0, tiled=True)]
    ppermute x6, waiting for transfers between devices: 24 us -> 10 us  [the longest x1 3.65 us: _shards(): first = lax.ppermute(q0, ('y', 'core'), _pairs(1))]
    all_to_all x0 -> x1, starting transfers between devices: none -> 8.47 us  [_shards(): q0 = lax.all_to_all(spread, ('zh', 'zl'), 0, 0, tiled=True)]
    all_to_all x0 -> x1, waiting for transfers between devices: none -> 6.42 us  [_shards(): q0 = lax.all_to_all(spread, ('zh', 'zl'), 0, 0, tiled=True)]
    ppermute x6, starting transfers between devices: 7.95 us -> 11.7 us  [the longest x1 4.25 us: _shards(): third = lax.ppermute(first, ('y', 'core'), _pairs(2))]
    unnamed x12, local copies, waits for them, and re-layouts: 4.18 us -> 7.58 us
    broadcast_in_dim x1, local copies, waits for them, and re-layouts: 0.02 us -> 1.48 us  [_shards(): spread = jnp.broadcast_to(q[None], (n_z, *q.shape))]
    pallas_call x1 -> x2, Pallas kernels: 1.56 us -> 1.88 us  [_merge(): pl.pallas_call(_merge_kernel, out_shape=jax.ShapeDtypeStruct(parts[0].sha...]
  transfers between devices with their start and end apart: 8 -> 9, of which waited for: 5 -> 6; matrix products, arithmetic and copies ran while one was open for 2% -> 12% of each run, Pallas kernels for 3% -> 10%
where the time goes in v3:
time: 73.8 us; the launch traced here: 73.3 us
  waiting for transfers between devices  27.6 us (37%)
  starting transfers between devices  23.6 us (32%)
  Pallas kernels  11.8 us (16%)
  local copies, waits for them, and re-layouts  9.06 us (12%)
  matrix products  0.75 us (1%)
    all_to_all x1, waiting for transfers between devices, _shards(): got = lax.all_to_all(merged, ('zh', 'zl'), 0, 0, tiled=True)  11.2 us
    pallas_call x4, Pallas kernels, _prompt(): pl.pallas_call(functools.partial(_prompt_kernel, wanted), out_shape=[jax....  8.99 us
    all_to_all x1, starting transfers between devices, _shards(): q0 = lax.all_to_all(spread, ('zh', 'zl'), 0, 0, tiled=True)  8.47 us
    unnamed x12, local copies, waits for them, and re-layouts  7.58 us
    all_to_all x1, waiting for transfers between devices, _shards(): q0 = lax.all_to_all(spread, ('zh', 'zl'), 0, 0, tiled=True)  6.42 us
    ppermute x1, starting transfers between devices, _shards(): third = lax.ppermute(first, ('y', 'core'), _pairs(2))  4.25 us
    ppermute x1, waiting for transfers between devices, _shards(): first = lax.ppermute(q0, ('y', 'core'), _pairs(1))  3.65 us
    all_to_all x1, starting transfers between devices, _shards(): got = lax.all_to_all(merged, ('zh', 'zl'), 0, 0, tiled=True)  3.42 us
  transfers between devices with their start and end apart: 9, of which 6 were waited for; matrix products, arithmetic and copies ran while one was open for 12% of the time, Pallas kernels for 10%

profile of v3, /device:TPU:2, one launch (start us, length us, event | category | flops | bytes accessed | tf_op | source)
XLA Modules:
  0.0 73.3 jit_solution(8410730091740994586)
XLA Ops:
  0.0 1.5 %broadcast_in_dim.26 = bf16[8,16,1024]{2,1,0:T(8,128)(2,1)} broadcast(bf16[16,1024]{1,0:T(8,128)(2,1)} %bitcast.35), dimensions={1,2} | broadcast | bytes 294912 | tf_op jit(solution)/shard_map/broadcast_in_dim | solution.py:237
  1.5 8.5 %all-to-all-start = ((bf16[8,16,1024]{2,1,0:T(8,128)(2,1)}), bf16[8,16,1024]{2,1,0:T(8,128)(2,1)S(1)}, u32[]{:S(2)}, u32[]{:S(2)}) async-start(bf16[8,16,1024]{2,1,0:T(8,128)(2,1)} %broadcast_in_dim.26), calls=%async_computation | async-start | bytes 524288 | tf_op jit(solution)/shard_map/all_to_all | solution.py:238
  9.9 5.5 %copy.13 = bf16[1,2,512,2,1024]{4,2,3,1,0:T(8,128)(2,1)} copy(bf16[1,2,512,2,1024]{4,3,2,1,0:T(2,128)(2,1)} %param.6) | data formatting | bytes 8388608 | tf_op args[1]
  15.4 6.4 %all-to-all-done.refs_0_ = bf16[8,16,1024]{2,1,0:T(8,128)(2,1)S(1)} async-done(((bf16[8,16,1024]{2,1,0:T(8,128)(2,1)}), bf16[8,16,1024]{2,1,0:T(8,128)(2,1)S(1)}, u32[]{:S(2)}, u32[]{:S(2)}) %all-to-all-start) | async-done | bytes 262176 | tf_op jit(solution)/shard_map/all_to_all | solution.py:238
  21.8 0.0 copy-start.2
  21.8 0.0 copy-start
  21.8 0.0 copy-start.1
  21.8 0.0 collective-permute-start
  21.8 1.7 %collective-permute-start.2 = (bf16[8,16,1024]{2,1,0:T(8,128)(2,1)S(1)}, bf16[8,16,1024]{2,1,0:T(8,128)(2,1)S(1)}, u32[]{:S(2)}, u32[]{:S(2)}) collective-permute-start(bf16[8,16,1024]{2,1,0:T(8,128)(2,1)S(1)} %all-to-all-done.refs_0_), channel_id=1, source_target_pairs={{0,64},{4,196},{64,0},{68,132},{128,192},{132,68},{192,128},{196,4... | collective-permute-start | bytes 786440 | tf_op jit(solution)/shard_map/ppermute | solution.py:241
  23.5 2.2 %collective-permute-start.1 = (bf16[8,16,1024]{2,1,0:T(8,128)(2,1)S(1)}, bf16[8,16,1024]{2,1,0:T(8,128)(2,1)S(1)}, u32[]{:S(2)}, u32[]{:S(2)}) collective-permute-start(bf16[8,16,1024]{2,1,0:T(8,128)(2,1)S(1)} %all-to-all-done.refs_0_), channel_id=1, source_target_pairs={{0,192},{4,68},{64,128},{68,4},{128,64},{132,196},{192,0},{196,132... | collective-permute-start | bytes 786440 | tf_op jit(solution)/shard_map/ppermute | solution.py:242
  25.7 3.6 %collective-permute-done.2.refs_0_ = bf16[8,16,1024]{2,1,0:T(8,128)(2,1)S(1)} collective-permute-done((bf16[8,16,1024]{2,1,0:T(8,128)(2,1)S(1)}, bf16[8,16,1024]{2,1,0:T(8,128)(2,1)S(1)}, u32[]{:S(2)}, u32[]{:S(2)}) %collective-permute-start.2) | collective-permute-done | bytes 262176 | tf_op jit(solution)/shard_map/ppermute | solution.py:241
  29.3 4.3 %collective-permute-start.3 = (bf16[8,16,1024]{2,1,0:T(8,128)(2,1)S(1)}, bf16[8,16,1024]{2,1,0:T(8,128)(2,1)S(1)}, u32[]{:S(2)}, u32[]{:S(2)}) collective-permute-start(bf16[8,16,1024]{2,1,0:T(8,128)(2,1)S(1)} %collective-permute-done.2.refs_0_), channel_id=1, source_target_pairs={{0,192},{4,68},{64,128},{68,4},{128,64},{132,196},{192,0},{196,132... | collective-permute-start | bytes 786440 | tf_op jit(solution)/shard_map/ppermute | solution.py:243
  33.6 2.1 %copy.14 = bf16[1,16,256,2,128]{4,2,1,3,0:T(8,128)(2,1)S(1)} copy(bf16[1,16,256,2,128]{4,3,2,1,0:T(2,128)(2,1)} %param.7) | data formatting | bytes 4194304 | tf_op args[2]
  35.7 0.0 copy-done.2
  35.7 0.0 collective-permute-done.1.refs_0_
  35.7 0.0 collective-permute-done.refs_2_
  35.7 0.0 copy-done
  35.7 0.0 copy-done.1
  35.7 2.3 %shard_map.56 = bf16[8,16,1152]{2,1,0:T(8,128)(2,1)S(1)} custom-call(s32[1,128]{1,0:T(1,128)S(1)} %copy-done.1, bf16[8,16,1024]{2,1,0:T(8,128)(2,1)S(1)} %collective-permute-done.1.refs_0_, bf16[2,2,512,1024]{3,2,1,0:T(8,128)(2,1)S(1)} %bitcast.28, bf16[2,2,512,1024]{3,2,1,0:T(8,128)(2,1)S(1)} %collective-permute-done.refs_2_), custom_call_target="tpu_custom_call" | custom-call | flops 1073741824 | bytes 2097152 | tf_op jit(solution)/shard_map/pallas_call | solution.py:129
  38.0 0.0 copy-start.3
  38.0 0.0 collective-permute-done.3.refs_0_
  38.0 2.3 %shard_map.58 = bf16[8,16,1152]{2,1,0:T(8,128)(2,1)S(1)} custom-call(s32[1,128]{1,0:T(1,128)S(1)} %copy-done.1, bf16[8,16,1024]{2,1,0:T(8,128)(2,1)S(1)} %collective-permute-done.3.refs_0_, bf16[2,2,512,1024]{3,2,1,0:T(8,128)(2,1)S(1)} %bitcast.29, bf16[2,2,512,1024]{3,2,1,0:T(8,128)(2,1)S(1)} %collective-permute-done.refs_2_), custom_call_target="tpu_custom_call" | custom-call | flops 1073741824 | bytes 2097152 | tf_op jit(solution)/shard_map/pallas_call | solution.py:129
  40.3 3.2 %collective-permute-start.5 = (bf16[8,16,1152]{2,1,0:T(8,128)(2,1)S(1)}, bf16[8,16,1152]{2,1,0:T(8,128)(2,1)S(1)}, u32[]{:S(2)}, u32[]{:S(2)}) collective-permute-start(bf16[8,16,1152]{2,1,0:T(8,128)(2,1)S(1)} %shard_map.58), channel_id=1, source_target_pairs={{0,192},{4,68},{64,128},{68,4},{128,64},{132,196},{192,0},{196,132... | collective-permute-start | bytes 884744 | tf_op jit(solution)/shard_map/ppermute | solution.py:252
  43.5 0.0 copy-done.3
  43.5 0.1 iota_compare_fusion
  43.6 0.1 collective-permute-start.4
  43.7 2.2 %shard_map.57.all_refs_0_ = bf16[8,16,1152]{2,1,0:T(8,128)(2,1)S(1)} custom-call(s32[1,128]{1,0:T(1,128)S(1)} %copy-done.1, bf16[8,16,1024]{2,1,0:T(8,128)(2,1)S(1)} %collective-permute-done.2.refs_0_, bf16[2,2,512,1024]{3,2,1,0:T(8,128)(2,1)S(1)} %bitcast.30, bf16[2,2,512,1024]{3,2,1,0:T(8,128)(2,1)S(1)} %collective-permute-done.refs_2_), custom_call_target="tpu_custom_call" | custom-call | flops 1073741824 | bytes 2097152 | tf_op jit(solution)/shard_map/pallas_call | solution.py:129
  45.9 2.4 %collective-permute-done.5.all_refs_1_ = bf16[8,16,1152]{2,1,0:T(8,128)(2,1)S(1)} collective-permute-done((bf16[8,16,1152]{2,1,0:T(8,128)(2,1)S(1)}, bf16[8,16,1152]{2,1,0:T(8,128)(2,1)S(1)}, u32[]{:S(2)}, u32[]{:S(2)}) %collective-permute-start.5) | collective-permute-done | bytes 294944 | tf_op jit(solution)/shard_map/ppermute | solution.py:252
  48.3 0.5 shard_map.59
  48.8 0.3 collective-permute-start.6
  49.1 0.5 fusion.7
  49.5 2.2 %shard_map.55.all_refs_0_ = bf16[8,16,1152]{2,1,0:T(8,128)(2,1)S(1)} custom-call(s32[1,128]{1,0:T(1,128)S(1)} %copy-done.1, bf16[8,16,1024]{2,1,0:T(8,128)(2,1)S(1)} %all-to-all-done.refs_0_, bf16[2,2,512,1024]{3,2,1,0:T(8,128)(2,1)S(1)} %bitcast.31, bf16[2,2,512,1024]{3,2,1,0:T(8,128)(2,1)S(1)} %collective-permute-done.refs_2_), custom_call_target="tpu_custom_call" | custom-call | flops 1073741824 | bytes 2097152 | tf_op jit(solution)/shard_map/pallas_call | solution.py:129
  51.8 2.7 %collective-permute-done.4.all_refs_1_ = bf16[8,16,1152]{2,1,0:T(8,128)(2,1)S(1)} collective-permute-done((bf16[8,16,1152]{2,1,0:T(8,128)(2,1)S(1)}, bf16[8,16,1152]{2,1,0:T(8,128)(2,1)S(1)}, u32[]{:S(2)}, u32[]{:S(2)}) %collective-permute-start.4) | collective-permute-done | bytes 294944 | tf_op jit(solution)/shard_map/ppermute | solution.py:251
  54.5 1.3 %collective-permute-done.6.all_refs_2_ = bf16[8,16,1152]{2,1,0:T(8,128)(2,1)S(1)} collective-permute-done((bf16[8,16,1152]{2,1,0:T(8,128)(2,1)S(1)}, bf16[8,16,1152]{2,1,0:T(8,128)(2,1)S(1)}, u32[]{:S(2)}, u32[]{:S(2)}) %collective-permute-start.6) | collective-permute-done | bytes 294944 | tf_op jit(solution)/shard_map/ppermute | solution.py:254
  55.8 1.4 %shard_map.60 = bf16[8,16,1152]{2,1,0:T(8,128)(2,1)} custom-call(bf16[8,16,1152]{2,1,0:T(8,128)(2,1)S(1)} %shard_map.55.all_refs_0_, bf16[8,16,1152]{2,1,0:T(8,128)(2,1)S(1)} %collective-permute-done.4.all_refs_1_, bf16[8,16,1152]{2,1,0:T(8,128)(2,1)S(1)} %collective-permute-done.6.all_refs_2_), custom_call_target="tpu_custom_call" | custom-call | tf_op jit(solution)/shard_map/pallas_call | solution.py:179
  57.2 3.4 %all-to-all-start.1 = ((bf16[8,16,1152]{2,1,0:T(8,128)(2,1)}), bf16[8,16,1152]{2,1,0:T(8,128)(2,1)S(1)}, u32[]{:S(2)}, u32[]{:S(2)}) async-start(bf16[8,16,1152]{2,1,0:T(8,128)(2,1)} %shard_map.60), calls=%async_computation.1 | async-start | bytes 589824 | tf_op jit(solution)/shard_map/all_to_all | solution.py:256
  60.6 0.2 fusion.1
  60.8 0.3 convolution_divide_fusion
  61.2 11.2 %all-to-all-done.1.p_ref = bf16[8,16,1152]{2,1,0:T(8,128)(2,1)S(1)} async-done(((bf16[8,16,1152]{2,1,0:T(8,128)(2,1)}), bf16[8,16,1152]{2,1,0:T(8,128)(2,1)S(1)}, u32[]{:S(2)}, u32[]{:S(2)}) %all-to-all-start.1) | async-done | bytes 294944 | tf_op jit(solution)/shard_map/all_to_all | solution.py:256
  72.3 1.0 %shard_map.61 = bf16[16,1024]{1,0:T(8,128)(2,1)} custom-call(bf16[8,16,1152]{2,1,0:T(8,128)(2,1)S(1)} %all-to-all-done.1.p_ref, f32[16,1024]{1,0:T(8,128)S(1)} %bitcast.32, f32[16,128]{1,0:T(8,128)S(1)} %pad.4.sl_ref), custom_call_target="tpu_custom_call" | custom-call | tf_op jit(solution)/shard_map/pallas_call | solution.py:201
  (4 shorter events, 0.1 us)
Async XLA Ops:
  1.5 20.3 %all-to-all-start = ((bf16[8,16,1024]{2,1,0:T(8,128)(2,1)}), bf16[8,16,1024]{2,1,0:T(8,128)(2,1)S(1)}, u32[]{:S(2)}, u32[]{:S(2)}) async-start(bf16[8,16,1024]{2,1,0:T(8,128)(2,1)} %broadcast_in_dim.26), calls=%async_computation | async-start | bytes 524288 | tf_op jit(solution)/shard_map/all_to_all | solution.py:238
  21.8 13.8 %copy-start.2 = (bf16[1,16,1024]{2,1,0:T(8,128)(2,1)S(1)}, bf16[1,16,1024]{2,1,0:T(8,128)(2,1)}, u32[]{:S(2)}) copy-start(bf16[1,16,1024]{2,1,0:T(8,128)(2,1)} %param.5) | copy-start | bytes 98308
  21.8 13.9 %copy-start = (bf16[1,2,512,2,1024]{4,2,3,1,0:T(8,128)(2,1)S(1)}, bf16[1,2,512,2,1024]{4,2,3,1,0:T(8,128)(2,1)}, u32[]{:S(2)}) copy-start(bf16[1,2,512,2,1024]{4,2,3,1,0:T(8,128)(2,1)} %copy.13) | copy-start | bytes 12582916
  21.8 13.9 %copy-start.1 = (s32[1,128]{1,0:T(1,128)S(1)}, s32[1,128]{1,0:T(1,128)}, u32[]{:S(2)}) copy-start(s32[1,128]{1,0:T(1,128)} %ids_ref.7) | copy-start | bytes 1540
  21.8 13.9 %collective-permute-start = (bf16[2,2,512,1024]{3,2,1,0:T(8,128)(2,1)}, bf16[2,2,512,1024]{3,2,1,0:T(8,128)(2,1)S(1)}, u32[]{:S(2)}, u32[]{:S(2)}) collective-permute-start(bf16[2,2,512,1024]{3,2,1,0:T(8,128)(2,1)} %bitcast.27), channel_id=1, source_target_pairs={{0,4},{4,0},{1,5},{5,1},{2,6},{6,2},{3,7},{7,3},{8,12},{12,8},{9,1... | collective-permute-start | bytes 12582920 | tf_op jit(solution)/shard_map/ppermute | solution.py:240
  21.8 7.5 %collective-permute-start.2 = (bf16[8,16,1024]{2,1,0:T(8,128)(2,1)S(1)}, bf16[8,16,1024]{2,1,0:T(8,128)(2,1)S(1)}, u32[]{:S(2)}, u32[]{:S(2)}) collective-permute-start(bf16[8,16,1024]{2,1,0:T(8,128)(2,1)S(1)} %all-to-all-done.refs_0_), channel_id=1, source_target_pairs={{0,64},{4,196},{64,0},{68,132},{128,192},{132,68},{192,128},{196,4... | collective-permute-start | bytes 786440 | tf_op jit(solution)/shard_map/ppermute | solution.py:241
  23.5 12.2 %collective-permute-start.1 = (bf16[8,16,1024]{2,1,0:T(8,128)(2,1)S(1)}, bf16[8,16,1024]{2,1,0:T(8,128)(2,1)S(1)}, u32[]{:S(2)}, u32[]{:S(2)}) collective-permute-start(bf16[8,16,1024]{2,1,0:T(8,128)(2,1)S(1)} %all-to-all-done.refs_0_), channel_id=1, source_target_pairs={{0,192},{4,68},{64,128},{68,4},{128,64},{132,196},{192,0},{196,132... | collective-permute-start | bytes 786440 | tf_op jit(solution)/shard_map/ppermute | solution.py:242
  29.3 8.7 %collective-permute-start.3 = (bf16[8,16,1024]{2,1,0:T(8,128)(2,1)S(1)}, bf16[8,16,1024]{2,1,0:T(8,128)(2,1)S(1)}, u32[]{:S(2)}, u32[]{:S(2)}) collective-permute-start(bf16[8,16,1024]{2,1,0:T(8,128)(2,1)S(1)} %collective-permute-done.2.refs_0_), channel_id=1, source_target_pairs={{0,192},{4,68},{64,128},{68,4},{128,64},{132,196},{192,0},{196,132... | collective-permute-start | bytes 786440 | tf_op jit(solution)/shard_map/ppermute | solution.py:243
  38.0 5.5 %copy-start.3 = (s32[1,16]{1,0:T(1,128)S(1)}, s32[1,16]{1,0:T(1,128)}, u32[]{:S(2)}) copy-start(s32[1,16]{1,0:T(1,128)} %param.8) | copy-start | bytes 196
  40.3 8.0 %collective-permute-start.5 = (bf16[8,16,1152]{2,1,0:T(8,128)(2,1)S(1)}, bf16[8,16,1152]{2,1,0:T(8,128)(2,1)S(1)}, u32[]{:S(2)}, u32[]{:S(2)}) collective-permute-start(bf16[8,16,1152]{2,1,0:T(8,128)(2,1)S(1)} %shard_map.58), channel_id=1, source_target_pairs={{0,192},{4,68},{64,128},{68,4},{128,64},{132,196},{192,0},{196,132... | collective-permute-start | bytes 884744 | tf_op jit(solution)/shard_map/ppermute | solution.py:252
  43.6 10.9 %collective-permute-start.4 = (bf16[8,16,1152]{2,1,0:T(8,128)(2,1)S(1)}, bf16[8,16,1152]{2,1,0:T(8,128)(2,1)S(1)}, u32[]{:S(2)}, u32[]{:S(2)}) collective-permute-start(bf16[8,16,1152]{2,1,0:T(8,128)(2,1)S(1)} %shard_map.56), channel_id=1, source_target_pairs={{0,192},{4,68},{64,128},{68,4},{128,64},{132,196},{192,0},{196,132... | collective-permute-start | bytes 884744 | tf_op jit(solution)/shard_map/ppermute | solution.py:251
  48.8 7.0 %collective-permute-start.6 = (bf16[8,16,1152]{2,1,0:T(8,128)(2,1)S(1)}, bf16[8,16,1152]{2,1,0:T(8,128)(2,1)S(1)}, u32[]{:S(2)}, u32[]{:S(2)}) collective-permute-start(bf16[8,16,1152]{2,1,0:T(8,128)(2,1)S(1)} %shard_map.59), channel_id=1, source_target_pairs={{0,64},{4,196},{64,0},{68,132},{128,192},{132,68},{192,128},{196,4... | collective-permute-start | bytes 884744 | tf_op jit(solution)/shard_map/ppermute | solution.py:254
  57.2 15.1 %all-to-all-start.1 = ((bf16[8,16,1152]{2,1,0:T(8,128)(2,1)}), bf16[8,16,1152]{2,1,0:T(8,128)(2,1)S(1)}, u32[]{:S(2)}, u32[]{:S(2)}) async-start(bf16[8,16,1152]{2,1,0:T(8,128)(2,1)} %shard_map.60), calls=%async_computation.1 | async-start | bytes 589824 | tf_op jit(solution)/shard_map/all_to_all | solution.py:256

commit v4 on v3

--- a/solution.py
+++ b/solution.py
@@ -242,8 +242,6 @@
     second = lax.ppermute(q0, ("y", "core"), _pairs(2))
     third = lax.ppermute(first, ("y", "core"), _pairs(2))
 
-    suffix_o, suffix_l2 = _suffix(q, suffix_kv[0], suffix_len[0])
-
     def part(which, block):
         return _prompt((which,), group_of, [block], own, par)[0]
 
@@ -253,6 +251,10 @@
     merged = _merge([part(1, first), back_third])
     back_first = lax.ppermute(merged, ("y", "core"), _pairs(1))
     merged = _merge([part(0, q0), back_second, back_first])
+    merged, q, suffix_kv, suffix_len = lax.optimization_barrier(
+        (merged, q, suffix_kv, suffix_len)
+    )
+    suffix_o, suffix_l2 = _suffix(q, suffix_kv[0], suffix_len[0])
     got = lax.all_to_all(merged, ("zh", "zl"), 0, 0, tiled=True)
     return _final(got, suffix_o, suffix_l2)[None]
 

time: 73.8 us -> 73.7 us (level)
    all_to_all x1, waiting for transfers between devices: 11.2 us -> 10 us  [_shards(): got = lax.all_to_all(merged, ('zh', 'zl'), 0, 0, tiled=True)]
    unnamed x12 -> x13, local copies, waits for them, and re-layouts: 7.58 us -> 7.71 us
  transfers between devices with their start and end apart: 9 -> 9, of which waited for: 6 -> 6; matrix products, arithmetic and copies ran while one was open for 12% -> 9% of each run, Pallas kernels for 10% -> 10%
where the time goes in v4:
time: 73.7 us; the launch traced here: 73.2 us
  waiting for transfers between devices  26.9 us (36%)
  starting transfers between devices  23.7 us (32%)
  Pallas kernels  11.8 us (16%)
  local copies, waits for them, and re-layouts  9.68 us (13%)
  matrix products  0.76 us (1%)
    all_to_all x1, waiting for transfers between devices, _shards(): got = lax.all_to_all(merged, ('zh', 'zl'), 0, 0, tiled=True)  10 us
    pallas_call x4, Pallas kernels, _prompt(): pl.pallas_call(functools.partial(_prompt_kernel, wanted), out_shape=[jax....  8.97 us
    all_to_all x1, starting transfers between devices, _shards(): q0 = lax.all_to_all(spread, ('zh', 'zl'), 0, 0, tiled=True)  8.47 us
    unnamed x13, local copies, waits for them, and re-layouts  7.71 us
    all_to_all x1, waiting for transfers between devices, _shards(): q0 = lax.all_to_all(spread, ('zh', 'zl'), 0, 0, tiled=True)  6.4 us
    ppermute x1, starting transfers between devices, _shards(): third = lax.ppermute(first, ('y', 'core'), _pairs(2))  4.44 us
    ppermute x1, waiting for transfers between devices, _shards(): first = lax.ppermute(q0, ('y', 'core'), _pairs(1))  3.54 us
    all_to_all x1, starting transfers between devices, _shards(): got = lax.all_to_all(merged, ('zh', 'zl'), 0, 0, tiled=True)  3.42 us
  transfers between devices with their start and end apart: 9, of which 6 were waited for; matrix products, arithmetic and copies ran while one was open for 9% of the time, Pallas kernels for 10%

profile of v4, /device:TPU:2, one launch (start us, length us, event | category | flops | bytes accessed | tf_op | source)
XLA Modules:
  0.0 73.2 jit_solution(6886561793099196350)
XLA Ops:
  0.0 1.5 %broadcast_in_dim.26 = bf16[8,16,1024]{2,1,0:T(8,128)(2,1)} broadcast(bf16[16,1024]{1,0:T(8,128)(2,1)} %bitcast.34), dimensions={1,2} | broadcast | bytes 294912 | tf_op jit(solution)/shard_map/broadcast_in_dim | solution.py:237
  1.5 8.5 %all-to-all-start = ((bf16[8,16,1024]{2,1,0:T(8,128)(2,1)}), bf16[8,16,1024]{2,1,0:T(8,128)(2,1)S(1)}, u32[]{:S(2)}, u32[]{:S(2)}) async-start(bf16[8,16,1024]{2,1,0:T(8,128)(2,1)} %broadcast_in_dim.26), calls=%async_computation | async-start | bytes 524288 | tf_op jit(solution)/shard_map/all_to_all | solution.py:238
  10.0 0.0 copy-start.1
  10.0 5.5 %copy.13 = bf16[1,2,512,2,1024]{4,2,3,1,0:T(8,128)(2,1)} copy(bf16[1,2,512,2,1024]{4,3,2,1,0:T(2,128)(2,1)} %param.6) | data formatting | bytes 8388608 | tf_op args[1]
  15.4 6.4 %all-to-all-done.refs_0_ = bf16[8,16,1024]{2,1,0:T(8,128)(2,1)S(1)} async-done(((bf16[8,16,1024]{2,1,0:T(8,128)(2,1)}), bf16[8,16,1024]{2,1,0:T(8,128)(2,1)S(1)}, u32[]{:S(2)}, u32[]{:S(2)}) %all-to-all-start) | async-done | bytes 262176 | tf_op jit(solution)/shard_map/all_to_all | solution.py:238
  21.8 0.0 collective-permute-start
  21.8 1.6 %collective-permute-start.2 = (bf16[8,16,1024]{2,1,0:T(8,128)(2,1)S(1)}, bf16[8,16,1024]{2,1,0:T(8,128)(2,1)S(1)}, u32[]{:S(2)}, u32[]{:S(2)}) collective-permute-start(bf16[8,16,1024]{2,1,0:T(8,128)(2,1)S(1)} %all-to-all-done.refs_0_), channel_id=1, source_target_pairs={{0,64},{4,196},{64,0},{68,132},{128,192},{132,68},{192,128},{196,4... | collective-permute-start | bytes 786440 | tf_op jit(solution)/shard_map/ppermute | solution.py:241
  23.4 2.2 %collective-permute-start.1 = (bf16[8,16,1024]{2,1,0:T(8,128)(2,1)S(1)}, bf16[8,16,1024]{2,1,0:T(8,128)(2,1)S(1)}, u32[]{:S(2)}, u32[]{:S(2)}) collective-permute-start(bf16[8,16,1024]{2,1,0:T(8,128)(2,1)S(1)} %all-to-all-done.refs_0_), channel_id=1, source_target_pairs={{0,192},{4,68},{64,128},{68,4},{128,64},{132,196},{192,0},{196,132... | collective-permute-start | bytes 786440 | tf_op jit(solution)/shard_map/ppermute | solution.py:242
  25.6 3.5 %collective-permute-done.2.refs_0_ = bf16[8,16,1024]{2,1,0:T(8,128)(2,1)S(1)} collective-permute-done((bf16[8,16,1024]{2,1,0:T(8,128)(2,1)S(1)}, bf16[8,16,1024]{2,1,0:T(8,128)(2,1)S(1)}, u32[]{:S(2)}, u32[]{:S(2)}) %collective-permute-start.2) | collective-permute-done | bytes 262176 | tf_op jit(solution)/shard_map/ppermute | solution.py:241
  29.1 4.4 %collective-permute-start.3 = (bf16[8,16,1024]{2,1,0:T(8,128)(2,1)S(1)}, bf16[8,16,1024]{2,1,0:T(8,128)(2,1)S(1)}, u32[]{:S(2)}, u32[]{:S(2)}) collective-permute-start(bf16[8,16,1024]{2,1,0:T(8,128)(2,1)S(1)} %collective-permute-done.2.refs_0_), channel_id=1, source_target_pairs={{0,192},{4,68},{64,128},{68,4},{128,64},{132,196},{192,0},{196,132... | collective-permute-start | bytes 786440 | tf_op jit(solution)/shard_map/ppermute | solution.py:243
  33.6 0.0 collective-permute-done.1.refs_0_
  33.6 0.0 collective-permute-done.refs_2_
  33.6 0.0 copy-done.1
  33.6 0.0 copy-start
  33.6 2.2 %copy-done = bf16[1,2,512,2,1024]{4,2,3,1,0:T(8,128)(2,1)S(1)} copy-done((bf16[1,2,512,2,1024]{4,2,3,1,0:T(8,128)(2,1)S(1)}, bf16[1,2,512,2,1024]{4,2,3,1,0:T(8,128)(2,1)}, u32[]{:S(2)}) %copy-start) | copy-done | bytes 4194328
  35.8 2.2 %shard_map.56 = bf16[8,16,1152]{2,1,0:T(8,128)(2,1)S(1)} custom-call(s32[1,128]{1,0:T(1,128)S(1)} %copy-done.1, bf16[8,16,1024]{2,1,0:T(8,128)(2,1)S(1)} %collective-permute-done.1.refs_0_, bf16[2,2,512,1024]{3,2,1,0:T(8,128)(2,1)S(1)} %bitcast.27, bf16[2,2,512,1024]{3,2,1,0:T(8,128)(2,1)S(1)} %collective-permute-done.refs_2_), custom_call_target="tpu_custom_call" | custom-call | flops 1073741824 | bytes 2097152 | tf_op jit(solution)/shard_map/pallas_call | solution.py:129
  38.0 0.0 collective-permute-done.3.refs_0_
  38.0 2.3 %shard_map.58 = bf16[8,16,1152]{2,1,0:T(8,128)(2,1)S(1)} custom-call(s32[1,128]{1,0:T(1,128)S(1)} %copy-done.1, bf16[8,16,1024]{2,1,0:T(8,128)(2,1)S(1)} %collective-permute-done.3.refs_0_, bf16[2,2,512,1024]{3,2,1,0:T(8,128)(2,1)S(1)} %bitcast.28, bf16[2,2,512,1024]{3,2,1,0:T(8,128)(2,1)S(1)} %collective-permute-done.refs_2_), custom_call_target="tpu_custom_call" | custom-call | flops 1073741824 | bytes 2097152 | tf_op jit(solution)/shard_map/pallas_call | solution.py:129
  40.3 3.2 %collective-permute-start.5 = (bf16[8,16,1152]{2,1,0:T(8,128)(2,1)S(1)}, bf16[8,16,1152]{2,1,0:T(8,128)(2,1)S(1)}, u32[]{:S(2)}, u32[]{:S(2)}) collective-permute-start(bf16[8,16,1152]{2,1,0:T(8,128)(2,1)S(1)} %shard_map.58), channel_id=1, source_target_pairs={{0,192},{4,68},{64,128},{68,4},{128,64},{132,196},{192,0},{196,132... | collective-permute-start | bytes 884744 | tf_op jit(solution)/shard_map/ppermute | solution.py:250
  43.5 0.1 collective-permute-start.4
  43.6 2.2 %shard_map.57.all_refs_0_ = bf16[8,16,1152]{2,1,0:T(8,128)(2,1)S(1)} custom-call(s32[1,128]{1,0:T(1,128)S(1)} %copy-done.1, bf16[8,16,1024]{2,1,0:T(8,128)(2,1)S(1)} %collective-permute-done.2.refs_0_, bf16[2,2,512,1024]{3,2,1,0:T(8,128)(2,1)S(1)} %bitcast.29, bf16[2,2,512,1024]{3,2,1,0:T(8,128)(2,1)S(1)} %collective-permute-done.refs_2_), custom_call_target="tpu_custom_call" | custom-call | flops 1073741824 | bytes 2097152 | tf_op jit(solution)/shard_map/pallas_call | solution.py:129
  45.8 2.5 %collective-permute-done.5.all_refs_1_ = bf16[8,16,1152]{2,1,0:T(8,128)(2,1)S(1)} collective-permute-done((bf16[8,16,1152]{2,1,0:T(8,128)(2,1)S(1)}, bf16[8,16,1152]{2,1,0:T(8,128)(2,1)S(1)}, u32[]{:S(2)}, u32[]{:S(2)}) %collective-permute-start.5) | collective-permute-done | bytes 294944 | tf_op jit(solution)/shard_map/ppermute | solution.py:250
  48.3 0.5 shard_map.59
  48.8 0.0 copy-start.4
  48.8 0.0 copy-start.3
  48.8 0.3 collective-permute-start.6
  49.1 0.0 copy-start.2
  49.1 2.3 %shard_map.55.all_refs_0_ = bf16[8,16,1152]{2,1,0:T(8,128)(2,1)S(1)} custom-call(s32[1,128]{1,0:T(1,128)S(1)} %copy-done.1, bf16[8,16,1024]{2,1,0:T(8,128)(2,1)S(1)} %all-to-all-done.refs_0_, bf16[2,2,512,1024]{3,2,1,0:T(8,128)(2,1)S(1)} %bitcast.30, bf16[2,2,512,1024]{3,2,1,0:T(8,128)(2,1)S(1)} %collective-permute-done.refs_2_), custom_call_target="tpu_custom_call" | custom-call | flops 1073741824 | bytes 2097152 | tf_op jit(solution)/shard_map/pallas_call | solution.py:129
  51.4 2.8 %collective-permute-done.4.all_refs_1_ = bf16[8,16,1152]{2,1,0:T(8,128)(2,1)S(1)} collective-permute-done((bf16[8,16,1152]{2,1,0:T(8,128)(2,1)S(1)}, bf16[8,16,1152]{2,1,0:T(8,128)(2,1)S(1)}, u32[]{:S(2)}, u32[]{:S(2)}) %collective-permute-start.4) | collective-permute-done | bytes 294944 | tf_op jit(solution)/shard_map/ppermute | solution.py:249
  54.1 1.7 %collective-permute-done.6.all_refs_2_ = bf16[8,16,1152]{2,1,0:T(8,128)(2,1)S(1)} collective-permute-done((bf16[8,16,1152]{2,1,0:T(8,128)(2,1)S(1)}, bf16[8,16,1152]{2,1,0:T(8,128)(2,1)S(1)}, u32[]{:S(2)}, u32[]{:S(2)}) %collective-permute-start.6) | collective-permute-done | bytes 294944 | tf_op jit(solution)/shard_map/ppermute | solution.py:252
  55.8 1.4 %shard_map.60 = bf16[8,16,1152]{2,1,0:T(8,128)(2,1)} custom-call(bf16[8,16,1152]{2,1,0:T(8,128)(2,1)S(1)} %shard_map.55.all_refs_0_, bf16[8,16,1152]{2,1,0:T(8,128)(2,1)S(1)} %collective-permute-done.4.all_refs_1_, bf16[8,16,1152]{2,1,0:T(8,128)(2,1)S(1)} %collective-permute-done.6.all_refs_2_), custom_call_target="tpu_custom_call" | custom-call | tf_op jit(solution)/shard_map/pallas_call | solution.py:179
  57.2 0.0 copy-done.4
  57.2 0.1 iota_compare_fusion
  57.3 3.4 %all-to-all-start.1 = ((bf16[8,16,1152]{2,1,0:T(8,128)(2,1)}), bf16[8,16,1152]{2,1,0:T(8,128)(2,1)S(1)}, u32[]{:S(2)}, u32[]{:S(2)}) async-start(bf16[8,16,1152]{2,1,0:T(8,128)(2,1)} %shard_map.60), calls=%async_computation.1 | async-start | bytes 589824 | tf_op jit(solution)/shard_map/all_to_all | solution.py:258
  60.7 0.0 copy-done.3
  60.7 0.0 copy-done.2
  60.7 0.5 copy.14
  61.2 0.5 fusion.7
  61.7 0.2 fusion.1
  61.9 0.3 convolution_divide_fusion
  62.2 10.0 %all-to-all-done.1.p_ref = bf16[8,16,1152]{2,1,0:T(8,128)(2,1)S(1)} async-done(((bf16[8,16,1152]{2,1,0:T(8,128)(2,1)}), bf16[8,16,1152]{2,1,0:T(8,128)(2,1)S(1)}, u32[]{:S(2)}, u32[]{:S(2)}) %all-to-all-start.1) | async-done | bytes 294944 | tf_op jit(solution)/shard_map/all_to_all | solution.py:258
  72.3 1.0 %shard_map.61 = bf16[16,1024]{1,0:T(8,128)(2,1)} custom-call(bf16[8,16,1152]{2,1,0:T(8,128)(2,1)S(1)} %all-to-all-done.1.p_ref, f32[16,1024]{1,0:T(8,128)S(1)} %bitcast.31, f32[16,128]{1,0:T(8,128)S(1)} %pad.4.sl_ref), custom_call_target="tpu_custom_call" | custom-call | tf_op jit(solution)/shard_map/pallas_call | solution.py:201
  (4 shorter events, 0.1 us)
Async XLA Ops:
  1.5 20.3 %all-to-all-start = ((bf16[8,16,1024]{2,1,0:T(8,128)(2,1)}), bf16[8,16,1024]{2,1,0:T(8,128)(2,1)S(1)}, u32[]{:S(2)}, u32[]{:S(2)}) async-start(bf16[8,16,1024]{2,1,0:T(8,128)(2,1)} %broadcast_in_dim.26), calls=%async_computation | async-start | bytes 524288 | tf_op jit(solution)/shard_map/all_to_all | solution.py:238
  10.0 23.6 %copy-start.1 = (s32[1,128]{1,0:T(1,128)S(1)}, s32[1,128]{1,0:T(1,128)}, u32[]{:S(2)}) copy-start(s32[1,128]{1,0:T(1,128)} %ids_ref.7) | copy-start | bytes 1540
  21.8 11.7 %collective-permute-start = (bf16[2,2,512,1024]{3,2,1,0:T(8,128)(2,1)}, bf16[2,2,512,1024]{3,2,1,0:T(8,128)(2,1)S(1)}, u32[]{:S(2)}, u32[]{:S(2)}) collective-permute-start(bf16[2,2,512,1024]{3,2,1,0:T(8,128)(2,1)} %bitcast.26), channel_id=1, source_target_pairs={{0,4},{4,0},{1,5},{5,1},{2,6},{6,2},{3,7},{7,3},{8,12},{12,8},{9,1... | collective-permute-start | bytes 12582920 | tf_op jit(solution)/shard_map/ppermute | solution.py:240
  21.8 7.3 %collective-permute-start.2 = (bf16[8,16,1024]{2,1,0:T(8,128)(2,1)S(1)}, bf16[8,16,1024]{2,1,0:T(8,128)(2,1)S(1)}, u32[]{:S(2)}, u32[]{:S(2)}) collective-permute-start(bf16[8,16,1024]{2,1,0:T(8,128)(2,1)S(1)} %all-to-all-done.refs_0_), channel_id=1, source_target_pairs={{0,64},{4,196},{64,0},{68,132},{128,192},{132,68},{192,128},{196,4... | collective-permute-start | bytes 786440 | tf_op jit(solution)/shard_map/ppermute | solution.py:241
  23.4 10.2 %collective-permute-start.1 = (bf16[8,16,1024]{2,1,0:T(8,128)(2,1)S(1)}, bf16[8,16,1024]{2,1,0:T(8,128)(2,1)S(1)}, u32[]{:S(2)}, u32[]{:S(2)}) collective-permute-start(bf16[8,16,1024]{2,1,0:T(8,128)(2,1)S(1)} %all-to-all-done.refs_0_), channel_id=1, source_target_pairs={{0,192},{4,68},{64,128},{68,4},{128,64},{132,196},{192,0},{196,132... | collective-permute-start | bytes 786440 | tf_op jit(solution)/shard_map/ppermute | solution.py:242
  29.1 8.9 %collective-permute-start.3 = (bf16[8,16,1024]{2,1,0:T(8,128)(2,1)S(1)}, bf16[8,16,1024]{2,1,0:T(8,128)(2,1)S(1)}, u32[]{:S(2)}, u32[]{:S(2)}) collective-permute-start(bf16[8,16,1024]{2,1,0:T(8,128)(2,1)S(1)} %collective-permute-done.2.refs_0_), channel_id=1, source_target_pairs={{0,192},{4,68},{64,128},{68,4},{128,64},{132,196},{192,0},{196,132... | collective-permute-start | bytes 786440 | tf_op jit(solution)/shard_map/ppermute | solution.py:243
  33.6 2.2 %copy-start = (bf16[1,2,512,2,1024]{4,2,3,1,0:T(8,128)(2,1)S(1)}, bf16[1,2,512,2,1024]{4,2,3,1,0:T(8,128)(2,1)}, u32[]{:S(2)}) copy-start(bf16[1,2,512,2,1024]{4,2,3,1,0:T(8,128)(2,1)} %copy.13) | copy-start | bytes 12582916
  40.3 8.0 %collective-permute-start.5 = (bf16[8,16,1152]{2,1,0:T(8,128)(2,1)S(1)}, bf16[8,16,1152]{2,1,0:T(8,128)(2,1)S(1)}, u32[]{:S(2)}, u32[]{:S(2)}) collective-permute-start(bf16[8,16,1152]{2,1,0:T(8,128)(2,1)S(1)} %shard_map.58), channel_id=1, source_target_pairs={{0,192},{4,68},{64,128},{68,4},{128,64},{132,196},{192,0},{196,132... | collective-permute-start | bytes 884744 | tf_op jit(solution)/shard_map/ppermute | solution.py:250
  43.5 10.7 %collective-permute-start.4 = (bf16[8,16,1152]{2,1,0:T(8,128)(2,1)S(1)}, bf16[8,16,1152]{2,1,0:T(8,128)(2,1)S(1)}, u32[]{:S(2)}, u32[]{:S(2)}) collective-permute-start(bf16[8,16,1152]{2,1,0:T(8,128)(2,1)S(1)} %shard_map.56), channel_id=1, source_target_pairs={{0,192},{4,68},{64,128},{68,4},{128,64},{132,196},{192,0},{196,132... | collective-permute-start | bytes 884744 | tf_op jit(solution)/shard_map/ppermute | solution.py:249
  48.8 8.4 %copy-start.4 = (s32[1,16]{1,0:T(1,128)S(1)}, s32[1,16]{1,0:T(1,128)}, u32[]{:S(2)}) copy-start(s32[1,16]{1,0:T(1,128)} %param.8) | copy-start | bytes 196
  48.8 11.9 %copy-start.3 = (bf16[1,16,1024]{2,1,0:T(8,128)(2,1)S(1)}, bf16[1,16,1024]{2,1,0:T(8,128)(2,1)}, u32[]{:S(2)}) copy-start(bf16[1,16,1024]{2,1,0:T(8,128)(2,1)} %param.5) | copy-start | bytes 98308
  48.8 7.0 %collective-permute-start.6 = (bf16[8,16,1152]{2,1,0:T(8,128)(2,1)S(1)}, bf16[8,16,1152]{2,1,0:T(8,128)(2,1)S(1)}, u32[]{:S(2)}, u32[]{:S(2)}) collective-permute-start(bf16[8,16,1152]{2,1,0:T(8,128)(2,1)S(1)} %shard_map.59), channel_id=1, source_target_pairs={{0,64},{4,196},{64,0},{68,132},{128,192},{132,68},{192,128},{196,4... | collective-permute-start | bytes 884744 | tf_op jit(solution)/shard_map/ppermute | solution.py:252
  49.1 11.6 %copy-start.2 = (bf16[1,16,256,2,128]{4,3,2,1,0:T(2,128)(2,1)S(1)}, bf16[1,16,256,2,128]{4,3,2,1,0:T(2,128)(2,1)}, u32[]{:S(2)}) copy-start(bf16[1,16,256,2,128]{4,3,2,1,0:T(2,128)(2,1)} %param.7) | copy-start | bytes 6291460
  57.3 15.0 %all-to-all-start.1 = ((bf16[8,16,1152]{2,1,0:T(8,128)(2,1)}), bf16[8,16,1152]{2,1,0:T(8,128)(2,1)S(1)}, u32[]{:S(2)}, u32[]{:S(2)}) async-start(bf16[8,16,1152]{2,1,0:T(8,128)(2,1)} %shard_map.60), calls=%async_computation.1 | async-start | bytes 589824 | tf_op jit(solution)/shard_map/all_to_all | solution.py:258

commit v5 on v4

--- a/solution.py
+++ b/solution.py
@@ -125,11 +125,12 @@
     span = own.shape[2]
     rows = zs // 2 * row_dev
     vmem = pl.BlockSpec(memory_space=pltpu.VMEM)
-    hbm = pl.BlockSpec(memory_space=pl.ANY)
+    hbm = pl.BlockSpec(memory_space=pltpu.HBM)
+    anywhere = pl.BlockSpec(memory_space=pl.ANY)
     return pl.pallas_call(
         functools.partial(_prompt_kernel, wanted),
         out_shape=[jax.ShapeDtypeStruct((zs, row_dev, width + HD), BF16)] * n,
-        in_specs=[vmem] * (n + 1) + [hbm, hbm],
+        in_specs=[vmem] * (n + 1) + [hbm, anywhere],
         out_specs=[vmem] * n,
         scratch_shapes=[
             pltpu.VMEM((n, 2, 2, 2 * span, 2 * HD), BF16),
@@ -239,16 +240,17 @@
     q0, own = lax.optimization_barrier((q0, own))
     par = lax.ppermute(own, "core", [(0, 1), (1, 0)])
     first = lax.ppermute(q0, ("y", "core"), _pairs(1))
+    first, q0 = lax.optimization_barrier((first, q0))
+    third = lax.ppermute(first, ("y", "core"), _pairs(2))
     second = lax.ppermute(q0, ("y", "core"), _pairs(2))
-    third = lax.ppermute(first, ("y", "core"), _pairs(2))
 
     def part(which, block):
         return _prompt((which,), group_of, [block], own, par)[0]
 
-    part_second, third = lax.optimization_barrier((part(2, second), third))
+    back_third = lax.ppermute(part(3, third), ("y", "core"), _pairs(2))
+    part_second, part_first = lax.optimization_barrier((part(2, second), part(1, first)))
     back_second = lax.ppermute(part_second, ("y", "core"), _pairs(2))
-    back_third = lax.ppermute(part(3, third), ("y", "core"), _pairs(2))
-    merged = _merge([part(1, first), back_third])
+    merged = _merge([part_first, back_third])
     back_first = lax.ppermute(merged, ("y", "core"), _pairs(1))
     merged = _merge([part(0, q0), back_second, back_first])
     merged, q, suffix_kv, suffix_len = lax.optimization_barrier(

time: 73.7 us -> 74.8 us (1.015)
  waiting for transfers between devices: 26.9 us -> 30.6 us
  starting transfers between devices: 23.7 us -> 20.4 us
    ppermute x1, waiting for transfers between devices: 0.01 us -> 4.35 us  [_shards(): third = lax.ppermute(first, ('y', 'core'), _pairs(2))]
    ppermute x1, waiting for transfers between devices: 2.46 us -> 0.1 us  [_shards(): back_third = lax.ppermute(part(3, third), ('y', 'core'), _pairs(2))]
    ppermute x1, starting transfers between devices: 2.18 us -> 0.22 us  [_shards(): second = lax.ppermute(q0, ('y', 'core'), _pairs(2))]
    ppermute x1, waiting for transfers between devices: 2.75 us -> 4.54 us  [_shards(): back_second = lax.ppermute(part_second, ('y', 'core'), _pairs(2))]
    ppermute x1, waiting for transfers between devices: 1.69 us -> 0.01 us  [_shards(): back_first = lax.ppermute(merged, ('y', 'core'), _pairs(1))]
    ppermute x1, starting transfers between devices: 4.44 us -> 3.01 us  [_shards(): third = lax.ppermute(first, ('y', 'core'), _pairs(2))]
    ppermute x1, waiting for transfers between devices: 3.54 us -> 4.8 us  [_shards(): first = lax.ppermute(q0, ('y', 'core'), _pairs(1))]
  transfers between devices with their start and end apart: 9 -> 9, of which waited for: 6 -> 6; matrix products, arithmetic and copies ran while one was open for 9% -> 9% of each run, Pallas kernels for 10% -> 13%
where the time goes in v5:
time: 74.8 us; the launch traced here: 73.7 us
  waiting for transfers between devices  30.6 us (41%)
  starting transfers between devices  20.4 us (27%)
  Pallas kernels  11.8 us (16%)
  local copies, waits for them, and re-layouts  9.69 us (13%)
  matrix products  0.76 us (1%)
    all_to_all x1, waiting for transfers between devices, _shards(): got = lax.all_to_all(merged, ('zh', 'zl'), 0, 0, tiled=True)  10.4 us
    pallas_call x4, Pallas kernels, _prompt(): pl.pallas_call(functools.partial(_prompt_kernel, wanted), out_shape=[jax....  8.97 us
    all_to_all x1, starting transfers between devices, _shards(): q0 = lax.all_to_all(spread, ('zh', 'zl'), 0, 0, tiled=True)  8.47 us
    unnamed x13, local copies, waits for them, and re-layouts  7.72 us
    all_to_all x1, waiting for transfers between devices, _shards(): q0 = lax.all_to_all(spread, ('zh', 'zl'), 0, 0, tiled=True)  6.4 us
    ppermute x1, waiting for transfers between devices, _shards(): first = lax.ppermute(q0, ('y', 'core'), _pairs(1))  4.8 us
    ppermute x1, waiting for transfers between devices, _shards(): back_second = lax.ppermute(part_second, ('y', 'core'), _pairs(2))  4.54 us
    ppermute x1, waiting for transfers between devices, _shards(): third = lax.ppermute(first, ('y', 'core'), _pairs(2))  4.35 us
  transfers between devices with their start and end apart: 9, of which 6 were waited for; matrix products, arithmetic and copies ran while one was open for 9% of the time, Pallas kernels for 13%

profile of v5, /device:TPU:2, one launch (start us, length us, event | category | flops | bytes accessed | tf_op | source)
XLA Modules:
  0.0 73.7 jit_solution(7498741087568233698)
XLA Ops:
  0.0 1.5 %broadcast_in_dim.26 = bf16[8,16,1024]{2,1,0:T(8,128)(2,1)} broadcast(bf16[16,1024]{1,0:T(8,128)(2,1)} %bitcast.34), dimensions={1,2} | broadcast | bytes 294912 | tf_op jit(solution)/shard_map/broadcast_in_dim | solution.py:238
  1.5 8.5 %all-to-all-start = ((bf16[8,16,1024]{2,1,0:T(8,128)(2,1)}), bf16[8,16,1024]{2,1,0:T(8,128)(2,1)S(1)}, u32[]{:S(2)}, u32[]{:S(2)}) async-start(bf16[8,16,1024]{2,1,0:T(8,128)(2,1)} %broadcast_in_dim.26), calls=%async_computation | async-start | bytes 524288 | tf_op jit(solution)/shard_map/all_to_all | solution.py:239
  10.0 0.0 copy-start.1
  10.0 5.5 %copy.13 = bf16[1,2,512,2,1024]{4,2,3,1,0:T(8,128)(2,1)} copy(bf16[1,2,512,2,1024]{4,3,2,1,0:T(2,128)(2,1)} %param.6) | data formatting | bytes 8388608 | tf_op args[1]
  15.4 6.4 %all-to-all-done.refs_0_ = bf16[8,16,1024]{2,1,0:T(8,128)(2,1)S(1)} async-done(((bf16[8,16,1024]{2,1,0:T(8,128)(2,1)}), bf16[8,16,1024]{2,1,0:T(8,128)(2,1)S(1)}, u32[]{:S(2)}, u32[]{:S(2)}) %all-to-all-start) | async-done | bytes 262176 | tf_op jit(solution)/shard_map/all_to_all | solution.py:239
  21.8 0.0 collective-permute-start.1
  21.8 1.6 %collective-permute-start = (bf16[8,16,1024]{2,1,0:T(8,128)(2,1)S(1)}, bf16[8,16,1024]{2,1,0:T(8,128)(2,1)S(1)}, u32[]{:S(2)}, u32[]{:S(2)}) collective-permute-start(bf16[8,16,1024]{2,1,0:T(8,128)(2,1)S(1)} %all-to-all-done.refs_0_), channel_id=1, source_target_pairs={{0,64},{4,196},{64,0},{68,132},{128,192},{132,68},{192,128},{196,4... | collective-permute-start | bytes 786440 | tf_op jit(solution)/shard_map/ppermute | solution.py:242
  23.4 4.8 %collective-permute-done.refs_0_ = bf16[8,16,1024]{2,1,0:T(8,128)(2,1)S(1)} collective-permute-done((bf16[8,16,1024]{2,1,0:T(8,128)(2,1)S(1)}, bf16[8,16,1024]{2,1,0:T(8,128)(2,1)S(1)}, u32[]{:S(2)}, u32[]{:S(2)}) %collective-permute-start) | collective-permute-done | bytes 262176 | tf_op jit(solution)/shard_map/ppermute | solution.py:242
  28.2 3.0 %collective-permute-start.4 = (bf16[8,16,1024]{2,1,0:T(8,128)(2,1)S(1)}, bf16[8,16,1024]{2,1,0:T(8,128)(2,1)S(1)}, u32[]{:S(2)}, u32[]{:S(2)}) collective-permute-start(bf16[8,16,1024]{2,1,0:T(8,128)(2,1)S(1)} %collective-permute-done.refs_0_), channel_id=1, source_target_pairs={{0,192},{4,68},{64,128},{68,4},{128,64},{132,196},{192,0},{196,132... | collective-permute-start | bytes 786440 | tf_op jit(solution)/shard_map/ppermute | solution.py:244
  31.2 0.2 collective-permute-start.2
  31.4 4.3 %collective-permute-done.4.refs_0_ = bf16[8,16,1024]{2,1,0:T(8,128)(2,1)S(1)} collective-permute-done((bf16[8,16,1024]{2,1,0:T(8,128)(2,1)S(1)}, bf16[8,16,1024]{2,1,0:T(8,128)(2,1)S(1)}, u32[]{:S(2)}, u32[]{:S(2)}) %collective-permute-start.4) | collective-permute-done | bytes 262176 | tf_op jit(solution)/shard_map/ppermute | solution.py:244
  35.8 0.0 collective-permute-done.1.refs_2_
  35.8 0.0 copy-done.1
  35.8 0.0 copy-start
  35.8 2.2 %copy-done = bf16[1,2,512,2,1024]{4,2,3,1,0:T(8,128)(2,1)S(1)} copy-done((bf16[1,2,512,2,1024]{4,2,3,1,0:T(8,128)(2,1)S(1)}, bf16[1,2,512,2,1024]{4,2,3,1,0:T(8,128)(2,1)}, u32[]{:S(2)}) %copy-start) | copy-done | bytes 4194328
  38.0 2.2 %shard_map.58 = bf16[8,16,1152]{2,1,0:T(8,128)(2,1)S(1)} custom-call(s32[1,128]{1,0:T(1,128)S(1)} %copy-done.1, bf16[8,16,1024]{2,1,0:T(8,128)(2,1)S(1)} %collective-permute-done.4.refs_0_, bf16[2,2,512,1024]{3,2,1,0:T(8,128)(2,1)S(1)} %bitcast.27, bf16[2,2,512,1024]{3,2,1,0:T(8,128)(2,1)S(1)} %collective-permute-done.1.refs_2_), custom_call_target="tpu_custom_call" | custom-call | flops 1073741824 | bytes 2097152 | tf_op jit(solution)/shard_map/pallas_call | solution.py:130
  40.2 3.1 %collective-permute-start.5 = (bf16[8,16,1152]{2,1,0:T(8,128)(2,1)S(1)}, bf16[8,16,1152]{2,1,0:T(8,128)(2,1)S(1)}, u32[]{:S(2)}, u32[]{:S(2)}) collective-permute-start(bf16[8,16,1152]{2,1,0:T(8,128)(2,1)S(1)} %shard_map.58), channel_id=1, source_target_pairs={{0,192},{4,68},{64,128},{68,4},{128,64},{132,196},{192,0},{196,132... | collective-permute-start | bytes 884744 | tf_op jit(solution)/shard_map/ppermute | solution.py:250
  43.3 2.2 %shard_map.57.all_refs_0_ = bf16[8,16,1152]{2,1,0:T(8,128)(2,1)S(1)} custom-call(s32[1,128]{1,0:T(1,128)S(1)} %copy-done.1, bf16[8,16,1024]{2,1,0:T(8,128)(2,1)S(1)} %collective-permute-done.refs_0_, bf16[2,2,512,1024]{3,2,1,0:T(8,128)(2,1)S(1)} %bitcast.28, bf16[2,2,512,1024]{3,2,1,0:T(8,128)(2,1)S(1)} %collective-permute-done.1.refs_2_), custom_call_target="tpu_custom_call" | custom-call | flops 1073741824 | bytes 2097152 | tf_op jit(solution)/shard_map/pallas_call | solution.py:130
  45.6 0.0 collective-permute-done.2.refs_0_
  45.6 2.3 %shard_map.56 = bf16[8,16,1152]{2,1,0:T(8,128)(2,1)S(1)} custom-call(s32[1,128]{1,0:T(1,128)S(1)} %copy-done.1, bf16[8,16,1024]{2,1,0:T(8,128)(2,1)S(1)} %collective-permute-done.2.refs_0_, bf16[2,2,512,1024]{3,2,1,0:T(8,128)(2,1)S(1)} %bitcast.29, bf16[2,2,512,1024]{3,2,1,0:T(8,128)(2,1)S(1)} %collective-permute-done.1.refs_2_), custom_call_target="tpu_custom_call" | custom-call | flops 1073741824 | bytes 2097152 | tf_op jit(solution)/shard_map/pallas_call | solution.py:130
  47.8 0.3 collective-permute-start.3
  48.2 0.1 collective-permute-done.5.all_refs_1_
  48.2 0.5 shard_map.59
  48.8 0.0 copy-start.4
  48.8 0.0 copy-start.3
  48.8 0.3 collective-permute-start.6
  49.1 0.0 copy-start.2
  49.1 2.3 %shard_map.55.all_refs_0_ = bf16[8,16,1152]{2,1,0:T(8,128)(2,1)S(1)} custom-call(s32[1,128]{1,0:T(1,128)S(1)} %copy-done.1, bf16[8,16,1024]{2,1,0:T(8,128)(2,1)S(1)} %all-to-all-done.refs_0_, bf16[2,2,512,1024]{3,2,1,0:T(8,128)(2,1)S(1)} %bitcast.30, bf16[2,2,512,1024]{3,2,1,0:T(8,128)(2,1)S(1)} %collective-permute-done.1.refs_2_), custom_call_target="tpu_custom_call" | custom-call | flops 1073741824 | bytes 2097152 | tf_op jit(solution)/shard_map/pallas_call | solution.py:130
  51.3 4.5 %collective-permute-done.3.all_refs_1_ = bf16[8,16,1152]{2,1,0:T(8,128)(2,1)S(1)} collective-permute-done((bf16[8,16,1152]{2,1,0:T(8,128)(2,1)S(1)}, bf16[8,16,1152]{2,1,0:T(8,128)(2,1)S(1)}, u32[]{:S(2)}, u32[]{:S(2)}) %collective-permute-start.3) | collective-permute-done | bytes 294944 | tf_op jit(solution)/shard_map/ppermute | solution.py:252
  55.9 0.0 collective-permute-done.6.all_refs_2_
  55.9 1.4 %shard_map.60 = bf16[8,16,1152]{2,1,0:T(8,128)(2,1)} custom-call(bf16[8,16,1152]{2,1,0:T(8,128)(2,1)S(1)} %shard_map.55.all_refs_0_, bf16[8,16,1152]{2,1,0:T(8,128)(2,1)S(1)} %collective-permute-done.3.all_refs_1_, bf16[8,16,1152]{2,1,0:T(8,128)(2,1)S(1)} %collective-permute-done.6.all_refs_2_), custom_call_target="tpu_custom_call" | custom-call | tf_op jit(solution)/shard_map/pallas_call | solution.py:180
  57.2 0.0 copy-done.4
  57.2 0.1 iota_compare_fusion
  57.3 3.4 %all-to-all-start.1 = ((bf16[8,16,1152]{2,1,0:T(8,128)(2,1)}), bf16[8,16,1152]{2,1,0:T(8,128)(2,1)S(1)}, u32[]{:S(2)}, u32[]{:S(2)}) async-start(bf16[8,16,1152]{2,1,0:T(8,128)(2,1)} %shard_map.60), calls=%async_computation.1 | async-start | bytes 589824 | tf_op jit(solution)/shard_map/all_to_all | solution.py:260
  60.8 0.0 copy-done.3
  60.8 0.0 copy-done.2
  60.8 0.5 copy.14
  61.3 0.5 fusion.7
  61.7 0.2 fusion.1
  61.9 0.3 convolution_divide_fusion
  62.3 10.4 %all-to-all-done.1.p_ref = bf16[8,16,1152]{2,1,0:T(8,128)(2,1)S(1)} async-done(((bf16[8,16,1152]{2,1,0:T(8,128)(2,1)}), bf16[8,16,1152]{2,1,0:T(8,128)(2,1)S(1)}, u32[]{:S(2)}, u32[]{:S(2)}) %all-to-all-start.1) | async-done | bytes 294944 | tf_op jit(solution)/shard_map/all_to_all | solution.py:260
  72.7 1.0 %shard_map.61 = bf16[16,1024]{1,0:T(8,128)(2,1)} custom-call(bf16[8,16,1152]{2,1,0:T(8,128)(2,1)S(1)} %all-to-all-done.1.p_ref, f32[16,1024]{1,0:T(8,128)S(1)} %bitcast.31, f32[16,128]{1,0:T(8,128)S(1)} %pad.4.sl_ref), custom_call_target="tpu_custom_call" | custom-call | tf_op jit(solution)/shard_map/pallas_call | solution.py:202
  (4 shorter events, 0.1 us)
Async XLA Ops:
  1.5 20.3 %all-to-all-start = ((bf16[8,16,1024]{2,1,0:T(8,128)(2,1)}), bf16[8,16,1024]{2,1,0:T(8,128)(2,1)S(1)}, u32[]{:S(2)}, u32[]{:S(2)}) async-start(bf16[8,16,1024]{2,1,0:T(8,128)(2,1)} %broadcast_in_dim.26), calls=%async_computation | async-start | bytes 524288 | tf_op jit(solution)/shard_map/all_to_all | solution.py:239
  10.0 25.8 %copy-start.1 = (s32[1,128]{1,0:T(1,128)S(1)}, s32[1,128]{1,0:T(1,128)}, u32[]{:S(2)}) copy-start(s32[1,128]{1,0:T(1,128)} %ids_ref.7) | copy-start | bytes 1540
  21.8 14.0 %collective-permute-start.1 = (bf16[2,2,512,1024]{3,2,1,0:T(8,128)(2,1)}, bf16[2,2,512,1024]{3,2,1,0:T(8,128)(2,1)S(1)}, u32[]{:S(2)}, u32[]{:S(2)}) collective-permute-start(bf16[2,2,512,1024]{3,2,1,0:T(8,128)(2,1)} %bitcast.26), channel_id=1, source_target_pairs={{0,4},{4,0},{1,5},{5,1},{2,6},{6,2},{3,7},{7,3},{8,12},{12,8},{9,1... | collective-permute-start | bytes 12582920 | tf_op jit(solution)/shard_map/ppermute | solution.py:241
  21.8 6.4 %collective-permute-start = (bf16[8,16,1024]{2,1,0:T(8,128)(2,1)S(1)}, bf16[8,16,1024]{2,1,0:T(8,128)(2,1)S(1)}, u32[]{:S(2)}, u32[]{:S(2)}) collective-permute-start(bf16[8,16,1024]{2,1,0:T(8,128)(2,1)S(1)} %all-to-all-done.refs_0_), channel_id=1, source_target_pairs={{0,64},{4,196},{64,0},{68,132},{128,192},{132,68},{192,128},{196,4... | collective-permute-start | bytes 786440 | tf_op jit(solution)/shard_map/ppermute | solution.py:242
  28.2 7.6 %collective-permute-start.4 = (bf16[8,16,1024]{2,1,0:T(8,128)(2,1)S(1)}, bf16[8,16,1024]{2,1,0:T(8,128)(2,1)S(1)}, u32[]{:S(2)}, u32[]{:S(2)}) collective-permute-start(bf16[8,16,1024]{2,1,0:T(8,128)(2,1)S(1)} %collective-permute-done.refs_0_), channel_id=1, source_target_pairs={{0,192},{4,68},{64,128},{68,4},{128,64},{132,196},{192,0},{196,132... | collective-permute-start | bytes 786440 | tf_op jit(solution)/shard_map/ppermute | solution.py:244
  31.2 14.3 %collective-permute-start.2 = (bf16[8,16,1024]{2,1,0:T(8,128)(2,1)S(1)}, bf16[8,16,1024]{2,1,0:T(8,128)(2,1)S(1)}, u32[]{:S(2)}, u32[]{:S(2)}) collective-permute-start(bf16[8,16,1024]{2,1,0:T(8,128)(2,1)S(1)} %all-to-all-done.refs_0_), channel_id=1, source_target_pairs={{0,192},{4,68},{64,128},{68,4},{128,64},{132,196},{192,0},{196,132... | collective-permute-start | bytes 786440 | tf_op jit(solution)/shard_map/ppermute | solution.py:245
  35.8 2.2 %copy-start = (bf16[1,2,512,2,1024]{4,2,3,1,0:T(8,128)(2,1)S(1)}, bf16[1,2,512,2,1024]{4,2,3,1,0:T(8,128)(2,1)}, u32[]{:S(2)}) copy-start(bf16[1,2,512,2,1024]{4,2,3,1,0:T(8,128)(2,1)} %copy.13) | copy-start | bytes 12582916
  40.2 8.0 %collective-permute-start.5 = (bf16[8,16,1152]{2,1,0:T(8,128)(2,1)S(1)}, bf16[8,16,1152]{2,1,0:T(8,128)(2,1)S(1)}, u32[]{:S(2)}, u32[]{:S(2)}) collective-permute-start(bf16[8,16,1152]{2,1,0:T(8,128)(2,1)S(1)} %shard_map.58), channel_id=1, source_target_pairs={{0,192},{4,68},{64,128},{68,4},{128,64},{132,196},{192,0},{196,132... | collective-permute-start | bytes 884744 | tf_op jit(solution)/shard_map/ppermute | solution.py:250
  47.8 8.0 %collective-permute-start.3 = (bf16[8,16,1152]{2,1,0:T(8,128)(2,1)S(1)}, bf16[8,16,1152]{2,1,0:T(8,128)(2,1)S(1)}, u32[]{:S(2)}, u32[]{:S(2)}) collective-permute-start(bf16[8,16,1152]{2,1,0:T(8,128)(2,1)S(1)} %shard_map.56), channel_id=1, source_target_pairs={{0,192},{4,68},{64,128},{68,4},{128,64},{132,196},{192,0},{196,132... | collective-permute-start | bytes 884744 | tf_op jit(solution)/shard_map/ppermute | solution.py:252
  48.8 8.5 %copy-start.4 = (s32[1,16]{1,0:T(1,128)S(1)}, s32[1,16]{1,0:T(1,128)}, u32[]{:S(2)}) copy-start(s32[1,16]{1,0:T(1,128)} %param.8) | copy-start | bytes 196
  48.8 12.0 %copy-start.3 = (bf16[1,16,1024]{2,1,0:T(8,128)(2,1)S(1)}, bf16[1,16,1024]{2,1,0:T(8,128)(2,1)}, u32[]{:S(2)}) copy-start(bf16[1,16,1024]{2,1,0:T(8,128)(2,1)} %param.5) | copy-start | bytes 98308
  48.8 7.1 %collective-permute-start.6 = (bf16[8,16,1152]{2,1,0:T(8,128)(2,1)S(1)}, bf16[8,16,1152]{2,1,0:T(8,128)(2,1)S(1)}, u32[]{:S(2)}, u32[]{:S(2)}) collective-permute-start(bf16[8,16,1152]{2,1,0:T(8,128)(2,1)S(1)} %shard_map.59), channel_id=1, source_target_pairs={{0,64},{4,196},{64,0},{68,132},{128,192},{132,68},{192,128},{196,4... | collective-permute-start | bytes 884744 | tf_op jit(solution)/shard_map/ppermute | solution.py:254
  49.1 11.7 %copy-start.2 = (bf16[1,16,256,2,128]{4,3,2,1,0:T(2,128)(2,1)S(1)}, bf16[1,16,256,2,128]{4,3,2,1,0:T(2,128)(2,1)}, u32[]{:S(2)}) copy-start(bf16[1,16,256,2,128]{4,3,2,1,0:T(2,128)(2,1)} %param.7) | copy-start | bytes 6291460
  57.3 15.4 %all-to-all-start.1 = ((bf16[8,16,1152]{2,1,0:T(8,128)(2,1)}), bf16[8,16,1152]{2,1,0:T(8,128)(2,1)S(1)}, u32[]{:S(2)}, u32[]{:S(2)}) async-start(bf16[8,16,1152]{2,1,0:T(8,128)(2,1)} %shard_map.60), calls=%async_computation.1 | async-start | bytes 589824 | tf_op jit(solution)/shard_map/all_to_all | solution.py:260

commit v6 on v5

--- a/solution.py
+++ b/solution.py
@@ -242,14 +242,15 @@
     first = lax.ppermute(q0, ("y", "core"), _pairs(1))
     first, q0 = lax.optimization_barrier((first, q0))
     third = lax.ppermute(first, ("y", "core"), _pairs(2))
+    q0, par = lax.optimization_barrier((q0, par))
     second = lax.ppermute(q0, ("y", "core"), _pairs(2))
 
     def part(which, block):
         return _prompt((which,), group_of, [block], own, par)[0]
 
+    part_first, third = lax.optimization_barrier((part(1, first), third))
     back_third = lax.ppermute(part(3, third), ("y", "core"), _pairs(2))
-    part_second, part_first = lax.optimization_barrier((part(2, second), part(1, first)))
-    back_second = lax.ppermute(part_second, ("y", "core"), _pairs(2))
+    back_second = lax.ppermute(part(2, second), ("y", "core"), _pairs(2))
     merged = _merge([part_first, back_third])
     back_first = lax.ppermute(merged, ("y", "core"), _pairs(1))
     merged = _merge([part(0, q0), back_second, back_first])

time: 74.8 us -> 75.5 us (level)
  starting transfers between devices: 20.4 us -> 23.2 us
  waiting for transfers between devices: 30.6 us -> 28.9 us
    ppermute x1, waiting for transfers between devices: 4.35 us -> 0.13 us  [_shards(): third = lax.ppermute(first, ('y', 'core'), _pairs(2))]
    ppermute x1, starting transfers between devices: 0.22 us -> 3.01 us  [_shards(): second = lax.ppermute(q0, ('y', 'core'), _pairs(2))]
    ppermute x1, starting transfers between devices: 0.31 us -> 3.1 us  [_shards(): back_second = lax.ppermute(part(2, second), ('y', 'core'), _pairs(2))]
    ppermute x1, starting transfers between devices: 3.1 us -> 0.31 us  [_shards(): back_third = lax.ppermute(part(3, third), ('y', 'core'), _pairs(2))]
    ppermute x1, waiting for transfers between devices: 4.54 us -> 2.2 us  [_shards(): back_second = lax.ppermute(part(2, second), ('y', 'core'), _pairs(2))]
    ppermute x1, waiting for transfers between devices: 0.01 us -> 2.24 us  [_shards(): back_first = lax.ppermute(merged, ('y', 'core'), _pairs(1))]
    ppermute x1, waiting for transfers between devices: 0.01 us -> 2.02 us  [_shards(): second = lax.ppermute(q0, ('y', 'core'), _pairs(2))]
    ppermute x1, waiting for transfers between devices: 0.1 us -> 1.41 us  [_shards(): back_third = lax.ppermute(part(3, third), ('y', 'core'), _pairs(2))]
  transfers between devices with their start and end apart: 9 -> 9, of which waited for: 6 -> 8; matrix products, arithmetic and copies ran while one was open for 9% -> 9% of each run, Pallas kernels for 13% -> 13%
where the time goes in v6:
time: 75.5 us; the launch traced here: 75 us
  waiting for transfers between devices  28.9 us (38%)
  starting transfers between devices  23.2 us (31%)
  Pallas kernels  11.8 us (16%)
  local copies, waits for them, and re-layouts  9.95 us (13%)
    all_to_all x1, waiting for transfers between devices, _shards(): got = lax.all_to_all(merged, ('zh', 'zl'), 0, 0, tiled=True)  9.73 us
    pallas_call x4, Pallas kernels, _prompt(): pl.pallas_call(functools.partial(_prompt_kernel, wanted), out_shape=[jax....  8.96 us
    all_to_all x1, starting transfers between devices, _shards(): q0 = lax.all_to_all(spread, ('zh', 'zl'), 0, 0, tiled=True)  8.47 us
    unnamed x13, local copies, waits for them, and re-layouts  7.97 us
    all_to_all x1, waiting for transfers between devices, _shards(): q0 = lax.all_to_all(spread, ('zh', 'zl'), 0, 0, tiled=True)  6.4 us
    ppermute x1, waiting for transfers between devices, _shards(): first = lax.ppermute(q0, ('y', 'core'), _pairs(1))  4.8 us
    all_to_all x1, starting transfers between devices, _shards(): got = lax.all_to_all(merged, ('zh', 'zl'), 0, 0, tiled=True)  3.42 us
    ppermute x1, starting transfers between devices, _shards(): back_second = lax.ppermute(part(2, second), ('y', 'core'), _pairs(2))  3.1 us
  transfers between devices with their start and end apart: 9, of which 8 were waited for; matrix products, arithmetic and copies ran while one was open for 9% of the time, Pallas kernels for 13%

profile of v6, /device:TPU:2, one launch (start us, length us, event | category | flops | bytes accessed | tf_op | source)
XLA Modules:
  0.0 75.0 jit_solution(11934800958940228577)
XLA Ops:
  0.0 1.5 %broadcast_in_dim.26 = bf16[8,16,1024]{2,1,0:T(8,128)(2,1)} broadcast(bf16[16,1024]{1,0:T(8,128)(2,1)} %bitcast.34), dimensions={1,2} | broadcast | bytes 294912 | tf_op jit(solution)/shard_map/broadcast_in_dim | solution.py:238
  1.5 8.5 %all-to-all-start = ((bf16[8,16,1024]{2,1,0:T(8,128)(2,1)}), bf16[8,16,1024]{2,1,0:T(8,128)(2,1)S(1)}, u32[]{:S(2)}, u32[]{:S(2)}) async-start(bf16[8,16,1024]{2,1,0:T(8,128)(2,1)} %broadcast_in_dim.26), calls=%async_computation | async-start | bytes 524288 | tf_op jit(solution)/shard_map/all_to_all | solution.py:239
  10.0 0.0 copy-start.1
  10.0 5.5 %copy.13 = bf16[1,2,512,2,1024]{4,2,3,1,0:T(8,128)(2,1)} copy(bf16[1,2,512,2,1024]{4,3,2,1,0:T(2,128)(2,1)} %param.6) | data formatting | bytes 8388608 | tf_op args[1]
  15.4 6.4 %all-to-all-done.refs_0_ = bf16[8,16,1024]{2,1,0:T(8,128)(2,1)S(1)} async-done(((bf16[8,16,1024]{2,1,0:T(8,128)(2,1)}), bf16[8,16,1024]{2,1,0:T(8,128)(2,1)S(1)}, u32[]{:S(2)}, u32[]{:S(2)}) %all-to-all-start) | async-done | bytes 262176 | tf_op jit(solution)/shard_map/all_to_all | solution.py:239
  21.8 0.0 collective-permute-start.1
  21.8 1.6 %collective-permute-start = (bf16[8,16,1024]{2,1,0:T(8,128)(2,1)S(1)}, bf16[8,16,1024]{2,1,0:T(8,128)(2,1)S(1)}, u32[]{:S(2)}, u32[]{:S(2)}) collective-permute-start(bf16[8,16,1024]{2,1,0:T(8,128)(2,1)S(1)} %all-to-all-done.refs_0_), channel_id=1, source_target_pairs={{0,64},{4,196},{64,0},{68,132},{128,192},{132,68},{192,128},{196,4... | collective-permute-start | bytes 786440 | tf_op jit(solution)/shard_map/ppermute | solution.py:242
  23.4 4.8 %collective-permute-done.refs_0_ = bf16[8,16,1024]{2,1,0:T(8,128)(2,1)S(1)} collective-permute-done((bf16[8,16,1024]{2,1,0:T(8,128)(2,1)S(1)}, bf16[8,16,1024]{2,1,0:T(8,128)(2,1)S(1)}, u32[]{:S(2)}, u32[]{:S(2)}) %collective-permute-start) | collective-permute-done | bytes 262176 | tf_op jit(solution)/shard_map/ppermute | solution.py:242
  28.2 3.0 %collective-permute-start.4 = (bf16[8,16,1024]{2,1,0:T(8,128)(2,1)S(1)}, bf16[8,16,1024]{2,1,0:T(8,128)(2,1)S(1)}, u32[]{:S(2)}, u32[]{:S(2)}) collective-permute-start(bf16[8,16,1024]{2,1,0:T(8,128)(2,1)S(1)} %collective-permute-done.refs_0_), channel_id=1, source_target_pairs={{0,192},{4,68},{64,128},{68,4},{128,64},{132,196},{192,0},{196,132... | collective-permute-start | bytes 786440 | tf_op jit(solution)/shard_map/ppermute | solution.py:244
  31.2 0.0 collective-permute-done.1.refs_2_
  31.2 0.0 copy-done.1
  31.2 0.0 copy-start
  31.2 2.2 %copy-done = bf16[1,2,512,2,1024]{4,2,3,1,0:T(8,128)(2,1)S(1)} copy-done((bf16[1,2,512,2,1024]{4,2,3,1,0:T(8,128)(2,1)S(1)}, bf16[1,2,512,2,1024]{4,2,3,1,0:T(8,128)(2,1)}, u32[]{:S(2)}) %copy-start) | copy-done | bytes 4194328
  33.4 2.2 %shard_map.57.all_refs_0_ = bf16[8,16,1152]{2,1,0:T(8,128)(2,1)S(1)} custom-call(s32[1,128]{1,0:T(1,128)S(1)} %copy-done.1, bf16[8,16,1024]{2,1,0:T(8,128)(2,1)S(1)} %collective-permute-done.refs_0_, bf16[2,2,512,1024]{3,2,1,0:T(8,128)(2,1)S(1)} %bitcast.27, bf16[2,2,512,1024]{3,2,1,0:T(8,128)(2,1)S(1)} %collective-permute-done.1.refs_2_), custom_call_target="tpu_custom_call" | custom-call | flops 1073741824 | bytes 2097152 | tf_op jit(solution)/shard_map/pallas_call | solution.py:130
  35.7 0.1 collective-permute-done.4.refs_0_
  35.8 3.0 %collective-permute-start.2 = (bf16[8,16,1024]{2,1,0:T(8,128)(2,1)S(1)}, bf16[8,16,1024]{2,1,0:T(8,128)(2,1)S(1)}, u32[]{:S(2)}, u32[]{:S(2)}) collective-permute-start(bf16[8,16,1024]{2,1,0:T(8,128)(2,1)S(1)} %all-to-all-done.refs_0_), channel_id=1, source_target_pairs={{0,192},{4,68},{64,128},{68,4},{128,64},{132,196},{192,0},{196,132... | collective-permute-start | bytes 786440 | tf_op jit(solution)/shard_map/ppermute | solution.py:246
  38.8 2.2 %shard_map.58 = bf16[8,16,1152]{2,1,0:T(8,128)(2,1)S(1)} custom-call(s32[1,128]{1,0:T(1,128)S(1)} %copy-done.1, bf16[8,16,1024]{2,1,0:T(8,128)(2,1)S(1)} %collective-permute-done.4.refs_0_, bf16[2,2,512,1024]{3,2,1,0:T(8,128)(2,1)S(1)} %bitcast.28, bf16[2,2,512,1024]{3,2,1,0:T(8,128)(2,1)S(1)} %collective-permute-done.1.refs_2_), custom_call_target="tpu_custom_call" | custom-call | flops 1073741824 | bytes 2097152 | tf_op jit(solution)/shard_map/pallas_call | solution.py:130
  41.0 0.3 collective-permute-start.5
  41.4 2.0 %collective-permute-done.2.refs_0_ = bf16[8,16,1024]{2,1,0:T(8,128)(2,1)S(1)} collective-permute-done((bf16[8,16,1024]{2,1,0:T(8,128)(2,1)S(1)}, bf16[8,16,1024]{2,1,0:T(8,128)(2,1)S(1)}, u32[]{:S(2)}, u32[]{:S(2)}) %collective-permute-start.2) | collective-permute-done | bytes 262176 | tf_op jit(solution)/shard_map/ppermute | solution.py:246
  43.4 2.2 %shard_map.56 = bf16[8,16,1152]{2,1,0:T(8,128)(2,1)S(1)} custom-call(s32[1,128]{1,0:T(1,128)S(1)} %copy-done.1, bf16[8,16,1024]{2,1,0:T(8,128)(2,1)S(1)} %collective-permute-done.2.refs_0_, bf16[2,2,512,1024]{3,2,1,0:T(8,128)(2,1)S(1)} %bitcast.29, bf16[2,2,512,1024]{3,2,1,0:T(8,128)(2,1)S(1)} %collective-permute-done.1.refs_2_), custom_call_target="tpu_custom_call" | custom-call | flops 1073741824 | bytes 2097152 | tf_op jit(solution)/shard_map/pallas_call | solution.py:130
  45.6 3.1 %collective-permute-start.3 = (bf16[8,16,1152]{2,1,0:T(8,128)(2,1)S(1)}, bf16[8,16,1152]{2,1,0:T(8,128)(2,1)S(1)}, u32[]{:S(2)}, u32[]{:S(2)}) collective-permute-start(bf16[8,16,1152]{2,1,0:T(8,128)(2,1)S(1)} %shard_map.56), channel_id=1, source_target_pairs={{0,192},{4,68},{64,128},{68,4},{128,64},{132,196},{192,0},{196,132... | collective-permute-start | bytes 884744 | tf_op jit(solution)/shard_map/ppermute | solution.py:253
  48.7 1.4 %collective-permute-done.5.all_refs_1_ = bf16[8,16,1152]{2,1,0:T(8,128)(2,1)S(1)} collective-permute-done((bf16[8,16,1152]{2,1,0:T(8,128)(2,1)S(1)}, bf16[8,16,1152]{2,1,0:T(8,128)(2,1)S(1)}, u32[]{:S(2)}, u32[]{:S(2)}) %collective-permute-start.5) | collective-permute-done | bytes 294944 | tf_op jit(solution)/shard_map/ppermute | solution.py:252
  50.1 0.5 shard_map.59
  50.6 0.3 collective-permute-start.6
  50.9 0.0 copy-start.2
  50.9 2.3 %shard_map.55.all_refs_0_ = bf16[8,16,1152]{2,1,0:T(8,128)(2,1)S(1)} custom-call(s32[1,128]{1,0:T(1,128)S(1)} %copy-done.1, bf16[8,16,1024]{2,1,0:T(8,128)(2,1)S(1)} %all-to-all-done.refs_0_, bf16[2,2,512,1024]{3,2,1,0:T(8,128)(2,1)S(1)} %bitcast.30, bf16[2,2,512,1024]{3,2,1,0:T(8,128)(2,1)S(1)} %collective-permute-done.1.refs_2_), custom_call_target="tpu_custom_call" | custom-call | flops 1073741824 | bytes 2097152 | tf_op jit(solution)/shard_map/pallas_call | solution.py:130
  53.2 2.2 %collective-permute-done.3.all_refs_1_ = bf16[8,16,1152]{2,1,0:T(8,128)(2,1)S(1)} collective-permute-done((bf16[8,16,1152]{2,1,0:T(8,128)(2,1)S(1)}, bf16[8,16,1152]{2,1,0:T(8,128)(2,1)S(1)}, u32[]{:S(2)}, u32[]{:S(2)}) %collective-permute-start.3) | collective-permute-done | bytes 294944 | tf_op jit(solution)/shard_map/ppermute | solution.py:253
  55.4 2.2 %collective-permute-done.6.all_refs_2_ = bf16[8,16,1152]{2,1,0:T(8,128)(2,1)S(1)} collective-permute-done((bf16[8,16,1152]{2,1,0:T(8,128)(2,1)S(1)}, bf16[8,16,1152]{2,1,0:T(8,128)(2,1)S(1)}, u32[]{:S(2)}, u32[]{:S(2)}) %collective-permute-start.6) | collective-permute-done | bytes 294944 | tf_op jit(solution)/shard_map/ppermute | solution.py:255
  57.6 1.4 %shard_map.60 = bf16[8,16,1152]{2,1,0:T(8,128)(2,1)} custom-call(bf16[8,16,1152]{2,1,0:T(8,128)(2,1)S(1)} %shard_map.55.all_refs_0_, bf16[8,16,1152]{2,1,0:T(8,128)(2,1)S(1)} %collective-permute-done.3.all_refs_1_, bf16[8,16,1152]{2,1,0:T(8,128)(2,1)S(1)} %collective-permute-done.6.all_refs_2_), custom_call_target="tpu_custom_call" | custom-call | tf_op jit(solution)/shard_map/pallas_call | solution.py:180
  59.0 0.0 copy-done.2
  59.0 0.0 copy-start.3
  59.0 0.0 copy-start.4
  59.0 0.5 copy.14
  59.5 0.3 copy-done.3
  59.8 0.0 copy-done.4
  59.8 0.1 iota_compare_fusion
  59.8 3.4 %all-to-all-start.1 = ((bf16[8,16,1152]{2,1,0:T(8,128)(2,1)}), bf16[8,16,1152]{2,1,0:T(8,128)(2,1)S(1)}, u32[]{:S(2)}, u32[]{:S(2)}) async-start(bf16[8,16,1152]{2,1,0:T(8,128)(2,1)} %shard_map.60), calls=%async_computation.1 | async-start | bytes 589824 | tf_op jit(solution)/shard_map/all_to_all | solution.py:261
  63.3 0.5 fusion.7
  63.7 0.2 fusion.1
  63.9 0.3 convolution_divide_fusion
  64.3 9.7 %all-to-all-done.1.p_ref = bf16[8,16,1152]{2,1,0:T(8,128)(2,1)S(1)} async-done(((bf16[8,16,1152]{2,1,0:T(8,128)(2,1)}), bf16[8,16,1152]{2,1,0:T(8,128)(2,1)S(1)}, u32[]{:S(2)}, u32[]{:S(2)}) %all-to-all-start.1) | async-done | bytes 294944 | tf_op jit(solution)/shard_map/all_to_all | solution.py:261
  74.0 1.0 %shard_map.61 = bf16[16,1024]{1,0:T(8,128)(2,1)} custom-call(bf16[8,16,1152]{2,1,0:T(8,128)(2,1)S(1)} %all-to-all-done.1.p_ref, f32[16,1024]{1,0:T(8,128)S(1)} %bitcast.31, f32[16,128]{1,0:T(8,128)S(1)} %pad.4.sl_ref), custom_call_target="tpu_custom_call" | custom-call | tf_op jit(solution)/shard_map/pallas_call | solution.py:202
  (4 shorter events, 0.0 us)
Async XLA Ops:
  1.5 20.3 %all-to-all-start = ((bf16[8,16,1024]{2,1,0:T(8,128)(2,1)}), bf16[8,16,1024]{2,1,0:T(8,128)(2,1)S(1)}, u32[]{:S(2)}, u32[]{:S(2)}) async-start(bf16[8,16,1024]{2,1,0:T(8,128)(2,1)} %broadcast_in_dim.26), calls=%async_computation | async-start | bytes 524288 | tf_op jit(solution)/shard_map/all_to_all | solution.py:239
  10.0 21.3 %copy-start.1 = (s32[1,128]{1,0:T(1,128)S(1)}, s32[1,128]{1,0:T(1,128)}, u32[]{:S(2)}) copy-start(s32[1,128]{1,0:T(1,128)} %ids_ref.7) | copy-start | bytes 1540
  21.8 9.4 %collective-permute-start.1 = (bf16[2,2,512,1024]{3,2,1,0:T(8,128)(2,1)}, bf16[2,2,512,1024]{3,2,1,0:T(8,128)(2,1)S(1)}, u32[]{:S(2)}, u32[]{:S(2)}) collective-permute-start(bf16[2,2,512,1024]{3,2,1,0:T(8,128)(2,1)} %bitcast.26), channel_id=1, source_target_pairs={{0,4},{4,0},{1,5},{5,1},{2,6},{6,2},{3,7},{7,3},{8,12},{12,8},{9,1... | collective-permute-start | bytes 12582920 | tf_op jit(solution)/shard_map/ppermute | solution.py:241
  21.8 6.4 %collective-permute-start = (bf16[8,16,1024]{2,1,0:T(8,128)(2,1)S(1)}, bf16[8,16,1024]{2,1,0:T(8,128)(2,1)S(1)}, u32[]{:S(2)}, u32[]{:S(2)}) collective-permute-start(bf16[8,16,1024]{2,1,0:T(8,128)(2,1)S(1)} %all-to-all-done.refs_0_), channel_id=1, source_target_pairs={{0,64},{4,196},{64,0},{68,132},{128,192},{132,68},{192,128},{196,4... | collective-permute-start | bytes 786440 | tf_op jit(solution)/shard_map/ppermute | solution.py:242
  28.2 7.6 %collective-permute-start.4 = (bf16[8,16,1024]{2,1,0:T(8,128)(2,1)S(1)}, bf16[8,16,1024]{2,1,0:T(8,128)(2,1)S(1)}, u32[]{:S(2)}, u32[]{:S(2)}) collective-permute-start(bf16[8,16,1024]{2,1,0:T(8,128)(2,1)S(1)} %collective-permute-done.refs_0_), channel_id=1, source_target_pairs={{0,192},{4,68},{64,128},{68,4},{128,64},{132,196},{192,0},{196,132... | collective-permute-start | bytes 786440 | tf_op jit(solution)/shard_map/ppermute | solution.py:244
  31.2 2.2 %copy-start = (bf16[1,2,512,2,1024]{4,2,3,1,0:T(8,128)(2,1)S(1)}, bf16[1,2,512,2,1024]{4,2,3,1,0:T(8,128)(2,1)}, u32[]{:S(2)}) copy-start(bf16[1,2,512,2,1024]{4,2,3,1,0:T(8,128)(2,1)} %copy.13) | copy-start | bytes 12582916
  35.8 7.6 %collective-permute-start.2 = (bf16[8,16,1024]{2,1,0:T(8,128)(2,1)S(1)}, bf16[8,16,1024]{2,1,0:T(8,128)(2,1)S(1)}, u32[]{:S(2)}, u32[]{:S(2)}) collective-permute-start(bf16[8,16,1024]{2,1,0:T(8,128)(2,1)S(1)} %all-to-all-done.refs_0_), channel_id=1, source_target_pairs={{0,192},{4,68},{64,128},{68,4},{128,64},{132,196},{192,0},{196,132... | collective-permute-start | bytes 786440 | tf_op jit(solution)/shard_map/ppermute | solution.py:246
  41.0 9.1 %collective-permute-start.5 = (bf16[8,16,1152]{2,1,0:T(8,128)(2,1)S(1)}, bf16[8,16,1152]{2,1,0:T(8,128)(2,1)S(1)}, u32[]{:S(2)}, u32[]{:S(2)}) collective-permute-start(bf16[8,16,1152]{2,1,0:T(8,128)(2,1)S(1)} %shard_map.58), channel_id=1, source_target_pairs={{0,192},{4,68},{64,128},{68,4},{128,64},{132,196},{192,0},{196,132... | collective-permute-start | bytes 884744 | tf_op jit(solution)/shard_map/ppermute | solution.py:252
  45.6 9.8 %collective-permute-start.3 = (bf16[8,16,1152]{2,1,0:T(8,128)(2,1)S(1)}, bf16[8,16,1152]{2,1,0:T(8,128)(2,1)S(1)}, u32[]{:S(2)}, u32[]{:S(2)}) collective-permute-start(bf16[8,16,1152]{2,1,0:T(8,128)(2,1)S(1)} %shard_map.56), channel_id=1, source_target_pairs={{0,192},{4,68},{64,128},{68,4},{128,64},{132,196},{192,0},{196,132... | collective-permute-start | bytes 884744 | tf_op jit(solution)/shard_map/ppermute | solution.py:253
  50.6 7.0 %collective-permute-start.6 = (bf16[8,16,1152]{2,1,0:T(8,128)(2,1)S(1)}, bf16[8,16,1152]{2,1,0:T(8,128)(2,1)S(1)}, u32[]{:S(2)}, u32[]{:S(2)}) collective-permute-start(bf16[8,16,1152]{2,1,0:T(8,128)(2,1)S(1)} %shard_map.59), channel_id=1, source_target_pairs={{0,64},{4,196},{64,0},{68,132},{128,192},{132,68},{192,128},{196,4... | collective-permute-start | bytes 884744 | tf_op jit(solution)/shard_map/ppermute | solution.py:255
  50.9 8.1 %copy-start.2 = (bf16[1,16,256,2,128]{4,3,2,1,0:T(2,128)(2,1)S(1)}, bf16[1,16,256,2,128]{4,3,2,1,0:T(2,128)(2,1)}, u32[]{:S(2)}) copy-start(bf16[1,16,256,2,128]{4,3,2,1,0:T(2,128)(2,1)} %param.7) | copy-start | bytes 6291460
  59.0 0.8 %copy-start.3 = (bf16[1,16,1024]{2,1,0:T(8,128)(2,1)S(1)}, bf16[1,16,1024]{2,1,0:T(8,128)(2,1)}, u32[]{:S(2)}) copy-start(bf16[1,16,1024]{2,1,0:T(8,128)(2,1)} %param.5) | copy-start | bytes 98308
  59.0 0.8 %copy-start.4 = (s32[1,16]{1,0:T(1,128)S(1)}, s32[1,16]{1,0:T(1,128)}, u32[]{:S(2)}) copy-start(s32[1,16]{1,0:T(1,128)} %param.8) | copy-start | bytes 196
  59.8 14.2 %all-to-all-start.1 = ((bf16[8,16,1152]{2,1,0:T(8,128)(2,1)}), bf16[8,16,1152]{2,1,0:T(8,128)(2,1)S(1)}, u32[]{:S(2)}, u32[]{:S(2)}) async-start(bf16[8,16,1152]{2,1,0:T(8,128)(2,1)} %shard_map.60), calls=%async_computation.1 | async-start | bytes 589824 | tf_op jit(solution)/shard_map/all_to_all | solution.py:261

commit v7 on v6

--- a/solution.py
+++ b/solution.py
@@ -242,7 +242,6 @@
     first = lax.ppermute(q0, ("y", "core"), _pairs(1))
     first, q0 = lax.optimization_barrier((first, q0))
     third = lax.ppermute(first, ("y", "core"), _pairs(2))
-    q0, par = lax.optimization_barrier((q0, par))
     second = lax.ppermute(q0, ("y", "core"), _pairs(2))
 
     def part(which, block):

time: 75.5 us -> 72.6 us (0.962)
  starting transfers between devices: 23.2 us -> 20.5 us
    ppermute x1, starting transfers between devices: 3.01 us -> 0.22 us  [_shards(): second = lax.ppermute(q0, ('y', 'core'), _pairs(2))]
    ppermute x1, starting transfers between devices: 0.31 us -> 3.1 us  [_shards(): back_third = lax.ppermute(part(3, third), ('y', 'core'), _pairs(2))]
    ppermute x1, starting transfers between devices: 3.1 us -> 0.44 us  [_shards(): back_second = lax.ppermute(part(2, second), ('y', 'core'), _pairs(2))]
    ppermute x1, waiting for transfers between devices: 2.2 us -> 4.35 us  [_shards(): back_second = lax.ppermute(part(2, second), ('y', 'core'), _pairs(2))]
    ppermute x1, waiting for transfers between devices: 2.24 us -> 0.1 us  [_shards(): back_first = lax.ppermute(merged, ('y', 'core'), _pairs(1))]
    ppermute x1, waiting for transfers between devices: 2.02 us -> 0.01 us  [_shards(): second = lax.ppermute(q0, ('y', 'core'), _pairs(2))]
    all_to_all x1, waiting for transfers between devices: 9.73 us -> 10.8 us  [_shards(): got = lax.all_to_all(merged, ('zh', 'zl'), 0, 0, tiled=True)]
    ppermute x1, waiting for transfers between devices: 1.41 us -> 2.24 us  [_shards(): back_third = lax.ppermute(part(3, third), ('y', 'core'), _pairs(2))]
  transfers between devices with their start and end apart: 9 -> 9, of which waited for: 8 -> 6; matrix products, arithmetic and copies ran while one was open for 9% -> 9% of each run, Pallas kernels for 13% -> 13%
where the time goes in v7:
time: 72.6 us; the launch traced here: 72.1 us
  waiting for transfers between devices  28.7 us (40%)
  starting transfers between devices  20.5 us (28%)
  Pallas kernels  11.8 us (16%)
  local copies, waits for them, and re-layouts  9.95 us (14%)
  matrix products  0.75 us (1%)
    all_to_all x1, waiting for transfers between devices, _shards(): got = lax.all_to_all(merged, ('zh', 'zl'), 0, 0, tiled=True)  10.8 us
    pallas_call x4, Pallas kernels, _prompt(): pl.pallas_call(functools.partial(_prompt_kernel, wanted), out_shape=[jax....  8.97 us
    all_to_all x1, starting transfers between devices, _shards(): q0 = lax.all_to_all(spread, ('zh', 'zl'), 0, 0, tiled=True)  8.47 us
    unnamed x13, local copies, waits for them, and re-layouts  7.97 us
    all_to_all x1, waiting for transfers between devices, _shards(): q0 = lax.all_to_all(spread, ('zh', 'zl'), 0, 0, tiled=True)  6.4 us
    ppermute x1, waiting for transfers between devices, _shards(): first = lax.ppermute(q0, ('y', 'core'), _pairs(1))  4.8 us
    ppermute x1, waiting for transfers between devices, _shards(): back_second = lax.ppermute(part(2, second), ('y', 'core'), _pairs(2))  4.35 us
    all_to_all x1, starting transfers between devices, _shards(): got = lax.all_to_all(merged, ('zh', 'zl'), 0, 0, tiled=True)  3.42 us
  transfers between devices with their start and end apart: 9, of which 6 were waited for; matrix products, arithmetic and copies ran while one was open for 9% of the time, Pallas kernels for 13%

profile of v7, /device:TPU:2, one launch (start us, length us, event | category | flops | bytes accessed | tf_op | source)
XLA Modules:
  0.0 72.1 jit_solution(6227980897991493061)
XLA Ops:
  0.0 1.5 %broadcast_in_dim.26 = bf16[8,16,1024]{2,1,0:T(8,128)(2,1)} broadcast(bf16[16,1024]{1,0:T(8,128)(2,1)} %bitcast.34), dimensions={1,2} | broadcast | bytes 294912 | tf_op jit(solution)/shard_map/broadcast_in_dim | solution.py:238
  1.5 8.5 %all-to-all-start = ((bf16[8,16,1024]{2,1,0:T(8,128)(2,1)}), bf16[8,16,1024]{2,1,0:T(8,128)(2,1)S(1)}, u32[]{:S(2)}, u32[]{:S(2)}) async-start(bf16[8,16,1024]{2,1,0:T(8,128)(2,1)} %broadcast_in_dim.26), calls=%async_computation | async-start | bytes 524288 | tf_op jit(solution)/shard_map/all_to_all | solution.py:239
  10.0 0.0 copy-start.1
  10.0 5.5 %copy.13 = bf16[1,2,512,2,1024]{4,2,3,1,0:T(8,128)(2,1)} copy(bf16[1,2,512,2,1024]{4,3,2,1,0:T(2,128)(2,1)} %param.6) | data formatting | bytes 8388608 | tf_op args[1]
  15.4 6.4 %all-to-all-done.refs_0_ = bf16[8,16,1024]{2,1,0:T(8,128)(2,1)S(1)} async-done(((bf16[8,16,1024]{2,1,0:T(8,128)(2,1)}), bf16[8,16,1024]{2,1,0:T(8,128)(2,1)S(1)}, u32[]{:S(2)}, u32[]{:S(2)}) %all-to-all-start) | async-done | bytes 262176 | tf_op jit(solution)/shard_map/all_to_all | solution.py:239
  21.8 0.0 collective-permute-start.1
  21.8 1.6 %collective-permute-start = (bf16[8,16,1024]{2,1,0:T(8,128)(2,1)S(1)}, bf16[8,16,1024]{2,1,0:T(8,128)(2,1)S(1)}, u32[]{:S(2)}, u32[]{:S(2)}) collective-permute-start(bf16[8,16,1024]{2,1,0:T(8,128)(2,1)S(1)} %all-to-all-done.refs_0_), channel_id=1, source_target_pairs={{0,64},{4,196},{64,0},{68,132},{128,192},{132,68},{192,128},{196,4... | collective-permute-start | bytes 786440 | tf_op jit(solution)/shard_map/ppermute | solution.py:242
  23.4 4.8 %collective-permute-done.refs_0_ = bf16[8,16,1024]{2,1,0:T(8,128)(2,1)S(1)} collective-permute-done((bf16[8,16,1024]{2,1,0:T(8,128)(2,1)S(1)}, bf16[8,16,1024]{2,1,0:T(8,128)(2,1)S(1)}, u32[]{:S(2)}, u32[]{:S(2)}) %collective-permute-start) | collective-permute-done | bytes 262176 | tf_op jit(solution)/shard_map/ppermute | solution.py:242
  28.2 3.0 %collective-permute-start.4 = (bf16[8,16,1024]{2,1,0:T(8,128)(2,1)S(1)}, bf16[8,16,1024]{2,1,0:T(8,128)(2,1)S(1)}, u32[]{:S(2)}, u32[]{:S(2)}) collective-permute-start(bf16[8,16,1024]{2,1,0:T(8,128)(2,1)S(1)} %collective-permute-done.refs_0_), channel_id=1, source_target_pairs={{0,192},{4,68},{64,128},{68,4},{128,64},{132,196},{192,0},{196,132... | collective-permute-start | bytes 786440 | tf_op jit(solution)/shard_map/ppermute | solution.py:244
  31.2 0.2 collective-permute-start.2
  31.4 0.0 collective-permute-done.1.refs_2_
  31.4 0.0 copy-done.1
  31.4 0.0 copy-start
  31.5 2.2 %copy-done = bf16[1,2,512,2,1024]{4,2,3,1,0:T(8,128)(2,1)S(1)} copy-done((bf16[1,2,512,2,1024]{4,2,3,1,0:T(8,128)(2,1)S(1)}, bf16[1,2,512,2,1024]{4,2,3,1,0:T(8,128)(2,1)}, u32[]{:S(2)}) %copy-start) | copy-done | bytes 4194328
  33.6 2.2 %shard_map.57.all_refs_0_ = bf16[8,16,1152]{2,1,0:T(8,128)(2,1)S(1)} custom-call(s32[1,128]{1,0:T(1,128)S(1)} %copy-done.1, bf16[8,16,1024]{2,1,0:T(8,128)(2,1)S(1)} %collective-permute-done.refs_0_, bf16[2,2,512,1024]{3,2,1,0:T(8,128)(2,1)S(1)} %bitcast.27, bf16[2,2,512,1024]{3,2,1,0:T(8,128)(2,1)S(1)} %collective-permute-done.1.refs_2_), custom_call_target="tpu_custom_call" | custom-call | flops 1073741824 | bytes 2097152 | tf_op jit(solution)/shard_map/pallas_call | solution.py:130
  35.9 0.0 collective-permute-done.4.refs_0_
  35.9 2.3 %shard_map.58 = bf16[8,16,1152]{2,1,0:T(8,128)(2,1)S(1)} custom-call(s32[1,128]{1,0:T(1,128)S(1)} %copy-done.1, bf16[8,16,1024]{2,1,0:T(8,128)(2,1)S(1)} %collective-permute-done.4.refs_0_, bf16[2,2,512,1024]{3,2,1,0:T(8,128)(2,1)S(1)} %bitcast.28, bf16[2,2,512,1024]{3,2,1,0:T(8,128)(2,1)S(1)} %collective-permute-done.1.refs_2_), custom_call_target="tpu_custom_call" | custom-call | flops 1073741824 | bytes 2097152 | tf_op jit(solution)/shard_map/pallas_call | solution.py:130
  38.2 3.1 %collective-permute-start.5 = (bf16[8,16,1152]{2,1,0:T(8,128)(2,1)S(1)}, bf16[8,16,1152]{2,1,0:T(8,128)(2,1)S(1)}, u32[]{:S(2)}, u32[]{:S(2)}) collective-permute-start(bf16[8,16,1152]{2,1,0:T(8,128)(2,1)S(1)} %shard_map.58), channel_id=1, source_target_pairs={{0,192},{4,68},{64,128},{68,4},{128,64},{132,196},{192,0},{196,132... | collective-permute-start | bytes 884744 | tf_op jit(solution)/shard_map/ppermute | solution.py:251
  41.3 0.0 collective-permute-done.2.refs_0_
  41.3 2.2 %shard_map.56 = bf16[8,16,1152]{2,1,0:T(8,128)(2,1)S(1)} custom-call(s32[1,128]{1,0:T(1,128)S(1)} %copy-done.1, bf16[8,16,1024]{2,1,0:T(8,128)(2,1)S(1)} %collective-permute-done.2.refs_0_, bf16[2,2,512,1024]{3,2,1,0:T(8,128)(2,1)S(1)} %bitcast.29, bf16[2,2,512,1024]{3,2,1,0:T(8,128)(2,1)S(1)} %collective-permute-done.1.refs_2_), custom_call_target="tpu_custom_call" | custom-call | flops 1073741824 | bytes 2097152 | tf_op jit(solution)/shard_map/pallas_call | solution.py:130
  43.5 0.4 collective-permute-start.3
  43.9 2.2 %collective-permute-done.5.all_refs_1_ = bf16[8,16,1152]{2,1,0:T(8,128)(2,1)S(1)} collective-permute-done((bf16[8,16,1152]{2,1,0:T(8,128)(2,1)S(1)}, bf16[8,16,1152]{2,1,0:T(8,128)(2,1)S(1)}, u32[]{:S(2)}, u32[]{:S(2)}) %collective-permute-start.5) | collective-permute-done | bytes 294944 | tf_op jit(solution)/shard_map/ppermute | solution.py:251
  46.2 0.5 shard_map.59
  46.7 0.3 collective-permute-start.6
  47.0 0.0 copy-start.2
  47.0 2.2 %shard_map.55.all_refs_0_ = bf16[8,16,1152]{2,1,0:T(8,128)(2,1)S(1)} custom-call(s32[1,128]{1,0:T(1,128)S(1)} %copy-done.1, bf16[8,16,1024]{2,1,0:T(8,128)(2,1)S(1)} %all-to-all-done.refs_0_, bf16[2,2,512,1024]{3,2,1,0:T(8,128)(2,1)S(1)} %bitcast.30, bf16[2,2,512,1024]{3,2,1,0:T(8,128)(2,1)S(1)} %collective-permute-done.1.refs_2_), custom_call_target="tpu_custom_call" | custom-call | flops 1073741824 | bytes 2097152 | tf_op jit(solution)/shard_map/pallas_call | solution.py:130
  49.2 4.3 %collective-permute-done.3.all_refs_1_ = bf16[8,16,1152]{2,1,0:T(8,128)(2,1)S(1)} collective-permute-done((bf16[8,16,1152]{2,1,0:T(8,128)(2,1)S(1)}, bf16[8,16,1152]{2,1,0:T(8,128)(2,1)S(1)}, u32[]{:S(2)}, u32[]{:S(2)}) %collective-permute-start.3) | collective-permute-done | bytes 294944 | tf_op jit(solution)/shard_map/ppermute | solution.py:252
  53.6 0.1 collective-permute-done.6.all_refs_2_
  53.7 1.4 %shard_map.60 = bf16[8,16,1152]{2,1,0:T(8,128)(2,1)} custom-call(bf16[8,16,1152]{2,1,0:T(8,128)(2,1)S(1)} %shard_map.55.all_refs_0_, bf16[8,16,1152]{2,1,0:T(8,128)(2,1)S(1)} %collective-permute-done.3.all_refs_1_, bf16[8,16,1152]{2,1,0:T(8,128)(2,1)S(1)} %collective-permute-done.6.all_refs_2_), custom_call_target="tpu_custom_call" | custom-call | tf_op jit(solution)/shard_map/pallas_call | solution.py:180
  55.0 0.0 copy-done.2
  55.1 0.0 copy-start.3
  55.1 0.0 copy-start.4
  55.1 0.5 copy.14
  55.5 0.3 copy-done.3
  55.8 0.0 copy-done.4
  55.8 0.1 iota_compare_fusion
  55.9 3.4 %all-to-all-start.1 = ((bf16[8,16,1152]{2,1,0:T(8,128)(2,1)}), bf16[8,16,1152]{2,1,0:T(8,128)(2,1)S(1)}, u32[]{:S(2)}, u32[]{:S(2)}) async-start(bf16[8,16,1152]{2,1,0:T(8,128)(2,1)} %shard_map.60), calls=%async_computation.1 | async-start | bytes 589824 | tf_op jit(solution)/shard_map/all_to_all | solution.py:260
  59.3 0.5 fusion.7
  59.8 0.2 fusion.1
  60.0 0.3 convolution_divide_fusion
  60.3 10.8 %all-to-all-done.1.p_ref = bf16[8,16,1152]{2,1,0:T(8,128)(2,1)S(1)} async-done(((bf16[8,16,1152]{2,1,0:T(8,128)(2,1)}), bf16[8,16,1152]{2,1,0:T(8,128)(2,1)S(1)}, u32[]{:S(2)}, u32[]{:S(2)}) %all-to-all-start.1) | async-done | bytes 294944 | tf_op jit(solution)/shard_map/all_to_all | solution.py:260
  71.2 1.0 %shard_map.61 = bf16[16,1024]{1,0:T(8,128)(2,1)} custom-call(bf16[8,16,1152]{2,1,0:T(8,128)(2,1)S(1)} %all-to-all-done.1.p_ref, f32[16,1024]{1,0:T(8,128)S(1)} %bitcast.31, f32[16,128]{1,0:T(8,128)S(1)} %pad.4.sl_ref), custom_call_target="tpu_custom_call" | custom-call | tf_op jit(solution)/shard_map/pallas_call | solution.py:202
  (4 shorter events, 0.0 us)
Async XLA Ops:
  1.5 20.3 %all-to-all-start = ((bf16[8,16,1024]{2,1,0:T(8,128)(2,1)}), bf16[8,16,1024]{2,1,0:T(8,128)(2,1)S(1)}, u32[]{:S(2)}, u32[]{:S(2)}) async-start(bf16[8,16,1024]{2,1,0:T(8,128)(2,1)} %broadcast_in_dim.26), calls=%async_computation | async-start | bytes 524288 | tf_op jit(solution)/shard_map/all_to_all | solution.py:239
  10.0 21.5 %copy-start.1 = (s32[1,128]{1,0:T(1,128)S(1)}, s32[1,128]{1,0:T(1,128)}, u32[]{:S(2)}) copy-start(s32[1,128]{1,0:T(1,128)} %ids_ref.7) | copy-start | bytes 1540
  21.8 9.6 %collective-permute-start.1 = (bf16[2,2,512,1024]{3,2,1,0:T(8,128)(2,1)}, bf16[2,2,512,1024]{3,2,1,0:T(8,128)(2,1)S(1)}, u32[]{:S(2)}, u32[]{:S(2)}) collective-permute-start(bf16[2,2,512,1024]{3,2,1,0:T(8,128)(2,1)} %bitcast.26), channel_id=1, source_target_pairs={{0,4},{4,0},{1,5},{5,1},{2,6},{6,2},{3,7},{7,3},{8,12},{12,8},{9,1... | collective-permute-start | bytes 12582920 | tf_op jit(solution)/shard_map/ppermute | solution.py:241
  21.8 6.4 %collective-permute-start = (bf16[8,16,1024]{2,1,0:T(8,128)(2,1)S(1)}, bf16[8,16,1024]{2,1,0:T(8,128)(2,1)S(1)}, u32[]{:S(2)}, u32[]{:S(2)}) collective-permute-start(bf16[8,16,1024]{2,1,0:T(8,128)(2,1)S(1)} %all-to-all-done.refs_0_), channel_id=1, source_target_pairs={{0,64},{4,196},{64,0},{68,132},{128,192},{132,68},{192,128},{196,4... | collective-permute-start | bytes 786440 | tf_op jit(solution)/shard_map/ppermute | solution.py:242
  28.2 7.7 %collective-permute-start.4 = (bf16[8,16,1024]{2,1,0:T(8,128)(2,1)S(1)}, bf16[8,16,1024]{2,1,0:T(8,128)(2,1)S(1)}, u32[]{:S(2)}, u32[]{:S(2)}) collective-permute-start(bf16[8,16,1024]{2,1,0:T(8,128)(2,1)S(1)} %collective-permute-done.refs_0_), channel_id=1, source_target_pairs={{0,192},{4,68},{64,128},{68,4},{128,64},{132,196},{192,0},{196,132... | collective-permute-start | bytes 786440 | tf_op jit(solution)/shard_map/ppermute | solution.py:244
  31.2 10.0 %collective-permute-start.2 = (bf16[8,16,1024]{2,1,0:T(8,128)(2,1)S(1)}, bf16[8,16,1024]{2,1,0:T(8,128)(2,1)S(1)}, u32[]{:S(2)}, u32[]{:S(2)}) collective-permute-start(bf16[8,16,1024]{2,1,0:T(8,128)(2,1)S(1)} %all-to-all-done.refs_0_), channel_id=1, source_target_pairs={{0,192},{4,68},{64,128},{68,4},{128,64},{132,196},{192,0},{196,132... | collective-permute-start | bytes 786440 | tf_op jit(solution)/shard_map/ppermute | solution.py:245
  31.4 2.2 %copy-start = (bf16[1,2,512,2,1024]{4,2,3,1,0:T(8,128)(2,1)S(1)}, bf16[1,2,512,2,1024]{4,2,3,1,0:T(8,128)(2,1)}, u32[]{:S(2)}) copy-start(bf16[1,2,512,2,1024]{4,2,3,1,0:T(8,128)(2,1)} %copy.13) | copy-start | bytes 12582916
  38.2 8.0 %collective-permute-start.5 = (bf16[8,16,1152]{2,1,0:T(8,128)(2,1)S(1)}, bf16[8,16,1152]{2,1,0:T(8,128)(2,1)S(1)}, u32[]{:S(2)}, u32[]{:S(2)}) collective-permute-start(bf16[8,16,1152]{2,1,0:T(8,128)(2,1)S(1)} %shard_map.58), channel_id=1, source_target_pairs={{0,192},{4,68},{64,128},{68,4},{128,64},{132,196},{192,0},{196,132... | collective-permute-start | bytes 884744 | tf_op jit(solution)/shard_map/ppermute | solution.py:251
  43.5 10.1 %collective-permute-start.3 = (bf16[8,16,1152]{2,1,0:T(8,128)(2,1)S(1)}, bf16[8,16,1152]{2,1,0:T(8,128)(2,1)S(1)}, u32[]{:S(2)}, u32[]{:S(2)}) collective-permute-start(bf16[8,16,1152]{2,1,0:T(8,128)(2,1)S(1)} %shard_map.56), channel_id=1, source_target_pairs={{0,192},{4,68},{64,128},{68,4},{128,64},{132,196},{192,0},{196,132... | collective-permute-start | bytes 884744 | tf_op jit(solution)/shard_map/ppermute | solution.py:252
  46.7 7.0 %collective-permute-start.6 = (bf16[8,16,1152]{2,1,0:T(8,128)(2,1)S(1)}, bf16[8,16,1152]{2,1,0:T(8,128)(2,1)S(1)}, u32[]{:S(2)}, u32[]{:S(2)}) collective-permute-start(bf16[8,16,1152]{2,1,0:T(8,128)(2,1)S(1)} %shard_map.59), channel_id=1, source_target_pairs={{0,64},{4,196},{64,0},{68,132},{128,192},{132,68},{192,128},{196,4... | collective-permute-start | bytes 884744 | tf_op jit(solution)/shard_map/ppermute | solution.py:254
  47.0 8.1 %copy-start.2 = (bf16[1,16,256,2,128]{4,3,2,1,0:T(2,128)(2,1)S(1)}, bf16[1,16,256,2,128]{4,3,2,1,0:T(2,128)(2,1)}, u32[]{:S(2)}) copy-start(bf16[1,16,256,2,128]{4,3,2,1,0:T(2,128)(2,1)} %param.7) | copy-start | bytes 6291460
  55.1 0.8 %copy-start.3 = (bf16[1,16,1024]{2,1,0:T(8,128)(2,1)S(1)}, bf16[1,16,1024]{2,1,0:T(8,128)(2,1)}, u32[]{:S(2)}) copy-start(bf16[1,16,1024]{2,1,0:T(8,128)(2,1)} %param.5) | copy-start | bytes 98308
  55.1 0.8 %copy-start.4 = (s32[1,16]{1,0:T(1,128)S(1)}, s32[1,16]{1,0:T(1,128)}, u32[]{:S(2)}) copy-start(s32[1,16]{1,0:T(1,128)} %param.8) | copy-start | bytes 196
  55.9 15.3 %all-to-all-start.1 = ((bf16[8,16,1152]{2,1,0:T(8,128)(2,1)}), bf16[8,16,1152]{2,1,0:T(8,128)(2,1)S(1)}, u32[]{:S(2)}, u32[]{:S(2)}) async-start(bf16[8,16,1152]{2,1,0:T(8,128)(2,1)} %shard_map.60), calls=%async_computation.1 | async-start | bytes 589824 | tf_op jit(solution)/shard_map/all_to_all | solution.py:260

commit v8 on v7

--- a/solution.py
+++ b/solution.py
@@ -240,7 +240,8 @@
     q0, own = lax.optimization_barrier((q0, own))
     par = lax.ppermute(own, "core", [(0, 1), (1, 0)])
     first = lax.ppermute(q0, ("y", "core"), _pairs(1))
-    first, q0 = lax.optimization_barrier((first, q0))
+    suffix_o, suffix_l2 = _suffix(q, suffix_kv[0], suffix_len[0])
+    first, q0, suffix_o, suffix_l2 = lax.optimization_barrier((first, q0, suffix_o, suffix_l2))
     third = lax.ppermute(first, ("y", "core"), _pairs(2))
     second = lax.ppermute(q0, ("y", "core"), _pairs(2))
 
@@ -253,10 +254,6 @@
     merged = _merge([part_first, back_third])
     back_first = lax.ppermute(merged, ("y", "core"), _pairs(1))
     merged = _merge([part(0, q0), back_second, back_first])
-    merged, q, suffix_kv, suffix_len = lax.optimization_barrier(
-        (merged, q, suffix_kv, suffix_len)
-    )
-    suffix_o, suffix_l2 = _suffix(q, suffix_kv[0], suffix_len[0])
     got = lax.all_to_all(merged, ("zh", "zl"), 0, 0, tiled=True)
     return _final(got, suffix_o, suffix_l2)[None]
 

time: 72.6 us -> 71.1 us (0.979)
  blocking collectives: 0 us -> 13.8 us
  waiting for transfers between devices: 28.7 us -> 19.2 us
  starting transfers between devices: 20.5 us -> 17.3 us
  local copies, waits for them, and re-layouts: 9.95 us -> 7.86 us
    all_to_all x0 -> x1, blocking collectives: none -> 13.8 us  [_shards(): got = lax.all_to_all(merged, ('zh', 'zl'), 0, 0, tiled=True)]
    all_to_all x1 -> x0, waiting for transfers between devices: 10.8 us -> none  [_shards(): got = lax.all_to_all(merged, ('zh', 'zl'), 0, 0, tiled=True)]
    all_to_all x1 -> x0, starting transfers between devices: 3.42 us -> none  [_shards(): got = lax.all_to_all(merged, ('zh', 'zl'), 0, 0, tiled=True)]
    ppermute x1, waiting for transfers between devices: 0.01 us -> 2.07 us  [_shards(): third = lax.ppermute(first, ('y', 'core'), _pairs(2))]
    unnamed x13 -> x14, local copies, waits for them, and re-layouts: 7.97 us -> 6.37 us
  transfers between devices with their start and end apart: 9 -> 8, of which waited for: 6 -> 6; matrix products, arithmetic and copies ran while one was open for 9% -> 10% of each run, Pallas kernels for 13% -> 13%
where the time goes in v8:
time: 71.1 us; the launch traced here: 70.4 us
  waiting for transfers between devices  19.2 us (27%)
  starting transfers between devices  17.3 us (24%)
  blocking collectives  13.8 us (19%)
  Pallas kernels  11.1 us (16%)
  local copies, waits for them, and re-layouts  7.86 us (11%)
  matrix products  0.75 us (1%)
    all_to_all x1, blocking collectives, _shards(): got = lax.all_to_all(merged, ('zh', 'zl'), 0, 0, tiled=True)  13.8 us
    pallas_call x4, Pallas kernels, _prompt(): pl.pallas_call(functools.partial(_prompt_kernel, wanted), out_shape=[jax....  8.97 us
    all_to_all x1, starting transfers between devices, _shards(): q0 = lax.all_to_all(spread, ('zh', 'zl'), 0, 0, tiled=True)  8.47 us
    unnamed x14, local copies, waits for them, and re-layouts  6.37 us
    all_to_all x1, waiting for transfers between devices, _shards(): q0 = lax.all_to_all(spread, ('zh', 'zl'), 0, 0, tiled=True)  6.27 us
    ppermute x1, waiting for transfers between devices, _shards(): first = lax.ppermute(q0, ('y', 'core'), _pairs(1))  4.43 us
    ppermute x1, waiting for transfers between devices, _shards(): back_second = lax.ppermute(part(2, second), ('y', 'core'), _pairs(2))  3.83 us
    ppermute x1, starting transfers between devices, _shards(): back_third = lax.ppermute(part(3, third), ('y', 'core'), _pairs(2))  3.1 us
  transfers between devices with their start and end apart: 8, of which 6 were waited for; matrix products, arithmetic and copies ran while one was open for 10% of the time, Pallas kernels for 13%

profile of v8, /device:TPU:2, one launch (start us, length us, event | category | flops | bytes accessed | tf_op | source)
XLA Modules:
  0.0 70.4 jit_solution(8385806281428154804)
XLA Ops:
  0.0 1.5 %broadcast_in_dim.26 = bf16[8,16,1024]{2,1,0:T(8,128)(2,1)} broadcast(bf16[16,1024]{1,0:T(8,128)(2,1)} %bitcast.35), dimensions={1,2} | broadcast | bytes 294912 | tf_op jit(solution)/shard_map/broadcast_in_dim | solution.py:238
  1.5 8.5 %all-to-all-start = ((bf16[8,16,1024]{2,1,0:T(8,128)(2,1)}), bf16[8,16,1024]{2,1,0:T(8,128)(2,1)S(1)}, u32[]{:S(2)}, u32[]{:S(2)}) async-start(bf16[8,16,1024]{2,1,0:T(8,128)(2,1)} %broadcast_in_dim.26), calls=%async_computation | async-start | bytes 524288 | tf_op jit(solution)/shard_map/all_to_all | solution.py:239
  9.9 0.0 copy-start.2
  9.9 5.6 %copy.13 = bf16[1,2,512,2,1024]{4,2,3,1,0:T(8,128)(2,1)} copy(bf16[1,2,512,2,1024]{4,3,2,1,0:T(2,128)(2,1)} %param.6) | data formatting | bytes 8388608 | tf_op args[1]
  15.6 6.3 %all-to-all-done.refs_0_ = bf16[8,16,1024]{2,1,0:T(8,128)(2,1)S(1)} async-done(((bf16[8,16,1024]{2,1,0:T(8,128)(2,1)}), bf16[8,16,1024]{2,1,0:T(8,128)(2,1)S(1)}, u32[]{:S(2)}, u32[]{:S(2)}) %all-to-all-start) | async-done | bytes 262176 | tf_op jit(solution)/shard_map/all_to_all | solution.py:239
  21.8 0.0 copy-start.3
  21.8 0.0 copy-start.4
  21.8 0.0 collective-permute-start.1
  21.8 0.0 copy-done.2
  21.8 0.0 copy-start
  21.8 0.5 copy.14
  22.3 0.0 copy-start.1
  22.3 0.2 copy-done.3
  22.6 0.0 copy-done.4
  22.6 0.1 iota_compare_fusion
  22.7 0.5 fusion.7
  23.1 0.2 fusion.1
  23.3 1.7 %collective-permute-start = (bf16[8,16,1024]{2,1,0:T(8,128)(2,1)S(1)}, bf16[8,16,1024]{2,1,0:T(8,128)(2,1)S(1)}, u32[]{:S(2)}, u32[]{:S(2)}) collective-permute-start(bf16[8,16,1024]{2,1,0:T(8,128)(2,1)S(1)} %all-to-all-done.refs_0_), channel_id=1, source_target_pairs={{0,64},{4,196},{64,0},{68,132},{128,192},{132,68},{192,128},{196,4... | collective-permute-start | bytes 786440 | tf_op jit(solution)/shard_map/ppermute | solution.py:242
  25.0 0.3 convolution_divide_fusion
  25.3 4.4 %collective-permute-done.refs_0_ = bf16[8,16,1024]{2,1,0:T(8,128)(2,1)S(1)} collective-permute-done((bf16[8,16,1024]{2,1,0:T(8,128)(2,1)S(1)}, bf16[8,16,1024]{2,1,0:T(8,128)(2,1)S(1)}, u32[]{:S(2)}, u32[]{:S(2)}) %collective-permute-start) | collective-permute-done | bytes 262176 | tf_op jit(solution)/shard_map/ppermute | solution.py:242
  29.8 3.0 %collective-permute-start.4 = (bf16[8,16,1024]{2,1,0:T(8,128)(2,1)S(1)}, bf16[8,16,1024]{2,1,0:T(8,128)(2,1)S(1)}, u32[]{:S(2)}, u32[]{:S(2)}) collective-permute-start(bf16[8,16,1024]{2,1,0:T(8,128)(2,1)S(1)} %collective-permute-done.refs_0_), channel_id=1, source_target_pairs={{0,192},{4,68},{64,128},{68,4},{128,64},{132,196},{192,0},{196,132... | collective-permute-start | bytes 786440 | tf_op jit(solution)/shard_map/ppermute | solution.py:245
  32.8 0.2 collective-permute-start.2
  33.0 0.0 collective-permute-done.1.refs_2_
  33.0 0.0 copy-done
  33.0 0.0 copy-done.1
  33.0 2.3 %shard_map.57.all_refs_0_ = bf16[8,16,1152]{2,1,0:T(8,128)(2,1)S(1)} custom-call(s32[1,128]{1,0:T(1,128)S(1)} %copy-done.1, bf16[8,16,1024]{2,1,0:T(8,128)(2,1)S(1)} %collective-permute-done.refs_0_, bf16[2,2,512,1024]{3,2,1,0:T(8,128)(2,1)S(1)} %bitcast.28, bf16[2,2,512,1024]{3,2,1,0:T(8,128)(2,1)S(1)} %collective-permute-done.1.refs_2_), custom_call_target="tpu_custom_call" | custom-call | flops 1073741824 | bytes 2097152 | tf_op jit(solution)/shard_map/pallas_call | solution.py:130
  35.3 2.1 %collective-permute-done.4.refs_0_ = bf16[8,16,1024]{2,1,0:T(8,128)(2,1)S(1)} collective-permute-done((bf16[8,16,1024]{2,1,0:T(8,128)(2,1)S(1)}, bf16[8,16,1024]{2,1,0:T(8,128)(2,1)S(1)}, u32[]{:S(2)}, u32[]{:S(2)}) %collective-permute-start.4) | collective-permute-done | bytes 262176 | tf_op jit(solution)/shard_map/ppermute | solution.py:245
  37.4 2.2 %shard_map.58 = bf16[8,16,1152]{2,1,0:T(8,128)(2,1)S(1)} custom-call(s32[1,128]{1,0:T(1,128)S(1)} %copy-done.1, bf16[8,16,1024]{2,1,0:T(8,128)(2,1)S(1)} %collective-permute-done.4.refs_0_, bf16[2,2,512,1024]{3,2,1,0:T(8,128)(2,1)S(1)} %bitcast.29, bf16[2,2,512,1024]{3,2,1,0:T(8,128)(2,1)S(1)} %collective-permute-done.1.refs_2_), custom_call_target="tpu_custom_call" | custom-call | flops 1073741824 | bytes 2097152 | tf_op jit(solution)/shard_map/pallas_call | solution.py:130
  39.6 3.1 %collective-permute-start.5 = (bf16[8,16,1152]{2,1,0:T(8,128)(2,1)S(1)}, bf16[8,16,1152]{2,1,0:T(8,128)(2,1)S(1)}, u32[]{:S(2)}, u32[]{:S(2)}) collective-permute-start(bf16[8,16,1152]{2,1,0:T(8,128)(2,1)S(1)} %shard_map.58), channel_id=1, source_target_pairs={{0,192},{4,68},{64,128},{68,4},{128,64},{132,196},{192,0},{196,132... | collective-permute-start | bytes 884744 | tf_op jit(solution)/shard_map/ppermute | solution.py:252
  42.7 0.0 collective-permute-done.2.refs_0_
  42.7 2.2 %shard_map.56 = bf16[8,16,1152]{2,1,0:T(8,128)(2,1)S(1)} custom-call(s32[1,128]{1,0:T(1,128)S(1)} %copy-done.1, bf16[8,16,1024]{2,1,0:T(8,128)(2,1)S(1)} %collective-permute-done.2.refs_0_, bf16[2,2,512,1024]{3,2,1,0:T(8,128)(2,1)S(1)} %bitcast.30, bf16[2,2,512,1024]{3,2,1,0:T(8,128)(2,1)S(1)} %collective-permute-done.1.refs_2_), custom_call_target="tpu_custom_call" | custom-call | flops 1073741824 | bytes 2097152 | tf_op jit(solution)/shard_map/pallas_call | solution.py:130
  44.9 0.8 %collective-permute-start.3 = (bf16[8,16,1152]{2,1,0:T(8,128)(2,1)S(1)}, bf16[8,16,1152]{2,1,0:T(8,128)(2,1)S(1)}, u32[]{:S(2)}, u32[]{:S(2)}) collective-permute-start(bf16[8,16,1152]{2,1,0:T(8,128)(2,1)S(1)} %shard_map.56), channel_id=1, source_target_pairs={{0,192},{4,68},{64,128},{68,4},{128,64},{132,196},{192,0},{196,132... | collective-permute-start | bytes 884744 | tf_op jit(solution)/shard_map/ppermute | solution.py:253
  45.7 1.9 %collective-permute-done.5.all_refs_1_ = bf16[8,16,1152]{2,1,0:T(8,128)(2,1)S(1)} collective-permute-done((bf16[8,16,1152]{2,1,0:T(8,128)(2,1)S(1)}, bf16[8,16,1152]{2,1,0:T(8,128)(2,1)S(1)}, u32[]{:S(2)}, u32[]{:S(2)}) %collective-permute-start.5) | collective-permute-done | bytes 294944 | tf_op jit(solution)/shard_map/ppermute | solution.py:252
  47.6 0.5 shard_map.59
  48.1 0.1 collective-permute-start.6
  48.2 2.3 %shard_map.55.all_refs_0_ = bf16[8,16,1152]{2,1,0:T(8,128)(2,1)S(1)} custom-call(s32[1,128]{1,0:T(1,128)S(1)} %copy-done.1, bf16[8,16,1024]{2,1,0:T(8,128)(2,1)S(1)} %all-to-all-done.refs_0_, bf16[2,2,512,1024]{3,2,1,0:T(8,128)(2,1)S(1)} %bitcast.31, bf16[2,2,512,1024]{3,2,1,0:T(8,128)(2,1)S(1)} %collective-permute-done.1.refs_2_), custom_call_target="tpu_custom_call" | custom-call | flops 1073741824 | bytes 2097152 | tf_op jit(solution)/shard_map/pallas_call | solution.py:130
  50.5 3.8 %collective-permute-done.3.all_refs_1_ = bf16[8,16,1152]{2,1,0:T(8,128)(2,1)S(1)} collective-permute-done((bf16[8,16,1152]{2,1,0:T(8,128)(2,1)S(1)}, bf16[8,16,1152]{2,1,0:T(8,128)(2,1)S(1)}, u32[]{:S(2)}, u32[]{:S(2)}) %collective-permute-start.3) | collective-permute-done | bytes 294944 | tf_op jit(solution)/shard_map/ppermute | solution.py:253
  54.3 0.6 collective-permute-done.6.all_refs_2_
  54.9 0.7 shard_map.60
  55.6 13.8 %all_to_all.10.p_ref = bf16[8,16,1152]{2,1,0:T(8,128)(2,1)S(1)} all-to-all(bf16[8,16,1152]{2,1,0:T(8,128)(2,1)S(1)} %shard_map.60), channel_id=1, replica_groups=mesh['y'=4,'zh'=2,'zl'=4,'core'=2,'grp'=4] {'zh','zl'}, dimensions={0} | all-to-all | bytes 589824 | tf_op jit(solution)/shard_map/all_to_all | solution.py:257
  69.4 1.0 %shard_map.61 = bf16[16,1024]{1,0:T(8,128)(2,1)} custom-call(bf16[8,16,1152]{2,1,0:T(8,128)(2,1)S(1)} %all_to_all.10.p_ref, f32[16,1024]{1,0:T(8,128)S(1)} %bitcast.32, f32[16,128]{1,0:T(8,128)S(1)} %pad.4.sl_ref), custom_call_target="tpu_custom_call" | custom-call | tf_op jit(solution)/shard_map/pallas_call | solution.py:202
  (4 shorter events, 0.0 us)
Async XLA Ops:
  1.5 20.3 %all-to-all-start = ((bf16[8,16,1024]{2,1,0:T(8,128)(2,1)}), bf16[8,16,1024]{2,1,0:T(8,128)(2,1)S(1)}, u32[]{:S(2)}, u32[]{:S(2)}) async-start(bf16[8,16,1024]{2,1,0:T(8,128)(2,1)} %broadcast_in_dim.26), calls=%async_computation | async-start | bytes 524288 | tf_op jit(solution)/shard_map/all_to_all | solution.py:239
  9.9 11.9 %copy-start.2 = (bf16[1,16,256,2,128]{4,3,2,1,0:T(2,128)(2,1)S(1)}, bf16[1,16,256,2,128]{4,3,2,1,0:T(2,128)(2,1)}, u32[]{:S(2)}) copy-start(bf16[1,16,256,2,128]{4,3,2,1,0:T(2,128)(2,1)} %param.7) | copy-start | bytes 6291460
  21.8 0.8 %copy-start.3 = (bf16[1,16,1024]{2,1,0:T(8,128)(2,1)S(1)}, bf16[1,16,1024]{2,1,0:T(8,128)(2,1)}, u32[]{:S(2)}) copy-start(bf16[1,16,1024]{2,1,0:T(8,128)(2,1)} %param.5) | copy-start | bytes 98308
  21.8 0.8 %copy-start.4 = (s32[1,16]{1,0:T(1,128)S(1)}, s32[1,16]{1,0:T(1,128)}, u32[]{:S(2)}) copy-start(s32[1,16]{1,0:T(1,128)} %param.8) | copy-start | bytes 196
  21.8 11.2 %collective-permute-start.1 = (bf16[2,2,512,1024]{3,2,1,0:T(8,128)(2,1)}, bf16[2,2,512,1024]{3,2,1,0:T(8,128)(2,1)S(1)}, u32[]{:S(2)}, u32[]{:S(2)}) collective-permute-start(bf16[2,2,512,1024]{3,2,1,0:T(8,128)(2,1)} %bitcast.27), channel_id=1, source_target_pairs={{0,4},{4,0},{1,5},{5,1},{2,6},{6,2},{3,7},{7,3},{8,12},{12,8},{9,1... | collective-permute-start | bytes 12582920 | tf_op jit(solution)/shard_map/ppermute | solution.py:241
  21.8 11.2 %copy-start = (bf16[1,2,512,2,1024]{4,2,3,1,0:T(8,128)(2,1)S(1)}, bf16[1,2,512,2,1024]{4,2,3,1,0:T(8,128)(2,1)}, u32[]{:S(2)}) copy-start(bf16[1,2,512,2,1024]{4,2,3,1,0:T(8,128)(2,1)} %copy.13) | copy-start | bytes 12582916
  22.3 10.7 %copy-start.1 = (s32[1,128]{1,0:T(1,128)S(1)}, s32[1,128]{1,0:T(1,128)}, u32[]{:S(2)}) copy-start(s32[1,128]{1,0:T(1,128)} %ids_ref.7) | copy-start | bytes 1540
  23.3 6.5 %collective-permute-start = (bf16[8,16,1024]{2,1,0:T(8,128)(2,1)S(1)}, bf16[8,16,1024]{2,1,0:T(8,128)(2,1)S(1)}, u32[]{:S(2)}, u32[]{:S(2)}) collective-permute-start(bf16[8,16,1024]{2,1,0:T(8,128)(2,1)S(1)} %all-to-all-done.refs_0_), channel_id=1, source_target_pairs={{0,64},{4,196},{64,0},{68,132},{128,192},{132,68},{192,128},{196,4... | collective-permute-start | bytes 786440 | tf_op jit(solution)/shard_map/ppermute | solution.py:242
  29.8 7.6 %collective-permute-start.4 = (bf16[8,16,1024]{2,1,0:T(8,128)(2,1)S(1)}, bf16[8,16,1024]{2,1,0:T(8,128)(2,1)S(1)}, u32[]{:S(2)}, u32[]{:S(2)}) collective-permute-start(bf16[8,16,1024]{2,1,0:T(8,128)(2,1)S(1)} %collective-permute-done.refs_0_), channel_id=1, source_target_pairs={{0,192},{4,68},{64,128},{68,4},{128,64},{132,196},{192,0},{196,132... | collective-permute-start | bytes 786440 | tf_op jit(solution)/shard_map/ppermute | solution.py:245
  32.8 9.9 %collective-permute-start.2 = (bf16[8,16,1024]{2,1,0:T(8,128)(2,1)S(1)}, bf16[8,16,1024]{2,1,0:T(8,128)(2,1)S(1)}, u32[]{:S(2)}, u32[]{:S(2)}) collective-permute-start(bf16[8,16,1024]{2,1,0:T(8,128)(2,1)S(1)} %all-to-all-done.refs_0_), channel_id=1, source_target_pairs={{0,192},{4,68},{64,128},{68,4},{128,64},{132,196},{192,0},{196,132... | collective-permute-start | bytes 786440 | tf_op jit(solution)/shard_map/ppermute | solution.py:246
  39.6 8.0 %collective-permute-start.5 = (bf16[8,16,1152]{2,1,0:T(8,128)(2,1)S(1)}, bf16[8,16,1152]{2,1,0:T(8,128)(2,1)S(1)}, u32[]{:S(2)}, u32[]{:S(2)}) collective-permute-start(bf16[8,16,1152]{2,1,0:T(8,128)(2,1)S(1)} %shard_map.58), channel_id=1, source_target_pairs={{0,192},{4,68},{64,128},{68,4},{128,64},{132,196},{192,0},{196,132... | collective-permute-start | bytes 884744 | tf_op jit(solution)/shard_map/ppermute | solution.py:252
  44.9 9.4 %collective-permute-start.3 = (bf16[8,16,1152]{2,1,0:T(8,128)(2,1)S(1)}, bf16[8,16,1152]{2,1,0:T(8,128)(2,1)S(1)}, u32[]{:S(2)}, u32[]{:S(2)}) collective-permute-start(bf16[8,16,1152]{2,1,0:T(8,128)(2,1)S(1)} %shard_map.56), channel_id=1, source_target_pairs={{0,192},{4,68},{64,128},{68,4},{128,64},{132,196},{192,0},{196,132... | collective-permute-start | bytes 884744 | tf_op jit(solution)/shard_map/ppermute | solution.py:253
  48.1 6.8 %collective-permute-start.6 = (bf16[8,16,1152]{2,1,0:T(8,128)(2,1)S(1)}, bf16[8,16,1152]{2,1,0:T(8,128)(2,1)S(1)}, u32[]{:S(2)}, u32[]{:S(2)}) collective-permute-start(bf16[8,16,1152]{2,1,0:T(8,128)(2,1)S(1)} %shard_map.59), channel_id=1, source_target_pairs={{0,64},{4,196},{64,0},{68,132},{128,192},{132,68},{192,128},{196,4... | collective-permute-start | bytes 884744 | tf_op jit(solution)/shard_map/ppermute | solution.py:255

commit v9 on v8

--- a/solution.py
+++ b/solution.py
@@ -237,11 +237,11 @@
     n_z = lax.axis_size("zh") * lax.axis_size("zl")
     spread = jnp.broadcast_to(q[None], (n_z, *q.shape))
     q0 = lax.all_to_all(spread, ("zh", "zl"), 0, 0, tiled=True)
-    q0, own = lax.optimization_barrier((q0, own))
+    suffix_o, suffix_l2 = _suffix(q, suffix_kv[0], suffix_len[0])
+    q0, own, suffix_o, suffix_l2 = lax.optimization_barrier((q0, own, suffix_o, suffix_l2))
     par = lax.ppermute(own, "core", [(0, 1), (1, 0)])
     first = lax.ppermute(q0, ("y", "core"), _pairs(1))
-    suffix_o, suffix_l2 = _suffix(q, suffix_kv[0], suffix_len[0])
-    first, q0, suffix_o, suffix_l2 = lax.optimization_barrier((first, q0, suffix_o, suffix_l2))
+    first, q0 = lax.optimization_barrier((first, q0))
     third = lax.ppermute(first, ("y", "core"), _pairs(2))
     second = lax.ppermute(q0, ("y", "core"), _pairs(2))
 

time: 71.1 us -> 69.8 us (0.982)
  waiting for transfers between devices: 19.2 us -> 16.5 us
  local copies, waits for them, and re-layouts: 7.86 us -> 9.22 us
    ppermute x1, waiting for transfers between devices: 2.07 us -> 0.01 us  [_shards(): third = lax.ppermute(first, ('y', 'core'), _pairs(2))]
    unnamed x14, local copies, waits for them, and re-layouts: 6.37 us -> 7.74 us
    all_to_all x1, waiting for transfers between devices: 6.27 us -> 5.23 us  [_shards(): q0 = lax.all_to_all(spread, ('zh', 'zl'), 0, 0, tiled=True)]
  transfers between devices with their start and end apart: 8 -> 8, of which waited for: 6 -> 5; matrix products, arithmetic and copies ran while one was open for 10% -> 9% of each run, Pallas kernels for 13% -> 14%
where the time goes in v9:
time: 69.8 us; the launch traced here: 69.1 us
  starting transfers between devices  17.2 us (25%)
  waiting for transfers between devices  16.5 us (24%)
  blocking collectives  13.9 us (20%)
  Pallas kernels  11.1 us (16%)
  local copies, waits for them, and re-layouts  9.22 us (13%)
  matrix products  0.75 us (1%)
    all_to_all x1, blocking collectives, _shards(): got = lax.all_to_all(merged, ('zh', 'zl'), 0, 0, tiled=True)  13.9 us
    pallas_call x4, Pallas kernels, _prompt(): pl.pallas_call(functools.partial(_prompt_kernel, wanted), out_shape=[jax....  8.97 us
    all_to_all x1, starting transfers between devices, _shards(): q0 = lax.all_to_all(spread, ('zh', 'zl'), 0, 0, tiled=True)  8.6 us
    unnamed x14, local copies, waits for them, and re-layouts  7.74 us
    all_to_all x1, waiting for transfers between devices, _shards(): q0 = lax.all_to_all(spread, ('zh', 'zl'), 0, 0, tiled=True)  5.23 us
    ppermute x1, waiting for transfers between devices, _shards(): first = lax.ppermute(q0, ('y', 'core'), _pairs(1))  4.8 us
    ppermute x1, waiting for transfers between devices, _shards(): back_second = lax.ppermute(part(2, second), ('y', 'core'), _pairs(2))  4.35 us
    ppermute x1, starting transfers between devices, _shards(): back_third = lax.ppermute(part(3, third), ('y', 'core'), _pairs(2))  3.1 us
  transfers between devices with their start and end apart: 8, of which 5 were waited for; matrix products, arithmetic and copies ran while one was open for 9% of the time, Pallas kernels for 14%

profile of v9, /device:TPU:2, one launch (start us, length us, event | category | flops | bytes accessed | tf_op | source)
XLA Modules:
  0.0 69.1 jit_solution(8840018407898110687)
XLA Ops:
  0.0 1.5 %broadcast_in_dim.26 = bf16[8,16,1024]{2,1,0:T(8,128)(2,1)} broadcast(bf16[16,1024]{1,0:T(8,128)(2,1)} %bitcast.35), dimensions={1,2} | broadcast | bytes 294912 | tf_op jit(solution)/shard_map/broadcast_in_dim | solution.py:238
  1.5 0.0 copy-start.3
  1.5 8.6 %all-to-all-start = ((bf16[8,16,1024]{2,1,0:T(8,128)(2,1)}), bf16[8,16,1024]{2,1,0:T(8,128)(2,1)S(1)}, u32[]{:S(2)}, u32[]{:S(2)}) async-start(bf16[8,16,1024]{2,1,0:T(8,128)(2,1)} %broadcast_in_dim.26), calls=%async_computation | async-start | bytes 524288 | tf_op jit(solution)/shard_map/all_to_all | solution.py:239
  10.1 0.0 copy-start.4
  10.1 0.0 copy-start.2
  10.1 2.2 %copy.14 = bf16[1,16,256,2,128]{4,2,1,3,0:T(8,128)(2,1)S(1)} copy(bf16[1,16,256,2,128]{4,3,2,1,0:T(2,128)(2,1)} %param.7) | data formatting | bytes 4194304 | tf_op args[2]
  12.3 0.0 copy-done.3
  12.4 0.0 copy-done.4
  12.4 0.1 iota_compare_fusion
  12.4 0.5 fusion.7
  12.9 0.2 fusion.1
  13.1 0.3 convolution_divide_fusion
  13.4 0.0 copy-done.2
  13.4 0.0 copy-start.1
  13.4 3.3 %copy.13 = bf16[1,2,512,2,1024]{4,2,3,1,0:T(8,128)(2,1)} copy(bf16[1,2,512,2,1024]{4,3,2,1,0:T(2,128)(2,1)S(1)} %copy-done.2) | data formatting | bytes 8388608 | tf_op args[1]
  16.7 5.2 %all-to-all-done.refs_0_ = bf16[8,16,1024]{2,1,0:T(8,128)(2,1)S(1)} async-done(((bf16[8,16,1024]{2,1,0:T(8,128)(2,1)}), bf16[8,16,1024]{2,1,0:T(8,128)(2,1)S(1)}, u32[]{:S(2)}, u32[]{:S(2)}) %all-to-all-start) | async-done | bytes 262176 | tf_op jit(solution)/shard_map/all_to_all | solution.py:239
  22.0 0.0 collective-permute-start.1
  22.0 1.6 %collective-permute-start = (bf16[8,16,1024]{2,1,0:T(8,128)(2,1)S(1)}, bf16[8,16,1024]{2,1,0:T(8,128)(2,1)S(1)}, u32[]{:S(2)}, u32[]{:S(2)}) collective-permute-start(bf16[8,16,1024]{2,1,0:T(8,128)(2,1)S(1)} %all-to-all-done.refs_0_), channel_id=1, source_target_pairs={{0,64},{4,196},{64,0},{68,132},{128,192},{132,68},{192,128},{196,4... | collective-permute-start | bytes 786440 | tf_op jit(solution)/shard_map/ppermute | solution.py:243
  23.5 4.8 %collective-permute-done.refs_0_ = bf16[8,16,1024]{2,1,0:T(8,128)(2,1)S(1)} collective-permute-done((bf16[8,16,1024]{2,1,0:T(8,128)(2,1)S(1)}, bf16[8,16,1024]{2,1,0:T(8,128)(2,1)S(1)}, u32[]{:S(2)}, u32[]{:S(2)}) %collective-permute-start) | collective-permute-done | bytes 262176 | tf_op jit(solution)/shard_map/ppermute | solution.py:243
  28.3 3.0 %collective-permute-start.4 = (bf16[8,16,1024]{2,1,0:T(8,128)(2,1)S(1)}, bf16[8,16,1024]{2,1,0:T(8,128)(2,1)S(1)}, u32[]{:S(2)}, u32[]{:S(2)}) collective-permute-start(bf16[8,16,1024]{2,1,0:T(8,128)(2,1)S(1)} %collective-permute-done.refs_0_), channel_id=1, source_target_pairs={{0,192},{4,68},{64,128},{68,4},{128,64},{132,196},{192,0},{196,132... | collective-permute-start | bytes 786440 | tf_op jit(solution)/shard_map/ppermute | solution.py:245
  31.3 0.2 collective-permute-start.2
  31.6 0.0 collective-permute-done.1.refs_2_
  31.6 0.0 copy-done.1
  31.6 0.0 copy-start
  31.6 2.2 %copy-done = bf16[1,2,512,2,1024]{4,2,3,1,0:T(8,128)(2,1)S(1)} copy-done((bf16[1,2,512,2,1024]{4,2,3,1,0:T(8,128)(2,1)S(1)}, bf16[1,2,512,2,1024]{4,2,3,1,0:T(8,128)(2,1)}, u32[]{:S(2)}) %copy-start) | copy-done | bytes 4194328
  33.8 2.2 %shard_map.57.all_refs_0_ = bf16[8,16,1152]{2,1,0:T(8,128)(2,1)S(1)} custom-call(s32[1,128]{1,0:T(1,128)S(1)} %copy-done.1, bf16[8,16,1024]{2,1,0:T(8,128)(2,1)S(1)} %collective-permute-done.refs_0_, bf16[2,2,512,1024]{3,2,1,0:T(8,128)(2,1)S(1)} %bitcast.28, bf16[2,2,512,1024]{3,2,1,0:T(8,128)(2,1)S(1)} %collective-permute-done.1.refs_2_), custom_call_target="tpu_custom_call" | custom-call | flops 1073741824 | bytes 2097152 | tf_op jit(solution)/shard_map/pallas_call | solution.py:130
  36.0 0.0 collective-permute-done.4.refs_0_
  36.0 2.3 %shard_map.58 = bf16[8,16,1152]{2,1,0:T(8,128)(2,1)S(1)} custom-call(s32[1,128]{1,0:T(1,128)S(1)} %copy-done.1, bf16[8,16,1024]{2,1,0:T(8,128)(2,1)S(1)} %collective-permute-done.4.refs_0_, bf16[2,2,512,1024]{3,2,1,0:T(8,128)(2,1)S(1)} %bitcast.29, bf16[2,2,512,1024]{3,2,1,0:T(8,128)(2,1)S(1)} %collective-permute-done.1.refs_2_), custom_call_target="tpu_custom_call" | custom-call | flops 1073741824 | bytes 2097152 | tf_op jit(solution)/shard_map/pallas_call | solution.py:130
  38.3 3.1 %collective-permute-start.5 = (bf16[8,16,1152]{2,1,0:T(8,128)(2,1)S(1)}, bf16[8,16,1152]{2,1,0:T(8,128)(2,1)S(1)}, u32[]{:S(2)}, u32[]{:S(2)}) collective-permute-start(bf16[8,16,1152]{2,1,0:T(8,128)(2,1)S(1)} %shard_map.58), channel_id=1, source_target_pairs={{0,192},{4,68},{64,128},{68,4},{128,64},{132,196},{192,0},{196,132... | collective-permute-start | bytes 884744 | tf_op jit(solution)/shard_map/ppermute | solution.py:252
  41.4 0.0 collective-permute-done.2.refs_0_
  41.4 2.2 %shard_map.56 = bf16[8,16,1152]{2,1,0:T(8,128)(2,1)S(1)} custom-call(s32[1,128]{1,0:T(1,128)S(1)} %copy-done.1, bf16[8,16,1024]{2,1,0:T(8,128)(2,1)S(1)} %collective-permute-done.2.refs_0_, bf16[2,2,512,1024]{3,2,1,0:T(8,128)(2,1)S(1)} %bitcast.30, bf16[2,2,512,1024]{3,2,1,0:T(8,128)(2,1)S(1)} %collective-permute-done.1.refs_2_), custom_call_target="tpu_custom_call" | custom-call | flops 1073741824 | bytes 2097152 | tf_op jit(solution)/shard_map/pallas_call | solution.py:130
  43.6 0.6 collective-permute-start.3
  44.2 2.0 %collective-permute-done.5.all_refs_1_ = bf16[8,16,1152]{2,1,0:T(8,128)(2,1)S(1)} collective-permute-done((bf16[8,16,1152]{2,1,0:T(8,128)(2,1)S(1)}, bf16[8,16,1152]{2,1,0:T(8,128)(2,1)S(1)}, u32[]{:S(2)}, u32[]{:S(2)}) %collective-permute-start.5) | collective-permute-done | bytes 294944 | tf_op jit(solution)/shard_map/ppermute | solution.py:252
  46.3 0.5 shard_map.59
  46.8 0.1 collective-permute-start.6
  46.9 2.3 %shard_map.55.all_refs_0_ = bf16[8,16,1152]{2,1,0:T(8,128)(2,1)S(1)} custom-call(s32[1,128]{1,0:T(1,128)S(1)} %copy-done.1, bf16[8,16,1024]{2,1,0:T(8,128)(2,1)S(1)} %all-to-all-done.refs_0_, bf16[2,2,512,1024]{3,2,1,0:T(8,128)(2,1)S(1)} %bitcast.31, bf16[2,2,512,1024]{3,2,1,0:T(8,128)(2,1)S(1)} %collective-permute-done.1.refs_2_), custom_call_target="tpu_custom_call" | custom-call | flops 1073741824 | bytes 2097152 | tf_op jit(solution)/shard_map/pallas_call | solution.py:130
  49.2 4.4 %collective-permute-done.3.all_refs_1_ = bf16[8,16,1152]{2,1,0:T(8,128)(2,1)S(1)} collective-permute-done((bf16[8,16,1152]{2,1,0:T(8,128)(2,1)S(1)}, bf16[8,16,1152]{2,1,0:T(8,128)(2,1)S(1)}, u32[]{:S(2)}, u32[]{:S(2)}) %collective-permute-start.3) | collective-permute-done | bytes 294944 | tf_op jit(solution)/shard_map/ppermute | solution.py:253
  53.5 0.1 collective-permute-done.6.all_refs_2_
  53.6 0.7 shard_map.60
  54.3 13.9 %all_to_all.10.p_ref = bf16[8,16,1152]{2,1,0:T(8,128)(2,1)S(1)} all-to-all(bf16[8,16,1152]{2,1,0:T(8,128)(2,1)S(1)} %shard_map.60), channel_id=1, replica_groups=mesh['y'=4,'zh'=2,'zl'=4,'core'=2,'grp'=4] {'zh','zl'}, dimensions={0} | all-to-all | bytes 589824 | tf_op jit(solution)/shard_map/all_to_all | solution.py:257
  68.2 1.0 %shard_map.61 = bf16[16,1024]{1,0:T(8,128)(2,1)} custom-call(bf16[8,16,1152]{2,1,0:T(8,128)(2,1)S(1)} %all_to_all.10.p_ref, f32[16,1024]{1,0:T(8,128)S(1)} %bitcast.32, f32[16,128]{1,0:T(8,128)S(1)} %pad.4.sl_ref), custom_call_target="tpu_custom_call" | custom-call | tf_op jit(solution)/shard_map/pallas_call | solution.py:202
  (4 shorter events, 0.1 us)
Async XLA Ops:
  1.5 10.8 %copy-start.3 = (bf16[1,16,1024]{2,1,0:T(8,128)(2,1)S(1)}, bf16[1,16,1024]{2,1,0:T(8,128)(2,1)}, u32[]{:S(2)}) copy-start(bf16[1,16,1024]{2,1,0:T(8,128)(2,1)} %param.5) | copy-start | bytes 98308
  1.5 20.5 %all-to-all-start = ((bf16[8,16,1024]{2,1,0:T(8,128)(2,1)}), bf16[8,16,1024]{2,1,0:T(8,128)(2,1)S(1)}, u32[]{:S(2)}, u32[]{:S(2)}) async-start(bf16[8,16,1024]{2,1,0:T(8,128)(2,1)} %broadcast_in_dim.26), calls=%async_computation | async-start | bytes 524288 | tf_op jit(solution)/shard_map/all_to_all | solution.py:239
  10.1 2.3 %copy-start.4 = (s32[1,16]{1,0:T(1,128)S(1)}, s32[1,16]{1,0:T(1,128)}, u32[]{:S(2)}) copy-start(s32[1,16]{1,0:T(1,128)} %param.8) | copy-start | bytes 196
  10.1 3.3 %copy-start.2 = (bf16[1,2,512,2,1024]{4,3,2,1,0:T(2,128)(2,1)S(1)}, bf16[1,2,512,2,1024]{4,3,2,1,0:T(2,128)(2,1)}, u32[]{:S(2)}) copy-start(bf16[1,2,512,2,1024]{4,3,2,1,0:T(2,128)(2,1)} %param.6) | copy-start | bytes 12582916
  13.4 18.1 %copy-start.1 = (s32[1,128]{1,0:T(1,128)S(1)}, s32[1,128]{1,0:T(1,128)}, u32[]{:S(2)}) copy-start(s32[1,128]{1,0:T(1,128)} %ids_ref.7) | copy-start | bytes 1540
  22.0 9.6 %collective-permute-start.1 = (bf16[2,2,512,1024]{3,2,1,0:T(8,128)(2,1)}, bf16[2,2,512,1024]{3,2,1,0:T(8,128)(2,1)S(1)}, u32[]{:S(2)}, u32[]{:S(2)}) collective-permute-start(bf16[2,2,512,1024]{3,2,1,0:T(8,128)(2,1)} %bitcast.27), channel_id=1, source_target_pairs={{0,4},{4,0},{1,5},{5,1},{2,6},{6,2},{3,7},{7,3},{8,12},{12,8},{9,1... | collective-permute-start | bytes 12582920 | tf_op jit(solution)/shard_map/ppermute | solution.py:242
  22.0 6.4 %collective-permute-start = (bf16[8,16,1024]{2,1,0:T(8,128)(2,1)S(1)}, bf16[8,16,1024]{2,1,0:T(8,128)(2,1)S(1)}, u32[]{:S(2)}, u32[]{:S(2)}) collective-permute-start(bf16[8,16,1024]{2,1,0:T(8,128)(2,1)S(1)} %all-to-all-done.refs_0_), channel_id=1, source_target_pairs={{0,64},{4,196},{64,0},{68,132},{128,192},{132,68},{192,128},{196,4... | collective-permute-start | bytes 786440 | tf_op jit(solution)/shard_map/ppermute | solution.py:243
  28.3 7.7 %collective-permute-start.4 = (bf16[8,16,1024]{2,1,0:T(8,128)(2,1)S(1)}, bf16[8,16,1024]{2,1,0:T(8,128)(2,1)S(1)}, u32[]{:S(2)}, u32[]{:S(2)}) collective-permute-start(bf16[8,16,1024]{2,1,0:T(8,128)(2,1)S(1)} %collective-permute-done.refs_0_), channel_id=1, source_target_pairs={{0,192},{4,68},{64,128},{68,4},{128,64},{132,196},{192,0},{196,132... | collective-permute-start | bytes 786440 | tf_op jit(solution)/shard_map/ppermute | solution.py:245
  31.3 10.0 %collective-permute-start.2 = (bf16[8,16,1024]{2,1,0:T(8,128)(2,1)S(1)}, bf16[8,16,1024]{2,1,0:T(8,128)(2,1)S(1)}, u32[]{:S(2)}, u32[]{:S(2)}) collective-permute-start(bf16[8,16,1024]{2,1,0:T(8,128)(2,1)S(1)} %all-to-all-done.refs_0_), channel_id=1, source_target_pairs={{0,192},{4,68},{64,128},{68,4},{128,64},{132,196},{192,0},{196,132... | collective-permute-start | bytes 786440 | tf_op jit(solution)/shard_map/ppermute | solution.py:246
  31.6 2.2 %copy-start = (bf16[1,2,512,2,1024]{4,2,3,1,0:T(8,128)(2,1)S(1)}, bf16[1,2,512,2,1024]{4,2,3,1,0:T(8,128)(2,1)}, u32[]{:S(2)}) copy-start(bf16[1,2,512,2,1024]{4,2,3,1,0:T(8,128)(2,1)} %copy.13) | copy-start | bytes 12582916
  38.3 8.0 %collective-permute-start.5 = (bf16[8,16,1152]{2,1,0:T(8,128)(2,1)S(1)}, bf16[8,16,1152]{2,1,0:T(8,128)(2,1)S(1)}, u32[]{:S(2)}, u32[]{:S(2)}) collective-permute-start(bf16[8,16,1152]{2,1,0:T(8,128)(2,1)S(1)} %shard_map.58), channel_id=1, source_target_pairs={{0,192},{4,68},{64,128},{68,4},{128,64},{132,196},{192,0},{196,132... | collective-permute-start | bytes 884744 | tf_op jit(solution)/shard_map/ppermute | solution.py:252
  43.6 9.9 %collective-permute-start.3 = (bf16[8,16,1152]{2,1,0:T(8,128)(2,1)S(1)}, bf16[8,16,1152]{2,1,0:T(8,128)(2,1)S(1)}, u32[]{:S(2)}, u32[]{:S(2)}) collective-permute-start(bf16[8,16,1152]{2,1,0:T(8,128)(2,1)S(1)} %shard_map.56), channel_id=1, source_target_pairs={{0,192},{4,68},{64,128},{68,4},{128,64},{132,196},{192,0},{196,132... | collective-permute-start | bytes 884744 | tf_op jit(solution)/shard_map/ppermute | solution.py:253
  46.8 6.8 %collective-permute-start.6 = (bf16[8,16,1152]{2,1,0:T(8,128)(2,1)S(1)}, bf16[8,16,1152]{2,1,0:T(8,128)(2,1)S(1)}, u32[]{:S(2)}, u32[]{:S(2)}) collective-permute-start(bf16[8,16,1152]{2,1,0:T(8,128)(2,1)S(1)} %shard_map.59), channel_id=1, source_target_pairs={{0,64},{4,196},{64,0},{68,132},{128,192},{132,68},{192,128},{196,4... | collective-permute-start | bytes 884744 | tf_op jit(solution)/shard_map/ppermute | solution.py:255
